TPU v7x, 32 devices: a whole 2x2x4 slice. The times are simulated.
32 devices in a mesh: lev: 4 (over y, core), tile: 8 (over z, x).
Axes of the slice: x: 2, y: 2, z: 4, core: 2. Of those that a mesh axis runs over, the one named last changes fastest.
Arguments:
- fields: float32 [64, 5, 64, 512], P('lev', None, 'tile'), may hold values from -4 to 4
- land_use: int32 [64, 512], P('tile'), may hold values from 0 to 7
- column_ops: float32 [5, 8, 64, 64], replicated, may hold values from -1 to 1, as said below
Outputs:
- fields_new: float32 [64, 5, 64, 512], P('lev', None, 'tile')
Inputs may be any that keep to these rules, and one draw needn't show every extreme that they name: `column_ops`: each matrix has independent entries.
All inputs are finite; a program needn't handle non-finite values.
Results may differ from a plain program's by a relative error of at most 0.0001.
Values sent between devices are 32-bit elements; how exact they have to be, the bound alone decides.
No kernel may reach another device: no remote copies, remote signals or barrier semaphores. Data moves between devices by JAX's collectives and lax.ppermute only.
A program may use at most 128 MiB of HBM per device.

v0:
```python
import jax
import jax.numpy as jnp
from jax import lax
from jax.sharding import PartitionSpec as P

COURANT = 0.4


def extended_2(block, sides, width):
    for axis, dim in sides:
        count = lax.axis_size(axis)
        forward = [(i, i + 1) for i in range(count - 1)]
        forward.append((count - 1, 0))
        backward = [(target, source) for source, target in forward]
        low = lax.ppermute(
            lax.slice_in_dim(block, block.shape[dim] - width, None, axis=dim), axis, forward
        )
        high = lax.ppermute(lax.slice_in_dim(block, 0, width, axis=dim), axis, backward)
        block = jnp.concatenate([low, block, high], axis=dim)
    return block


def tendency(state):
    u_wind = state[:, 2:3]
    v_wind = state[:, 3:4]
    face_x = (
        7.0 * (state[:, :, 1:-2] + state[:, :, 2:-1]) - (state[:, :, :-3] + state[:, :, 3:])
    ) / 12.0
    flux_x = 0.5 * (u_wind[:, :, 1:-2] + u_wind[:, :, 2:-1]) * face_x
    div_x = flux_x[:, :, 1:] - flux_x[:, :, :-1]
    inner = state[:, :, 2:-2]
    v_inner = v_wind[:, :, 2:-2]
    face_y = (
        7.0 * (inner + jnp.roll(inner, -1, axis=3))
        - (jnp.roll(inner, 1, axis=3) + jnp.roll(inner, -2, axis=3))
    ) / 12.0
    flux_y = 0.5 * (v_inner + jnp.roll(v_inner, -1, axis=3)) * face_y
    div_y = flux_y - jnp.roll(flux_y, 1, axis=3)
    return -COURANT * (div_x + div_y)


def mix_columns(operators, column, categories):
    mixed = None
    for cat in range(operators.shape[1]):
        chosen = (categories == cat).astype(jnp.float32)
        term = chosen * jnp.einsum(
            "fij,jfxy->ifxy", operators[:, cat], column, precision=lax.Precision.HIGHEST
        )
        mixed = term if mixed is None else mixed + term
    return mixed


def per_device(fields, land_use, column_ops):
    coefs = (1.0 / 3.0, 0.5, 1.0)
    current = fields
    for coef in coefs:
        extended = extended_2(current, (("tile", 2),), 2)
        current = fields + coef * tendency(extended)
    lev_count = lax.axis_size("lev")
    lev_place = lax.axis_index("lev")
    columns = lax.all_to_all(current, "lev", split_axis=2, concat_axis=0, tiled=True)
    part_rows = current.shape[2] // lev_count
    own_cats = lax.dynamic_slice_in_dim(land_use, lev_place * part_rows, part_rows, 0)
    mixed = mix_columns(column_ops, columns, own_cats)
    result = lax.all_to_all(mixed, "lev", split_axis=0, concat_axis=2, tiled=True)
    return result


def solution(mesh):
    in_specs = (P("lev", None, "tile", None), P("tile", None), P())
    out_specs = P("lev", None, "tile", None)
    return jax.shard_map(
        per_device, mesh=mesh, in_specs=in_specs, out_specs=out_specs, check_vma=False
    )
```

profile of v0, /device:TPU:0, one launch (start us, length us, event | category | flops | bytes accessed | tf_op | source)
XLA Modules:
  0.0 121.6 jit_solution(14283208866931050102)
XLA Ops:
  0.0 2.1 %copy.59 = f32[16,5,8,512]{3,0,2,1:T(8,128)S(1)} copy(f32[16,5,8,512]{3,2,1,0:T(8,128)} %param.3) | data formatting | bytes 2621440 | tf_op args[0]
  2.1 3.0 %collective-permute-start = (f32[16,5,2,512]{3,0,2,1:T(8,128)S(1)}, f32[16,5,2,512]{3,0,2,1:T(8,128)S(1)}, u32[]{:S(2)}, u32[]{:S(2)}) collective-permute-start(f32[16,5,2,512]{3,0,2,1:T(8,128)S(1)} %get-tuple-element.24), channel_id=1, source_target_pairs={{0,1},{1,2},{2,3},{3,4},{4,5},{5,6},{6,7},{7,0},{8,9},{9,10},{10,1... | collective-permute-start | bytes 983048 | tf_op jit(solution)/shard_map/ppermute | solution.py:15
  5.1 3.1 %collective-permute-start.1 = (f32[16,5,2,512]{3,0,2,1:T(8,128)S(1)}, f32[16,5,2,512]{3,0,2,1:T(8,128)S(1)}, u32[]{:S(2)}, u32[]{:S(2)}) collective-permute-start(f32[16,5,2,512]{3,0,2,1:T(8,128)S(1)} %get-tuple-element.25), channel_id=1, source_target_pairs={{1,0},{2,1},{3,2},{4,3},{5,4},{6,5},{7,6},{0,7},{9,8},{10,9},{11,1... | collective-permute-start | bytes 983048 | tf_op jit(solution)/shard_map/ppermute | solution.py:18
  9.6 9.5 %collective-permute-done = f32[16,5,2,512]{3,0,2,1:T(8,128)S(1)} collective-permute-done((f32[16,5,2,512]{3,0,2,1:T(8,128)S(1)}, f32[16,5,2,512]{3,0,2,1:T(8,128)S(1)}, u32[]{:S(2)}, u32[]{:S(2)}) %collective-permute-start) | collective-permute-done | bytes 327712 | tf_op jit(solution)/shard_map/ppermute | solution.py:15
  19.1 1.5 %fusion.40 = (f32[16,5,8,512]{3,0,2,1:T(8,128)S(1)}, f32[16,5,10,512]{3,0,2,1:T(8,128)S(1)}, f32[16,5,10,512]{3,0,2,1:T(8,128)S(1)}) fusion(f32[16,5,8,1]{3,0,2,1:T(8,128)S(1)} %get-tuple-element.21, f32[16,5,8,511]{3,0,2,1:T(8,128)S(1)} %get-tuple-element.23, f32[16,5,8,511]{3,0,2,1:T(8,128)S(1)} %get-tuple-element.22, ...), kind=kLoop, calls=%fused_computation.70 | loop fusion | flops 2621439 | bytes 10420224 | tf_op jit(solution)/shard_map/mul | solution.py:37
  22.0 1.5 %fusion.37 = f32[16,5,8,512]{3,0,2,1:T(8,128)S(1)} fusion(f32[16,5,9,512]{3,0,2,1:T(8,128)S(1)} %fusion.19, f32[16,5,8,512]{3,0,2,1:T(8,128)S(1)} %get-tuple-element.17, f32[16,5,8,511]{3,0,2,1:T(8,128)S(1)} %bitcast.104, f32[16,5,8,1]{3,0,2,1:T(8,128)S(1)} %slice.353, f32[16,5,8,512]{3,2,1,0:T(8,128)S(1)} %copy-done), kind=kLoop, calls=%fused_computation.66 | loop fusion | flops 1966080 | bytes 7864320 | tf_op jit(solution)/shard_map/add | solution.py:58
  24.4 1.9 %collective-permute-start.2 = (f32[16,5,2,512]{3,0,2,1:T(8,128)S(1)}, f32[16,5,2,512]{3,0,2,1:T(8,128)S(1)}, u32[]{:S(2)}, u32[]{:S(2)}) collective-permute-start(f32[16,5,2,512]{3,0,2,1:T(8,128)S(1)} %get-tuple-element.15), channel_id=1, source_target_pairs={{0,1},{1,2},{2,3},{3,4},{4,5},{5,6},{6,7},{7,0},{8,9},{9,10},{10,1... | collective-permute-start | bytes 983048 | tf_op jit(solution)/shard_map/ppermute | solution.py:15
  26.3 3.1 %collective-permute-start.3 = (f32[16,5,2,512]{3,0,2,1:T(8,128)S(1)}, f32[16,5,2,512]{3,0,2,1:T(8,128)S(1)}, u32[]{:S(2)}, u32[]{:S(2)}) collective-permute-start(f32[16,5,2,512]{3,0,2,1:T(8,128)S(1)} %get-tuple-element.16), channel_id=1, source_target_pairs={{1,0},{2,1},{3,2},{4,3},{5,4},{6,5},{7,6},{0,7},{9,8},{10,9},{11,1... | collective-permute-start | bytes 983048 | tf_op jit(solution)/shard_map/ppermute | solution.py:18
  30.9 8.5 %collective-permute-done.2 = f32[16,5,2,512]{3,0,2,1:T(8,128)S(1)} collective-permute-done((f32[16,5,2,512]{3,0,2,1:T(8,128)S(1)}, f32[16,5,2,512]{3,0,2,1:T(8,128)S(1)}, u32[]{:S(2)}, u32[]{:S(2)}) %collective-permute-start.2) | collective-permute-done | bytes 327712 | tf_op jit(solution)/shard_map/ppermute | solution.py:15
  39.4 2.4 %collective-permute-done.3 = f32[16,5,2,512]{3,0,2,1:T(8,128)S(1)} collective-permute-done((f32[16,5,2,512]{3,0,2,1:T(8,128)S(1)}, f32[16,5,2,512]{3,0,2,1:T(8,128)S(1)}, u32[]{:S(2)}, u32[]{:S(2)}) %collective-permute-start.3) | collective-permute-done | bytes 327712 | tf_op jit(solution)/shard_map/ppermute | solution.py:18
  42.2 1.5 %fusion.34 = f32[16,5,8,512]{3,0,2,1:T(8,128)S(1)} fusion(f32[16,5,9,512]{3,0,2,1:T(8,128)S(1)} %fusion.12, f32[16,5,8,512]{3,0,2,1:T(8,128)S(1)} %fusion.43, f32[16,5,8,511]{3,0,2,1:T(8,128)S(1)} %bitcast.105, f32[16,5,8,1]{3,0,2,1:T(8,128)S(1)} %slice.376, f32[16,5,8,512]{3,2,1,0:T(8,128)S(1)} %copy-done), kind=kLoop, calls=%fused_computation.62 | loop fusion | flops 1966080 | bytes 7864320 | tf_op jit(solution)/shard_map/add | solution.py:58
  44.7 4.6 %collective-permute-start.5 = (f32[16,5,2,512]{3,0,2,1:T(8,128)S(1)}, f32[16,5,2,512]{3,0,2,1:T(8,128)S(1)}, u32[]{:S(2)}, u32[]{:S(2)}) collective-permute-start(f32[16,5,2,512]{3,0,2,1:T(8,128)S(1)} %get-tuple-element.10), channel_id=1, source_target_pairs={{1,0},{2,1},{3,2},{4,3},{5,4},{6,5},{7,6},{0,7},{9,8},{10,9},{11,1... | collective-permute-start | bytes 983048 | tf_op jit(solution)/shard_map/ppermute | solution.py:18
  50.9 6.7 %collective-permute-done.4 = f32[16,5,2,512]{3,0,2,1:T(8,128)S(1)} collective-permute-done((f32[16,5,2,512]{3,0,2,1:T(8,128)S(1)}, f32[16,5,2,512]{3,0,2,1:T(8,128)S(1)}, u32[]{:S(2)}, u32[]{:S(2)}) %collective-permute-start.4) | collective-permute-done | bytes 327712 | tf_op jit(solution)/shard_map/ppermute | solution.py:15
  57.6 4.5 %collective-permute-done.5 = f32[16,5,2,512]{3,0,2,1:T(8,128)S(1)} collective-permute-done((f32[16,5,2,512]{3,0,2,1:T(8,128)S(1)}, f32[16,5,2,512]{3,0,2,1:T(8,128)S(1)}, u32[]{:S(2)}, u32[]{:S(2)}) %collective-permute-start.5) | collective-permute-done | bytes 327712 | tf_op jit(solution)/shard_map/ppermute | solution.py:18
  62.6 1.5 %fusion.31 = f32[16,5,8,512]{3,0,2,1:T(8,128)S(1)} fusion(f32[16,5,9,512]{3,0,2,1:T(8,128)S(1)} %fusion.3, f32[16,5,8,512]{3,0,2,1:T(8,128)S(1)} %fusion.46, f32[16,5,8,511]{3,0,2,1:T(8,128)S(1)} %bitcast.106, f32[16,5,8,1]{3,0,2,1:T(8,128)S(1)} %slice.399, f32[16,5,8,512]{3,2,1,0:T(8,128)S(1)} %copy-done), kind=kLoop, calls=%fused_computation.58 | loop fusion | flops 1966080 | bytes 7864320 | tf_op jit(solution)/shard_map/add | solution.py:58
  65.2 3.5 %all-to-all-start = ((f32[16,5,8,512]{3,0,1,2:T(8,128)}), f32[16,5,8,512]{3,0,1,2:T(8,128)S(1)}, u32[]{:S(2)}, u32[]{:S(2)}) async-start(f32[16,5,8,512]{3,0,1,2:T(8,128)} %copy.60), calls=%async_computation | async-start | bytes 2621440 | tf_op jit(solution)/shard_map/all_to_all | solution.py:61
  69.5 16.5 %all-to-all-done = f32[16,5,8,512]{3,0,1,2:T(8,128)S(1)} async-done(((f32[16,5,8,512]{3,0,1,2:T(8,128)}), f32[16,5,8,512]{3,0,1,2:T(8,128)S(1)}, u32[]{:S(2)}, u32[]{:S(2)}) %all-to-all-start) | async-done | bytes 1310752 | tf_op jit(solution)/shard_map/all_to_all | solution.py:61
  88.6 1.3 %fusion.28 = f32[5,2,512,64]{2,3,1,0:T(8,128)S(1)} fusion(f32[5,2,512,64]{2,3,1,0:T(8,128)S(1)} %convolution_multiply_fusion.7, f32[64,5,2,512]{3,0,2,1:T(8,128)S(1)} %bitcast.97, f32[2,512]{1,0:T(2,128)S(1)} %get-tuple-element.27, f32[5,8,64,64]{3,2,1,0:T(8,128)S(1)} %copy-done.1), kind=kOutput, calls=%fused_computation.53 | convolution fusion | flops 252313600 | bytes 4100096 | tf_op jit(solution)/shard_map/fij,jfxy->ifxy/dot_general | solution.py:46
  90.0 1.3 %fusion.27 = f32[5,2,512,64]{2,3,1,0:T(8,128)S(1)} fusion(f32[5,2,512,64]{2,3,1,0:T(8,128)S(1)} %fusion.28, f32[64,5,2,512]{3,0,2,1:T(8,128)S(1)} %bitcast.98, f32[2,512]{1,0:T(2,128)S(1)} %get-tuple-element.28, f32[5,8,64,64]{3,2,1,0:T(8,128)S(1)} %copy-done.1), kind=kOutput, calls=%fused_computation.51 | convolution fusion | flops 252313600 | bytes 4100096 | tf_op jit(solution)/shard_map/fij,jfxy->ifxy/dot_general | solution.py:46
  94.0 1.4 %fusion.24 = f32[5,2,512,64]{2,3,1,0:T(8,128)S(1)} fusion(f32[5,2,512,64]{2,3,1,0:T(8,128)S(1)} %fusion.25, f32[64,5,2,512]{3,0,2,1:T(8,128)S(1)} %bitcast.101, f32[2,512]{1,0:T(2,128)S(1)} %get-tuple-element.31, f32[5,8,64,64]{3,2,1,0:T(8,128)S(1)} %copy-done.1), kind=kOutput, calls=%fused_computation.45 | convolution fusion | flops 252313600 | bytes 4100096 | tf_op jit(solution)/shard_map/fij,jfxy->ifxy/dot_general | solution.py:46
  95.4 1.3 %fusion.23 = f32[5,2,512,64]{2,3,1,0:T(8,128)S(1)} fusion(f32[5,2,512,64]{2,3,1,0:T(8,128)S(1)} %fusion.24, f32[64,5,2,512]{3,0,2,1:T(8,128)S(1)} %bitcast.102, f32[2,512]{1,0:T(2,128)S(1)} %get-tuple-element.32, f32[5,8,64,64]{3,2,1,0:T(8,128)S(1)} %copy-done.1), kind=kOutput, calls=%fused_computation.43 | convolution fusion | flops 252313600 | bytes 4100096 | tf_op jit(solution)/shard_map/fij,jfxy->ifxy/dot_general | solution.py:46
  96.7 1.4 %fusion.22 = f32[64,5,2,512]{3,0,2,1:T(8,128)S(1)} fusion(f32[5,2,512,64]{2,3,1,0:T(8,128)S(1)} %fusion.23, f32[64,5,2,512]{3,0,2,1:T(8,128)S(1)} %bitcast.103, f32[2,512]{1,0:T(2,128)S(1)} %get-tuple-element.26, f32[5,8,64,64]{3,2,1,0:T(8,128)S(1)} %copy-done.1), kind=kOutput, calls=%fused_computation.41 | convolution fusion | flops 252313600 | bytes 4100096 | tf_op jit(solution)/shard_map/fij,jfxy->ifxy/dot_general | solution.py:46
  99.1 19.7 %all_to_all.36 = f32[64,5,2,512]{3,2,1,0:T(2,128)S(1)} all-to-all(f32[64,5,2,512]{3,2,1,0:T(2,128)S(1)} %copy.70), channel_id=1, replica_groups=mesh['lev'=4,'tile'=8] {'lev'}, dimensions={0} | all-to-all | bytes 2621440 | tf_op jit(solution)/shard_map/all_to_all | solution.py:65
  119.6 2.0 %all_to_all.33 = f32[16,5,8,512]{3,2,1,0:T(8,128)} reshape(f32[16,5,4,2,512]{4,3,2,1,0:T(2,128)S(1)} %copy.71) | data formatting | bytes 2621440 | tf_op jit(solution)/shard_map/all_to_all | solution.py:65
  (51 shorter events, 17.3 us)
Async XLA Ops:
  2.1 17.0 %collective-permute-start = (f32[16,5,2,512]{3,0,2,1:T(8,128)S(1)}, f32[16,5,2,512]{3,0,2,1:T(8,128)S(1)}, u32[]{:S(2)}, u32[]{:S(2)}) collective-permute-start(f32[16,5,2,512]{3,0,2,1:T(8,128)S(1)} %get-tuple-element.24), channel_id=1, source_target_pairs={{0,1},{1,2},{2,3},{3,4},{4,5},{5,6},{6,7},{7,0},{8,9},{9,10},{10,1... | collective-permute-start | bytes 983048 | tf_op jit(solution)/shard_map/ppermute | solution.py:15
  5.1 16.2 %collective-permute-start.1 = (f32[16,5,2,512]{3,0,2,1:T(8,128)S(1)}, f32[16,5,2,512]{3,0,2,1:T(8,128)S(1)}, u32[]{:S(2)}, u32[]{:S(2)}) collective-permute-start(f32[16,5,2,512]{3,0,2,1:T(8,128)S(1)} %get-tuple-element.25), channel_id=1, source_target_pairs={{1,0},{2,1},{3,2},{4,3},{5,4},{6,5},{7,6},{0,7},{9,8},{10,9},{11,1... | collective-permute-start | bytes 983048 | tf_op jit(solution)/shard_map/ppermute | solution.py:18
  9.1 10.0 %copy-start = (f32[16,5,8,512]{3,2,1,0:T(8,128)S(1)}, f32[16,5,8,512]{3,2,1,0:T(8,128)}, u32[]{:S(2)}) copy-start(f32[16,5,8,512]{3,2,1,0:T(8,128)} %param.3) | copy-start | bytes 3932164
  24.4 15.0 %collective-permute-start.2 = (f32[16,5,2,512]{3,0,2,1:T(8,128)S(1)}, f32[16,5,2,512]{3,0,2,1:T(8,128)S(1)}, u32[]{:S(2)}, u32[]{:S(2)}) collective-permute-start(f32[16,5,2,512]{3,0,2,1:T(8,128)S(1)} %get-tuple-element.15), channel_id=1, source_target_pairs={{0,1},{1,2},{2,3},{3,4},{4,5},{5,6},{6,7},{7,0},{8,9},{9,10},{10,1... | collective-permute-start | bytes 983048 | tf_op jit(solution)/shard_map/ppermute | solution.py:15
  26.3 15.5 %collective-permute-start.3 = (f32[16,5,2,512]{3,0,2,1:T(8,128)S(1)}, f32[16,5,2,512]{3,0,2,1:T(8,128)S(1)}, u32[]{:S(2)}, u32[]{:S(2)}) collective-permute-start(f32[16,5,2,512]{3,0,2,1:T(8,128)S(1)} %get-tuple-element.16), channel_id=1, source_target_pairs={{1,0},{2,1},{3,2},{4,3},{5,4},{6,5},{7,6},{0,7},{9,8},{10,9},{11,1... | collective-permute-start | bytes 983048 | tf_op jit(solution)/shard_map/ppermute | solution.py:18
  44.6 13.1 %collective-permute-start.4 = (f32[16,5,2,512]{3,0,2,1:T(8,128)S(1)}, f32[16,5,2,512]{3,0,2,1:T(8,128)S(1)}, u32[]{:S(2)}, u32[]{:S(2)}) collective-permute-start(f32[16,5,2,512]{3,0,2,1:T(8,128)S(1)} %get-tuple-element.9), channel_id=1, source_target_pairs={{0,1},{1,2},{2,3},{3,4},{4,5},{5,6},{6,7},{7,0},{8,9},{9,10},{10,1... | collective-permute-start | bytes 983048 | tf_op jit(solution)/shard_map/ppermute | solution.py:15
  44.7 17.5 %collective-permute-start.5 = (f32[16,5,2,512]{3,0,2,1:T(8,128)S(1)}, f32[16,5,2,512]{3,0,2,1:T(8,128)S(1)}, u32[]{:S(2)}, u32[]{:S(2)}) collective-permute-start(f32[16,5,2,512]{3,0,2,1:T(8,128)S(1)} %get-tuple-element.10), channel_id=1, source_target_pairs={{1,0},{2,1},{3,2},{4,3},{5,4},{6,5},{7,6},{0,7},{9,8},{10,9},{11,1... | collective-permute-start | bytes 983048 | tf_op jit(solution)/shard_map/ppermute | solution.py:18
  65.2 20.8 %all-to-all-start = ((f32[16,5,8,512]{3,0,1,2:T(8,128)}), f32[16,5,8,512]{3,0,1,2:T(8,128)S(1)}, u32[]{:S(2)}, u32[]{:S(2)}) async-start(f32[16,5,8,512]{3,0,1,2:T(8,128)} %copy.60), calls=%async_computation | async-start | bytes 2621440 | tf_op jit(solution)/shard_map/all_to_all | solution.py:61
  86.0 1.3 %copy-start.1 = (f32[5,8,64,64]{3,2,1,0:T(8,128)S(1)}, f32[5,8,64,64]{3,2,1,0:T(8,128)}, u32[]{:S(2)}) copy-start(f32[5,8,64,64]{3,2,1,0:T(8,128)} %param.5) | copy-start | bytes 1966084
where the time goes:
time: 122 us
  waiting for transfers between devices  48.8 us (40%)
  blocking collectives  19.7 us (16%)
  starting transfers between devices  19.4 us (16%)
  local copies, waits for them, and re-layouts  12.6 us (10%)
  matrix products  10.7 us (9%)
  other arithmetic  9.94 us (8%)
    ppermute x3, waiting for transfers between devices, extended_2(): lax.ppermute(lax.slice_in_dim(block, block.shape[dim] - width, None, axis...  24.8 us
    all_to_all x1, blocking collectives, per_device(): lax.all_to_all(mixed, 'lev', split_axis=0, concat_axis=2, tiled=True)  19.7 us
    all_to_all x1, waiting for transfers between devices, per_device(): lax.all_to_all(current, 'lev', split_axis=2, concat_axis=0, tiled=True)  16.5 us
    ppermute x3, starting transfers between devices, extended_2(): lax.ppermute(lax.slice_in_dim(block, 0, width, axis=dim), axis, backward)  10.8 us
    dot_general x8, matrix products, mix_columns(): jnp.einsum('fij,jfxy->ifxy', operators[:, cat], column, precision=lax.Pre...  10.7 us
    ppermute x3, waiting for transfers between devices, extended_2(): lax.ppermute(lax.slice_in_dim(block, 0, width, axis=dim), axis, backward)  7.6 us
    ppermute x3, starting transfers between devices, extended_2(): lax.ppermute(lax.slice_in_dim(block, block.shape[dim] - width, None, axis...  5.02 us
    add x3, other arithmetic, per_device(): current = fields + coef * tendency(extended)  4.44 us
  transfers between devices with their start and end apart: 7, of which 7 were waited for; matrix products, arithmetic and copies ran while one was open for 5% of the time, Pallas kernels for 0%

commit v1 on v0

v1 whole, which is shorter than its diff:
```python
import functools

import jax
import jax.numpy as jnp
from jax import lax
from jax.experimental import pallas as pl
from jax.experimental.pallas import tpu as pltpu
from jax.sharding import PartitionSpec as P

COURANT = 0.4
COEFS = (1.0 / 3.0, 0.5, 1.0)
CHUNKS = ((2, 3), (0,), (1,), (4,))
HALO = 6
UNROLL = 4
VMEM = pl.BlockSpec(memory_space=pltpu.VMEM)
PARAMS = pltpu.CompilerParams(vmem_limit_bytes=14 * 2**20)
F32 = jnp.float32


def cost(flops, arrays):
    size = sum(a.size * a.dtype.itemsize for a in arrays)
    return pl.CostEstimate(flops=int(flops), bytes_accessed=int(size), transcendentals=0)


def sds(*shape, dtype=F32):
    return jax.ShapeDtypeStruct(shape, dtype)


def prep_kernel(chunk, x_ref, keep_ref, send_ref):
    rows, _, half, _ = keep_ref.shape
    odd = lax.rem(lax.axis_index("tile"), 2)
    for n, f in enumerate(chunk):
        kept = jnp.swapaxes(x_ref[pl.ds(odd * half, half), f], 0, 1)
        sent = jnp.swapaxes(x_ref[pl.ds((1 - odd) * half, half), f], 0, 1)
        for r in range(rows):
            turned = jnp.where(odd == 0, r, rows - 1 - r)
            keep_ref[turned, n] = kept[r]
            send_ref[rows - 1 - turned, n] = sent[r]


def roll(a, shift):
    return pltpu.roll(a, shift % a.shape[1], 1)


def in_groups(first, end, rows, state):
    if UNROLL is None:
        return rows(first, end - first, state)

    def body(step, state):
        return rows(first + step * UNROLL, UNROLL, state)

    return lax.fori_loop(0, (end - first) // UNROLL, body, state)


def stage_rows(first, last, base, off_base, old, off_old, new, off_new, faces, fields, scales):
    ux, vr, vl = faces

    def wind(i):
        if scales is not None:
            ux[i - first + 1] = (old[off_old + i, 0] + old[off_old + i + 1, 0]) * scales[0]
        return ux[i - first + 1]

    def face(i, n, u):
        near = old[off_old + i, n] + old[off_old + i + 1, n]
        far = old[off_old + i - 1, n] + old[off_old + i + 2, n]
        return u * (7.0 * near - far)

    def rows(low, count, flux):
        flux = list(flux)
        for more in range(count):
            i = low + more
            u = wind(i)
            for n in range(fields)[::-1]:
                s = old[off_old + i, n]
                l1, l2, r1, r2 = roll(s, 1), roll(s, 2), roll(s, -1), roll(s, -2)
                left, right = s + l1, s + r1
                if scales is not None and n == 1:
                    vr[i - first] = right * scales[1]
                    vl[i - first] = left * scales[1]
                wide = vr[i - first] * (7.0 * right - (l1 + r2)) - vl[i - first] * (7.0 * left - (l2 + r1))
                here = face(i, n, u)
                new[off_new + i, n] = base[off_base + i, n] + ((here - flux[n]) + wide)
                flux[n] = here
        return tuple(flux)

    u = wind(first - 1)
    in_groups(first, last + 1, rows, tuple(face(first - 1, n, u) for n in range(fields)))


def gather_rows(parts, ext):
    at = 0
    for part in parts:
        for i in range(part.shape[0]):
            ext[at + i] = part[i]
        at += part.shape[0]


def scatter_blocks(adv, outs, lev_count, own):
    lev = lax.axis_index("lev")
    for a in range(lev_count):
        there = lev ^ a
        for q in range(own):
            outs[2 * a][q] = adv[there * own + q]
            outs[2 * a + 1][q] = adv[2 * lev_count * own - 1 - there * own - q]


def advect_kernel(lev_count, winds, before, keep, recv, after, *refs):
    rows = 2 * keep.shape[0]
    own = keep.shape[0] // lev_count
    faces, outs = refs[:9], refs[9 : 9 + 2 * lev_count]
    ext, s1, s2, adv = refs[9 + 2 * lev_count :]
    gather_rows((before, keep, recv, after), ext)
    sign = jnp.where(lax.rem(lax.axis_index("tile"), 2) == 0, 1.0, -1.0).astype(F32)
    states = ((ext, HALO), (s1, HALO - 2), (s2, HALO - 4), (adv, 0))
    for k, coef in enumerate(COEFS):
        reach = HALO - 2 * (k + 1)
        scale = -COURANT * coef / 24.0
        stage_rows(
            -reach, rows - 1 + reach, ext, HALO, *states[k], *states[k + 1],
            faces[3 * k : 3 * k + 3], keep.shape[1], (sign * scale, scale) if winds else None,
        )
    scatter_blocks(adv, outs, lev_count, own)


def advect(parts, faces, lev_count):
    keep = parts[1]
    tile_rows, fields, half, ny = keep.shape
    rows = 2 * tile_rows
    own = tile_rows // lev_count
    block = sds(own, fields, half, ny)
    sizes = [rows + 2 * (HALO - 2 * (k + 1)) for k in range(3)]
    scratch = [pltpu.VMEM((n, fields, half, ny), F32) for n in (rows + 2 * HALO, *sizes[:2], rows)]
    blocks = [block] * (2 * lev_count)
    outs, args = blocks, parts
    if faces is None:
        outs = [sds(n, half, ny) for size in sizes for n in (size + 1, size, size)] + blocks
    else:
        args = (*parts, *faces)
    return pl.pallas_call(
        functools.partial(advect_kernel, lev_count, faces is None),
        out_shape=outs,
        in_specs=[VMEM] * len(args),
        out_specs=[VMEM] * len(outs),
        scratch_shapes=scratch,
        compiler_params=PARAMS,
        cost_estimate=cost(sum(sizes) * fields * half * ny * 30, args),
    )(*args)


def mix_kernel(lev_count, use_ref, ops_ref, *refs):
    blocks, outs = refs[: 2 * lev_count], refs[2 * lev_count : 3 * lev_count]
    data, split, result = refs[3 * lev_count :]
    own, fields, half, ny = blocks[0].shape
    levels, per = data.shape[0], 2 * half
    cats = ops_ref.shape[1] // levels
    lev = lax.axis_index("lev")
    odd = lax.rem(lax.axis_index("tile"), 2)
    use = []
    for q in range(own):
        row = lev * own + q
        row = jnp.where(odd == 0, row, use_ref.shape[0] - 1 - row)
        use.append(use_ref[pl.ds(row, 1), :])
    for n in range(fields):
        for a in range(lev_count):
            for b in range(2):
                part = odd if b == 0 else 1 - odd
                at = pl.multiple_of((lev ^ a) * per + part * half, 8)
                for q in range(own):
                    data[pl.ds(at, half), q * ny : (q + 1) * ny] = blocks[2 * a + b][q, n]
        whole = data[...]
        high = whole.astype(jnp.bfloat16)
        split[0:levels] = high
        split[levels : 2 * levels] = high
        split[2 * levels :] = (whole - high.astype(F32)).astype(jnp.bfloat16)
        for q in range(own):
            for col in range(0, ny, 256):
                cols = slice(q * ny + col, q * ny + col + 256)
                every = jnp.dot(ops_ref[n], split[:, cols], preferred_element_type=F32)
                here = use[q][:, col : col + 256]
                mixed = every[:levels]
                for c in range(1, cats):
                    mixed = jnp.where(here == c, every[c * levels : (c + 1) * levels], mixed)
                result[:, cols] = mixed
        for a in range(lev_count):
            at = pl.multiple_of((lev ^ a) * per, 8)
            for q in range(own):
                outs[a][q, n] = result[pl.ds(at, per), q * ny : (q + 1) * ny]


def mix(use, ops, blocks, lev_count):
    own, fields, half, ny = blocks[0].shape
    levels = ops.shape[2] // 3
    return pl.pallas_call(
        functools.partial(mix_kernel, lev_count),
        out_shape=[sds(own, fields, 2 * half, ny)] * lev_count,
        in_specs=[VMEM] * (2 + len(blocks)),
        out_specs=[VMEM] * lev_count,
        scratch_shapes=[
            pltpu.VMEM((levels, own * ny), F32),
            pltpu.VMEM((3 * levels, own * ny), jnp.bfloat16),
            pltpu.VMEM((levels, own * ny), F32),
        ],
        compiler_params=PARAMS,
        cost_estimate=cost(2 * fields * ops.shape[1] * ops.shape[2] * own * ny, blocks),
    )(use, ops, *blocks)


def final_kernel(lev_count, *refs):
    out, turn = refs[-2:]
    lev = lax.axis_index("lev")
    odd = lax.rem(lax.axis_index("tile"), 2)
    for c, chunk in enumerate(CHUNKS):
        for n, f in enumerate(chunk):
            for a in range(lev_count):
                block = refs[c * lev_count + a]
                own = block.shape[0]
                for q in range(own):
                    row = (lev ^ a) * own + q
                    row = jnp.where(odd == 0, row, own * lev_count - 1 - row)
                    turn[row] = block[q, n]
            for low in range(0, out.shape[0], 8):
                out[low : low + 8, f] = jnp.swapaxes(turn[:, low : low + 8], 0, 1)


def per_device(fields, land_use, column_ops):
    lev_count, tile_count = lax.axis_size("lev"), lax.axis_size("tile")
    depth, total, rows, ny = fields.shape
    half = depth // 2
    levels = column_ops.shape[2]

    def send(array, target):
        pairs = [
            (lev * tile_count + tile, there * tile_count + to)
            for lev in range(lev_count)
            for tile in range(tile_count)
            for there, to in [target(lev, tile)]
        ]
        return lax.ppermute(array, ("lev", "tile"), pairs)

    def outward(lev, tile):
        return lev, (tile + (2 if tile % 2 else -2)) % tile_count

    def inward(lev, tile):
        return lev, (tile + (-2 if tile % 2 else 2)) % tile_count

    def other(lev, tile):
        return lev, tile ^ 1

    halves = []
    for chunk in CHUNKS:
        shape = sds(rows, len(chunk), half, ny)
        halves.append(
            pl.pallas_call(
                functools.partial(prep_kernel, chunk),
                out_shape=[shape, shape],
                in_specs=[VMEM],
                out_specs=[VMEM, VMEM],
                compiler_params=PARAMS,
                cost_estimate=cost(shape.size * 2, [shape] * 4),
            )(fields)
        )
    ops = column_ops.reshape(total, -1, levels)
    high = lax.reduce_precision(ops, 8, 7)
    ops = jnp.concatenate([high, ops - high, high], axis=2).astype(jnp.bfloat16)

    parts = []
    for keep, away in halves:
        recv = send(away, other)
        after = send(keep[:HALO], outward)
        before = send(recv[rows - HALO :], inward)
        parts.append((before, keep, recv, after))

    faces = None
    returned = []
    for chunk, part in zip(CHUNKS, parts):
        outs = advect(part, faces, lev_count)
        if faces is None:
            faces, outs = outs[:9], outs[9:]
        blocks = []
        for a in range(lev_count):
            for b in range(2):
                blocks.append(
                    send(outs[2 * a + b], lambda lev, tile: (lev ^ a, tile ^ b)) if a + b else outs[0]
                )
        own_ops = jnp.stack([ops[f] for f in chunk])
        mixed = mix(land_use, own_ops, blocks, lev_count)
        for a in range(lev_count):
            returned.append(send(mixed[a], lambda lev, tile: (lev ^ a, tile)) if a else mixed[0])

    return pl.pallas_call(
        functools.partial(final_kernel, lev_count),
        out_shape=sds(*fields.shape),
        in_specs=[VMEM] * len(returned),
        out_specs=VMEM,
        scratch_shapes=[pltpu.VMEM((rows, depth, ny), F32)],
        compiler_params=PARAMS,
        cost_estimate=cost(fields.size, returned + returned),
    )(*returned)


def solution(mesh):
    in_specs = (P("lev", None, "tile", None), P("tile", None), P())
    out_specs = P("lev", None, "tile", None)
    return jax.shard_map(
        per_device, mesh=mesh, in_specs=in_specs, out_specs=out_specs, check_vma=False
    )
```

time: 122 us -> 93.5 us (0.77)
  starting transfers between devices: 19.4 us -> 58.9 us
  waiting for transfers between devices: 48.8 us -> 17.7 us
  blocking collectives: 19.7 us -> 0 us
  Pallas kernels: 0 us -> 13.9 us
  local copies, waits for them, and re-layouts: 12.6 us -> 1.43 us
  matrix products: 10.7 us -> 0 us
  other arithmetic: 9.94 us -> 1.2 us
    ppermute x6 -> x52, starting transfers between devices: 15.9 us -> 58.9 us  [send(): return lax.ppermute(array, ('lev', 'tile'), pairs)]
    all_to_all x1 -> x0, blocking collectives: 19.7 us -> none  [per_device(): lax.all_to_all(mixed, 'lev', split_axis=0, concat_axis=2, tiled=True)]
    all_to_all x1 -> x0, waiting for transfers between devices: 16.5 us -> none  [per_device(): lax.all_to_all(current, 'lev', split_axis=2, concat_axis=0, tiled=True)]
    ppermute x6 -> x52, waiting for transfers between devices: 32.3 us -> 17.7 us  [send(): return lax.ppermute(array, ('lev', 'tile'), pairs)]
    pallas_call x0 -> x13, Pallas kernels: none -> 13.9 us  [the longest x4 9.89 us: advect(): pl.pallas_call(functools.partial(advect_kernel, lev_count, faces is None)...]
    dot_general x8 -> x0, matrix products: 10.7 us -> none  [mix_columns(): jnp.einsum('fij,jfxy->ifxy', operators[:, cat], column, precision=lax.Pre...]
    mul x12 -> x0, other arithmetic: 4.76 us -> none  [the longest x6 3.43 us: tendency(): flux_y = 0.5 * (v_inner + jnp.roll(v_inner, -1, axis=3)) * face_y]
    add x3 -> x0, other arithmetic: 4.44 us -> none  [per_device(): current = fields + coef * tendency(extended)]
  transfers between devices with their start and end apart: 7 -> 52, of which waited for: 7 -> 9; matrix products, arithmetic and copies ran while one was open for 5% -> 1% of each run, Pallas kernels for 0% -> 13%
where the time goes in v1:
time: 93.5 us; the launch traced here: 93.4 us
  starting transfers between devices  58.9 us (63%)
  waiting for transfers between devices  17.7 us (19%)
  Pallas kernels  13.9 us (15%)
  local copies, waits for them, and re-layouts  1.43 us (2%)
  other arithmetic  1.2 us (1%)
    ppermute x52, starting transfers between devices, send(): return lax.ppermute(array, ('lev', 'tile'), pairs)  58.9 us
    ppermute x52, waiting for transfers between devices, send(): return lax.ppermute(array, ('lev', 'tile'), pairs)  17.7 us
    pallas_call x4, Pallas kernels, advect(): pl.pallas_call(functools.partial(advect_kernel, lev_count, faces is None)...  9.89 us
    pallas_call x4, Pallas kernels, mix(): pl.pallas_call(functools.partial(mix_kernel, lev_count), out_shape=[sds(o...  2.26 us
  transfers between devices with their start and end apart: 52, of which 9 were waited for; matrix products, arithmetic and copies ran while one was open for 1% of the time, Pallas kernels for 13%

profile of v1, /device:TPU:0, one launch (start us, length us, event | category | flops | bytes accessed | tf_op | source)
XLA Modules:
  0.0 93.4 jit_solution(1454490279360509564)
XLA Ops:
  1.4 3.0 %collective-permute-start = (f32[8,2,8,512]{3,2,1,0:T(8,128)S(1)}, f32[8,2,8,512]{3,2,1,0:T(8,128)S(1)}, u32[]{:S(2)}, u32[]{:S(2)}) collective-permute-start(f32[8,2,8,512]{3,2,1,0:T(8,128)S(1)} %get-tuple-element.70), channel_id=1, source_target_pairs={{0,1},{1,0},{2,3},{3,2},{4,5},{5,4},{6,7},{7,6},{8,9},{9,8},{10,11... | collective-permute-start | bytes 786440 | tf_op jit(solution)/shard_map/ppermute | solution.py:238
  4.6 4.2 %collective-permute-start.2 = (f32[6,2,8,512]{3,2,1,0:T(8,128)S(1)}, f32[6,2,8,512]{3,2,1,0:T(8,128)S(1)}, u32[]{:S(2)}, u32[]{:S(2)}) collective-permute-start(f32[6,2,8,512]{3,2,1,0:T(8,128)S(1)} %slice.37), channel_id=1, source_target_pairs={{0,6},{1,3},{2,0},{3,5},{4,2},{5,7},{6,4},{7,1},{8,14},{9,11},{10,... | collective-permute-start | bytes 589832 | tf_op jit(solution)/shard_map/ppermute | solution.py:238
  8.8 2.8 %collective-permute-done.recv = f32[8,2,8,512]{3,2,1,0:T(8,128)S(1)} collective-permute-done((f32[8,2,8,512]{3,2,1,0:T(8,128)S(1)}, f32[8,2,8,512]{3,2,1,0:T(8,128)S(1)}, u32[]{:S(2)}, u32[]{:S(2)}) %collective-permute-start) | collective-permute-done | bytes 262176 | tf_op jit(solution)/shard_map/ppermute | solution.py:238
  11.6 2.2 %collective-permute-start.1 = (f32[6,2,8,512]{3,2,1,0:T(8,128)S(1)}, f32[6,2,8,512]{3,2,1,0:T(8,128)S(1)}, u32[]{:S(2)}, u32[]{:S(2)}) collective-permute-start(f32[6,2,8,512]{3,2,1,0:T(8,128)S(1)} %slice.47), channel_id=1, source_target_pairs={{0,2},{1,7},{2,4},{3,1},{4,6},{5,3},{6,0},{7,5},{8,10},{9,15},{10,... | collective-permute-start | bytes 589832 | tf_op jit(solution)/shard_map/ppermute | solution.py:238
  13.8 3.6 %collective-permute-start.26 = (f32[8,1,8,512]{3,2,1,0:T(8,128)S(1)}, f32[8,1,8,512]{3,2,1,0:T(8,128)S(1)}, u32[]{:S(2)}, u32[]{:S(2)}) collective-permute-start(f32[8,1,8,512]{3,2,1,0:T(8,128)S(1)} %get-tuple-element.107), channel_id=1, source_target_pairs={{0,1},{1,0},{2,3},{3,2},{4,5},{5,4},{6,7},{7,6},{8,9},{9,8},{10,11... | collective-permute-start | bytes 393224 | tf_op jit(solution)/shard_map/ppermute | solution.py:238
  18.4 3.9 %collective-permute-done.15.after = f32[6,1,8,512]{3,2,1,0:T(8,128)S(1)} collective-permute-done((f32[6,1,8,512]{3,2,1,0:T(8,128)S(1)}, f32[6,1,8,512]{3,2,1,0:T(8,128)S(1)}, u32[]{:S(2)}, u32[]{:S(2)}) %collective-permute-start.15) | collective-permute-done | bytes 98336 | tf_op jit(solution)/shard_map/ppermute | solution.py:238
  22.3 3.8 %collective-permute-start.28 = (f32[6,1,8,512]{3,2,1,0:T(8,128)S(1)}, f32[6,1,8,512]{3,2,1,0:T(8,128)S(1)}, u32[]{:S(2)}, u32[]{:S(2)}) collective-permute-start(f32[6,1,8,512]{3,2,1,0:T(8,128)S(1)} %slice.43), channel_id=1, source_target_pairs={{0,6},{1,3},{2,0},{3,5},{4,2},{5,7},{6,4},{7,1},{8,14},{9,11},{10,... | collective-permute-start | bytes 294920 | tf_op jit(solution)/shard_map/ppermute | solution.py:238
  26.3 3.9 %collective-permute-start.41 = (f32[6,1,8,512]{3,2,1,0:T(8,128)S(1)}, f32[6,1,8,512]{3,2,1,0:T(8,128)S(1)}, u32[]{:S(2)}, u32[]{:S(2)}) collective-permute-start(f32[6,1,8,512]{3,2,1,0:T(8,128)S(1)} %slice.46), channel_id=1, source_target_pairs={{0,6},{1,3},{2,0},{3,5},{4,2},{5,7},{6,4},{7,1},{8,14},{9,11},{10,... | collective-permute-start | bytes 294920 | tf_op jit(solution)/shard_map/ppermute | solution.py:238
  30.2 3.3 %shard_map.38 = (f32[25,8,512]{2,1,0:T(8,128)S(1)}, f32[24,8,512]{2,1,0:T(8,128)S(1)}, f32[24,8,512]{2,1,0:T(8,128)S(1)}, f32[21,8,512]{2,1,0:T(8,128)S(1)}, f32...) custom-call(f32[6,2,8,512]{3,2,1,0:T(8,128)S(1)} %collective-permute, ...), custom_call_target="tpu_custom_call" | custom-call | flops 14745600 | bytes 917504 | tf_op jit(solution)/shard_map/pallas_call | solution.py:139
  33.5 2.2 %shard_map.41 = (f32[2,1,8,512]{3,2,1,0:T(8,128)S(1)}, f32[2,1,8,512]{3,2,1,0:T(8,128)S(1)}, f32[2,1,8,512]{3,2,1,0:T(8,128)S(1)}, f32[2,1,8,512]{3,2,1,0:T(8,12...) custom-call(f32[6,1,8,512]{3,2,1,0:T(8,128)S(1)} %collective-permute, ...), custom_call_target="tpu_custom_call" | custom-call | flops 7372800 | bytes 3457024 | tf_op jit(solution)/shard_map/pallas_call | solution.py:139
  35.7 4.0 %collective-permute-start.16 = (f32[2,1,8,512]{3,2,1,0:T(8,128)S(1)}, f32[2,1,8,512]{3,2,1,0:T(8,128)S(1)}, u32[]{:S(2)}, u32[]{:S(2)}) collective-permute-start(f32[2,1,8,512]{3,2,1,0:T(8,128)S(1)} %get-tuple-element.96), channel_id=1, source_target_pairs={{0,1},{1,0},{2,3},{3,2},{4,5},{5,4},{6,7},{7,6},{8,9},{9,8},{10,11... | collective-permute-start | bytes 98312 | tf_op jit(solution)/shard_map/ppermute | solution.py:238
  39.9 2.2 %shard_map.44 = (f32[2,1,8,512]{3,2,1,0:T(8,128)S(1)}, f32[2,1,8,512]{3,2,1,0:T(8,128)S(1)}, f32[2,1,8,512]{3,2,1,0:T(8,128)S(1)}, f32[2,1,8,512]{3,2,1,0:T(8,12...) custom-call(f32[6,1,8,512]{3,2,1,0:T(8,128)S(1)} %collective-permute, ...), custom_call_target="tpu_custom_call" | custom-call | flops 7372800 | bytes 3457024 | tf_op jit(solution)/shard_map/pallas_call | solution.py:139
  42.1 1.6 %collective-permute-start.19 = (f32[2,1,8,512]{3,2,1,0:T(8,128)S(1)}, f32[2,1,8,512]{3,2,1,0:T(8,128)S(1)}, u32[]{:S(2)}, u32[]{:S(2)}) collective-permute-start(f32[2,1,8,512]{3,2,1,0:T(8,128)S(1)} %get-tuple-element.99), channel_id=1, source_target_pairs={{0,16},{1,17},{2,18},{3,19},{4,20},{5,21},{6,22},{7,23},{8,24},{9,... | collective-permute-start | bytes 98312 | tf_op jit(solution)/shard_map/ppermute | solution.py:238
  43.7 1.9 %collective-permute-start.20 = (f32[2,1,8,512]{3,2,1,0:T(8,128)S(1)}, f32[2,1,8,512]{3,2,1,0:T(8,128)S(1)}, u32[]{:S(2)}, u32[]{:S(2)}) collective-permute-start(f32[2,1,8,512]{3,2,1,0:T(8,128)S(1)} %get-tuple-element.100), channel_id=1, source_target_pairs={{0,17},{1,16},{2,19},{3,18},{4,21},{5,20},{6,23},{7,22},{8,25},{9,... | collective-permute-start | bytes 98312 | tf_op jit(solution)/shard_map/ppermute | solution.py:238
  46.9 1.9 %collective-permute-start.29 = (f32[2,1,8,512]{3,2,1,0:T(8,128)S(1)}, f32[2,1,8,512]{3,2,1,0:T(8,128)S(1)}, u32[]{:S(2)}, u32[]{:S(2)}) collective-permute-start(f32[2,1,8,512]{3,2,1,0:T(8,128)S(1)} %get-tuple-element.110), channel_id=1, source_target_pairs={{0,1},{1,0},{2,3},{3,2},{4,5},{5,4},{6,7},{7,6},{8,9},{9,8},{10,11... | collective-permute-start | bytes 98312 | tf_op jit(solution)/shard_map/ppermute | solution.py:238
  50.5 1.9 %collective-permute-start.33 = (f32[2,1,8,512]{3,2,1,0:T(8,128)S(1)}, f32[2,1,8,512]{3,2,1,0:T(8,128)S(1)}, u32[]{:S(2)}, u32[]{:S(2)}) collective-permute-start(f32[2,1,8,512]{3,2,1,0:T(8,128)S(1)} %get-tuple-element.114), channel_id=1, source_target_pairs={{0,17},{1,16},{2,19},{3,18},{4,21},{5,20},{6,23},{7,22},{8,25},{9,... | collective-permute-start | bytes 98312 | tf_op jit(solution)/shard_map/ppermute | solution.py:238
  53.0 2.2 %shard_map.47 = (f32[2,1,8,512]{3,2,1,0:T(8,128)S(1)}, f32[2,1,8,512]{3,2,1,0:T(8,128)S(1)}, f32[2,1,8,512]{3,2,1,0:T(8,128)S(1)}, f32[2,1,8,512]{3,2,1,0:T(8,12...) custom-call(f32[6,1,8,512]{3,2,1,0:T(8,128)S(1)} %collective-permute, ...), custom_call_target="tpu_custom_call" | custom-call | flops 7372800 | bytes 3457024 | tf_op jit(solution)/shard_map/pallas_call | solution.py:139
  56.3 1.6 %collective-permute-start.42 = (f32[2,1,8,512]{3,2,1,0:T(8,128)S(1)}, f32[2,1,8,512]{3,2,1,0:T(8,128)S(1)}, u32[]{:S(2)}, u32[]{:S(2)}) collective-permute-start(f32[2,1,8,512]{3,2,1,0:T(8,128)S(1)} %get-tuple-element.124), channel_id=1, source_target_pairs={{0,1},{1,0},{2,3},{3,2},{4,5},{5,4},{6,7},{7,6},{8,9},{9,8},{10,11... | collective-permute-start | bytes 98312 | tf_op jit(solution)/shard_map/ppermute | solution.py:238
  58.5 1.5 %collective-permute-start.45 = (f32[2,1,8,512]{3,2,1,0:T(8,128)S(1)}, f32[2,1,8,512]{3,2,1,0:T(8,128)S(1)}, u32[]{:S(2)}, u32[]{:S(2)}) collective-permute-start(f32[2,1,8,512]{3,2,1,0:T(8,128)S(1)} %get-tuple-element.127), channel_id=1, source_target_pairs={{0,16},{1,17},{2,18},{3,19},{4,20},{5,21},{6,22},{7,23},{8,24},{9,... | collective-permute-start | bytes 98312 | tf_op jit(solution)/shard_map/ppermute | solution.py:238
  60.0 1.6 %collective-permute-start.3 = (f32[2,2,8,512]{3,2,1,0:T(8,128)S(1)}, f32[2,2,8,512]{3,2,1,0:T(8,128)S(1)}, u32[]{:S(2)}, u32[]{:S(2)}) collective-permute-start(f32[2,2,8,512]{3,2,1,0:T(8,128)S(1)} %get-tuple-element.73), channel_id=1, source_target_pairs={{0,1},{1,0},{2,3},{3,2},{4,5},{5,4},{6,7},{7,6},{8,9},{9,8},{10,11... | collective-permute-start | bytes 196616 | tf_op jit(solution)/shard_map/ppermute | solution.py:238
  61.6 1.5 %collective-permute-start.46 = (f32[2,1,8,512]{3,2,1,0:T(8,128)S(1)}, f32[2,1,8,512]{3,2,1,0:T(8,128)S(1)}, u32[]{:S(2)}, u32[]{:S(2)}) collective-permute-start(f32[2,1,8,512]{3,2,1,0:T(8,128)S(1)} %get-tuple-element.128), channel_id=1, source_target_pairs={{0,17},{1,16},{2,19},{3,18},{4,21},{5,20},{6,23},{7,22},{8,25},{9,... | collective-permute-start | bytes 98312 | tf_op jit(solution)/shard_map/ppermute | solution.py:238
  65.1 1.5 %collective-permute-done.46.refs_5_ = f32[2,1,8,512]{3,2,1,0:T(8,128)S(1)} collective-permute-done((f32[2,1,8,512]{3,2,1,0:T(8,128)S(1)}, f32[2,1,8,512]{3,2,1,0:T(8,128)S(1)}, u32[]{:S(2)}, u32[]{:S(2)}) %collective-permute-start.46) | collective-permute-done | bytes 32800 | tf_op jit(solution)/shard_map/ppermute | solution.py:238
  70.3 1.6 %collective-permute-start.9 = (f32[2,2,8,512]{3,2,1,0:T(8,128)S(1)}, f32[2,2,8,512]{3,2,1,0:T(8,128)S(1)}, u32[]{:S(2)}, u32[]{:S(2)}) collective-permute-start(f32[2,2,8,512]{3,2,1,0:T(8,128)S(1)} %get-tuple-element.79), channel_id=1, source_target_pairs={{0,25},{1,24},{2,27},{3,26},{4,29},{5,28},{6,31},{7,30},{8,17},{9,... | collective-permute-start | bytes 196616 | tf_op jit(solution)/shard_map/ppermute | solution.py:238
  85.2 5.8 %collective-permute-done.50.refs_14_ = f32[2,1,16,512]{3,2,1,0:T(8,128)S(1)} collective-permute-done((f32[2,1,16,512]{3,2,1,0:T(8,128)S(1)}, f32[2,1,16,512]{3,2,1,0:T(8,128)S(1)}, u32[]{:S(2)}, u32[]{:S(2)}) %collective-permute-start.50) | collective-permute-done | bytes 65568 | tf_op jit(solution)/shard_map/ppermute | solution.py:238
  (111 shorter events, 29.6 us)
Async XLA Ops:
  1.4 10.1 %collective-permute-start = (f32[8,2,8,512]{3,2,1,0:T(8,128)S(1)}, f32[8,2,8,512]{3,2,1,0:T(8,128)S(1)}, u32[]{:S(2)}, u32[]{:S(2)}) collective-permute-start(f32[8,2,8,512]{3,2,1,0:T(8,128)S(1)} %get-tuple-element.70), channel_id=1, source_target_pairs={{0,1},{1,0},{2,3},{3,2},{4,5},{5,4},{6,7},{7,6},{8,9},{9,8},{10,11... | collective-permute-start | bytes 786440 | tf_op jit(solution)/shard_map/ppermute | solution.py:238
  4.5 13.1 %collective-permute-start.13 = (f32[8,1,8,512]{3,2,1,0:T(8,128)S(1)}, f32[8,1,8,512]{3,2,1,0:T(8,128)S(1)}, u32[]{:S(2)}, u32[]{:S(2)}) collective-permute-start(f32[8,1,8,512]{3,2,1,0:T(8,128)S(1)} %get-tuple-element.84), channel_id=1, source_target_pairs={{0,1},{1,0},{2,3},{3,2},{4,5},{5,4},{6,7},{7,6},{8,9},{9,8},{10,11... | collective-permute-start | bytes 393224 | tf_op jit(solution)/shard_map/ppermute | solution.py:238
  4.6 21.6 %collective-permute-start.2 = (f32[6,2,8,512]{3,2,1,0:T(8,128)S(1)}, f32[6,2,8,512]{3,2,1,0:T(8,128)S(1)}, u32[]{:S(2)}, u32[]{:S(2)}) collective-permute-start(f32[6,2,8,512]{3,2,1,0:T(8,128)S(1)} %slice.37), channel_id=1, source_target_pairs={{0,6},{1,3},{2,0},{3,5},{4,2},{5,7},{6,4},{7,1},{8,14},{9,11},{10,... | collective-permute-start | bytes 589832 | tf_op jit(solution)/shard_map/ppermute | solution.py:238
  11.6 18.5 %collective-permute-start.1 = (f32[6,2,8,512]{3,2,1,0:T(8,128)S(1)}, f32[6,2,8,512]{3,2,1,0:T(8,128)S(1)}, u32[]{:S(2)}, u32[]{:S(2)}) collective-permute-start(f32[6,2,8,512]{3,2,1,0:T(8,128)S(1)} %slice.47), channel_id=1, source_target_pairs={{0,2},{1,7},{2,4},{3,1},{4,6},{5,3},{6,0},{7,5},{8,10},{9,15},{10,... | collective-permute-start | bytes 589832 | tf_op jit(solution)/shard_map/ppermute | solution.py:238
  13.8 8.5 %collective-permute-start.26 = (f32[8,1,8,512]{3,2,1,0:T(8,128)S(1)}, f32[8,1,8,512]{3,2,1,0:T(8,128)S(1)}, u32[]{:S(2)}, u32[]{:S(2)}) collective-permute-start(f32[8,1,8,512]{3,2,1,0:T(8,128)S(1)} %get-tuple-element.107), channel_id=1, source_target_pairs={{0,1},{1,0},{2,3},{3,2},{4,5},{5,4},{6,7},{7,6},{8,9},{9,8},{10,11... | collective-permute-start | bytes 393224 | tf_op jit(solution)/shard_map/ppermute | solution.py:238
  17.5 8.7 %collective-permute-start.39 = (f32[8,1,8,512]{3,2,1,0:T(8,128)S(1)}, f32[8,1,8,512]{3,2,1,0:T(8,128)S(1)}, u32[]{:S(2)}, u32[]{:S(2)}) collective-permute-start(f32[8,1,8,512]{3,2,1,0:T(8,128)S(1)} %get-tuple-element.121), channel_id=1, source_target_pairs={{0,1},{1,0},{2,3},{3,2},{4,5},{5,4},{6,7},{7,6},{8,9},{9,8},{10,11... | collective-permute-start | bytes 393224 | tf_op jit(solution)/shard_map/ppermute | solution.py:238
  22.3 11.3 %collective-permute-start.14 = (f32[6,1,8,512]{3,2,1,0:T(8,128)S(1)}, f32[6,1,8,512]{3,2,1,0:T(8,128)S(1)}, u32[]{:S(2)}, u32[]{:S(2)}) collective-permute-start(f32[6,1,8,512]{3,2,1,0:T(8,128)S(1)} %slice.48), channel_id=1, source_target_pairs={{0,2},{1,7},{2,4},{3,1},{4,6},{5,3},{6,0},{7,5},{8,10},{9,15},{10,... | collective-permute-start | bytes 294920 | tf_op jit(solution)/shard_map/ppermute | solution.py:238
  22.3 17.4 %collective-permute-start.28 = (f32[6,1,8,512]{3,2,1,0:T(8,128)S(1)}, f32[6,1,8,512]{3,2,1,0:T(8,128)S(1)}, u32[]{:S(2)}, u32[]{:S(2)}) collective-permute-start(f32[6,1,8,512]{3,2,1,0:T(8,128)S(1)} %slice.43), channel_id=1, source_target_pairs={{0,6},{1,3},{2,0},{3,5},{4,2},{5,7},{6,4},{7,1},{8,14},{9,11},{10,... | collective-permute-start | bytes 294920 | tf_op jit(solution)/shard_map/ppermute | solution.py:238
  26.2 13.5 %collective-permute-start.27 = (f32[6,1,8,512]{3,2,1,0:T(8,128)S(1)}, f32[6,1,8,512]{3,2,1,0:T(8,128)S(1)}, u32[]{:S(2)}, u32[]{:S(2)}) collective-permute-start(f32[6,1,8,512]{3,2,1,0:T(8,128)S(1)} %slice.49), channel_id=1, source_target_pairs={{0,2},{1,7},{2,4},{3,1},{4,6},{5,3},{6,0},{7,5},{8,10},{9,15},{10,... | collective-permute-start | bytes 294920 | tf_op jit(solution)/shard_map/ppermute | solution.py:238
  26.3 15.8 %collective-permute-start.41 = (f32[6,1,8,512]{3,2,1,0:T(8,128)S(1)}, f32[6,1,8,512]{3,2,1,0:T(8,128)S(1)}, u32[]{:S(2)}, u32[]{:S(2)}) collective-permute-start(f32[6,1,8,512]{3,2,1,0:T(8,128)S(1)} %slice.46), channel_id=1, source_target_pairs={{0,6},{1,3},{2,0},{3,5},{4,2},{5,7},{6,4},{7,1},{8,14},{9,11},{10,... | collective-permute-start | bytes 294920 | tf_op jit(solution)/shard_map/ppermute | solution.py:238
  30.1 13.6 %collective-permute-start.40 = (f32[6,1,8,512]{3,2,1,0:T(8,128)S(1)}, f32[6,1,8,512]{3,2,1,0:T(8,128)S(1)}, u32[]{:S(2)}, u32[]{:S(2)}) collective-permute-start(f32[6,1,8,512]{3,2,1,0:T(8,128)S(1)} %slice.50), channel_id=1, source_target_pairs={{0,2},{1,7},{2,4},{3,1},{4,6},{5,3},{6,0},{7,5},{8,10},{9,15},{10,... | collective-permute-start | bytes 294920 | tf_op jit(solution)/shard_map/ppermute | solution.py:238
  35.7 9.8 %collective-permute-start.16 = (f32[2,1,8,512]{3,2,1,0:T(8,128)S(1)}, f32[2,1,8,512]{3,2,1,0:T(8,128)S(1)}, u32[]{:S(2)}, u32[]{:S(2)}) collective-permute-start(f32[2,1,8,512]{3,2,1,0:T(8,128)S(1)} %get-tuple-element.96), channel_id=1, source_target_pairs={{0,1},{1,0},{2,3},{3,2},{4,5},{5,4},{6,7},{7,6},{8,9},{9,8},{10,11... | collective-permute-start | bytes 98312 | tf_op jit(solution)/shard_map/ppermute | solution.py:238
  39.7 7.2 %collective-permute-start.18 = (f32[2,1,8,512]{3,2,1,0:T(8,128)S(1)}, f32[2,1,8,512]{3,2,1,0:T(8,128)S(1)}, u32[]{:S(2)}, u32[]{:S(2)}) collective-permute-start(f32[2,1,8,512]{3,2,1,0:T(8,128)S(1)} %get-tuple-element.98), channel_id=1, source_target_pairs={{0,9},{1,8},{2,11},{3,10},{4,13},{5,12},{6,15},{7,14},{8,1},{9,0},... | collective-permute-start | bytes 98312 | tf_op jit(solution)/shard_map/ppermute | solution.py:238
  48.8 7.5 %collective-permute-start.31 = (f32[2,1,8,512]{3,2,1,0:T(8,128)S(1)}, f32[2,1,8,512]{3,2,1,0:T(8,128)S(1)}, u32[]{:S(2)}, u32[]{:S(2)}) collective-permute-start(f32[2,1,8,512]{3,2,1,0:T(8,128)S(1)} %get-tuple-element.112), channel_id=1, source_target_pairs={{0,9},{1,8},{2,11},{3,10},{4,13},{5,12},{6,15},{7,14},{8,1},{9,0},... | collective-permute-start | bytes 98312 | tf_op jit(solution)/shard_map/ppermute | solution.py:238
  49.2 8.7 %collective-permute-start.32 = (f32[2,1,8,512]{3,2,1,0:T(8,128)S(1)}, f32[2,1,8,512]{3,2,1,0:T(8,128)S(1)}, u32[]{:S(2)}, u32[]{:S(2)}) collective-permute-start(f32[2,1,8,512]{3,2,1,0:T(8,128)S(1)} %get-tuple-element.113), channel_id=1, source_target_pairs={{0,16},{1,17},{2,18},{3,19},{4,20},{5,21},{6,22},{7,23},{8,24},{9,... | collective-permute-start | bytes 98312 | tf_op jit(solution)/shard_map/ppermute | solution.py:238
  50.5 7.4 %collective-permute-start.33 = (f32[2,1,8,512]{3,2,1,0:T(8,128)S(1)}, f32[2,1,8,512]{3,2,1,0:T(8,128)S(1)}, u32[]{:S(2)}, u32[]{:S(2)}) collective-permute-start(f32[2,1,8,512]{3,2,1,0:T(8,128)S(1)} %get-tuple-element.114), channel_id=1, source_target_pairs={{0,17},{1,16},{2,19},{3,18},{4,21},{5,20},{6,23},{7,22},{8,25},{9,... | collective-permute-start | bytes 98312 | tf_op jit(solution)/shard_map/ppermute | solution.py:238
  60.0 9.2 %collective-permute-start.3 = (f32[2,2,8,512]{3,2,1,0:T(8,128)S(1)}, f32[2,2,8,512]{3,2,1,0:T(8,128)S(1)}, u32[]{:S(2)}, u32[]{:S(2)}) collective-permute-start(f32[2,2,8,512]{3,2,1,0:T(8,128)S(1)} %get-tuple-element.73), channel_id=1, source_target_pairs={{0,1},{1,0},{2,3},{3,2},{4,5},{5,4},{6,7},{7,6},{8,9},{9,8},{10,11... | collective-permute-start | bytes 196616 | tf_op jit(solution)/shard_map/ppermute | solution.py:238
  61.6 8.7 %collective-permute-start.4 = (f32[2,2,8,512]{3,2,1,0:T(8,128)S(1)}, f32[2,2,8,512]{3,2,1,0:T(8,128)S(1)}, u32[]{:S(2)}, u32[]{:S(2)}) collective-permute-start(f32[2,2,8,512]{3,2,1,0:T(8,128)S(1)} %get-tuple-element.74), channel_id=1, source_target_pairs={{0,8},{1,9},{2,10},{3,11},{4,12},{5,13},{6,14},{7,15},{8,0},{9,1},... | collective-permute-start | bytes 196616 | tf_op jit(solution)/shard_map/ppermute | solution.py:238
  69.2 6.8 %collective-permute-start.8 = (f32[2,2,8,512]{3,2,1,0:T(8,128)S(1)}, f32[2,2,8,512]{3,2,1,0:T(8,128)S(1)}, u32[]{:S(2)}, u32[]{:S(2)}) collective-permute-start(f32[2,2,8,512]{3,2,1,0:T(8,128)S(1)} %get-tuple-element.78), channel_id=1, source_target_pairs={{0,24},{1,25},{2,26},{3,27},{4,28},{5,29},{6,30},{7,31},{8,16},{9,... | collective-permute-start | bytes 196616 | tf_op jit(solution)/shard_map/ppermute | solution.py:238
  80.3 11.6 %collective-permute-start.10 = (f32[2,2,16,512]{3,2,1,0:T(8,128)S(1)}, f32[2,2,16,512]{3,2,1,0:T(8,128)S(1)}, u32[]{:S(2)}, u32[]{:S(2)}) collective-permute-start(f32[2,2,16,512]{3,2,1,0:T(8,128)S(1)} %get-tuple-element.81), channel_id=1, source_target_pairs={{0,8},{1,9},{2,10},{3,11},{4,12},{5,13},{6,14},{7,15},{8,0},{9,1},... | collective-permute-start | bytes 393224 | tf_op jit(solution)/shard_map/ppermute | solution.py:238
  80.4 11.5 %collective-permute-start.11 = (f32[2,2,16,512]{3,2,1,0:T(8,128)S(1)}, f32[2,2,16,512]{3,2,1,0:T(8,128)S(1)}, u32[]{:S(2)}, u32[]{:S(2)}) collective-permute-start(f32[2,2,16,512]{3,2,1,0:T(8,128)S(1)} %get-tuple-element.82), channel_id=1, source_target_pairs={{0,16},{1,17},{2,18},{3,19},{4,20},{5,21},{6,22},{7,23},{8,24},{9,... | collective-permute-start | bytes 393224 | tf_op jit(solution)/shard_map/ppermute | solution.py:238
  81.6 10.3 %collective-permute-start.12 = (f32[2,2,16,512]{3,2,1,0:T(8,128)S(1)}, f32[2,2,16,512]{3,2,1,0:T(8,128)S(1)}, u32[]{:S(2)}, u32[]{:S(2)}) collective-permute-start(f32[2,2,16,512]{3,2,1,0:T(8,128)S(1)} %get-tuple-element.83), channel_id=1, source_target_pairs={{0,24},{1,25},{2,26},{3,27},{4,28},{5,29},{6,30},{7,31},{8,16},{9,... | collective-permute-start | bytes 393224 | tf_op jit(solution)/shard_map/ppermute | solution.py:238
  83.5 7.5 %collective-permute-start.50 = (f32[2,1,16,512]{3,2,1,0:T(8,128)S(1)}, f32[2,1,16,512]{3,2,1,0:T(8,128)S(1)}, u32[]{:S(2)}, u32[]{:S(2)}) collective-permute-start(f32[2,1,16,512]{3,2,1,0:T(8,128)S(1)} %get-tuple-element.133), channel_id=1, source_target_pairs={{0,16},{1,17},{2,18},{3,19},{4,20},{5,21},{6,22},{7,23},{8,24},{9,... | collective-permute-start | bytes 196616 | tf_op jit(solution)/shard_map/ppermute | solution.py:238
  84.3 7.6 %collective-permute-start.51 = (f32[2,1,16,512]{3,2,1,0:T(8,128)S(1)}, f32[2,1,16,512]{3,2,1,0:T(8,128)S(1)}, u32[]{:S(2)}, u32[]{:S(2)}) collective-permute-start(f32[2,1,16,512]{3,2,1,0:T(8,128)S(1)} %get-tuple-element.134), channel_id=1, source_target_pairs={{0,24},{1,25},{2,26},{3,27},{4,28},{5,29},{6,30},{7,31},{8,16},{9,... | collective-permute-start | bytes 196616 | tf_op jit(solution)/shard_map/ppermute | solution.py:238
  (31 other events, 169.5 us)

commit v2 on v1

v2 whole, which is shorter than its diff:
```python
import functools

import jax
import jax.numpy as jnp
from jax import lax
from jax.experimental import pallas as pl
from jax.experimental.pallas import tpu as pltpu
from jax.sharding import PartitionSpec as P

COURANT = 0.4
COEFS = (1.0 / 3.0, 0.5, 1.0)
CHUNKS = ((2, 3, 0), (1, 4))
HALO = 6
UNROLL = 4
VMEM = pl.BlockSpec(memory_space=pltpu.VMEM)
PARAMS = pltpu.CompilerParams(vmem_limit_bytes=14 * 2**20)
F32 = jnp.float32


def cost(flops, arrays):
    size = sum(a.size * a.dtype.itemsize for a in arrays)
    return pl.CostEstimate(flops=int(flops), bytes_accessed=int(size), transcendentals=0)


def sds(*shape, dtype=F32):
    return jax.ShapeDtypeStruct(shape, dtype)


def prep_kernel(chunk, x_ref, keep_ref, send_ref, edge_ref, buf, sem):
    rows, _, half, _ = keep_ref.shape
    odd = lax.rem(lax.axis_index("tile"), 2)
    copies = [pltpu.make_async_copy(x_ref.at[:, f], buf.at[n], sem.at[n]) for n, f in enumerate(chunk)]
    for copy in copies:
        copy.start()
    for n, copy in enumerate(copies):
        copy.wait()
        kept = jnp.swapaxes(buf[n, pl.ds(odd * half, half)], 0, 1)
        sent = jnp.swapaxes(buf[n, pl.ds((1 - odd) * half, half)], 0, 1)
        for r in range(rows):
            turned = jnp.where(odd == 0, r, rows - 1 - r)
            keep_ref[turned, n] = kept[r]
            send_ref[rows - 1 - turned, n] = sent[r]
    for r in range(HALO):
        edge_ref[r] = keep_ref[r]


def prep(fields, chunk):
    depth, _, rows, ny = fields.shape
    shape = sds(rows, len(chunk), depth // 2, ny)
    return pl.pallas_call(
        functools.partial(prep_kernel, chunk),
        out_shape=[shape, shape, sds(HALO, *shape.shape[1:])],
        in_specs=[pl.BlockSpec(memory_space=pltpu.HBM)],
        out_specs=[VMEM] * 3,
        scratch_shapes=[
            pltpu.VMEM((len(chunk), depth, rows, ny), F32),
            pltpu.SemaphoreType.DMA((len(chunk),)),
        ],
        compiler_params=PARAMS,
        cost_estimate=cost(shape.size * 2, [shape] * 4),
    )(fields)


def ops_kernel(per, ops_ref, out_ref):
    total, cats, levels, _ = ops_ref.shape
    core = lax.rem(lax.axis_index("lev"), 2)
    line = lax.broadcasted_iota(jnp.int32, (levels, 3 * levels), 0)
    column = lax.broadcasted_iota(jnp.int32, (levels, 3 * levels), 1)
    outer = ((column == line) | (column == line + 2 * levels)).astype(jnp.bfloat16)
    middle = (column == line + levels).astype(jnp.bfloat16)
    for f in range(total):
        rows = []
        for cat in range(cats):
            for low in range(0, levels, 2 * per):
                rows.append(ops_ref[f, cat, pl.ds(pl.multiple_of(low + core * per, 8), per), :])
        rows = jnp.concatenate(rows, axis=0)
        high = rows.astype(jnp.bfloat16)
        low = (rows - high.astype(F32)).astype(jnp.bfloat16)
        spread = jnp.dot(high, outer, preferred_element_type=F32)
        spread = spread + jnp.dot(low, middle, preferred_element_type=F32)
        out_ref[f] = spread.astype(jnp.bfloat16)


def lay_ops(column_ops, per):
    total, cats, levels, _ = column_ops.shape
    out = sds(total, cats * levels // 2, 3 * levels, dtype=jnp.bfloat16)
    return pl.pallas_call(
        functools.partial(ops_kernel, per),
        out_shape=out,
        in_specs=[VMEM],
        out_specs=VMEM,
        compiler_params=PARAMS,
        cost_estimate=cost(out.size, [out, column_ops]),
    )(column_ops)


def edge_kernel(recv_ref, *refs):
    out = refs[-1]
    for r in range(HALO):
        out[r] = recv_ref[recv_ref.shape[0] - HALO + r]


def edge(recv, *earlier):
    shape = sds(HALO, *recv.shape[1:])
    return pl.pallas_call(
        edge_kernel,
        out_shape=shape,
        in_specs=[VMEM] + [pl.BlockSpec(memory_space=pl.ANY)] * len(earlier),
        out_specs=VMEM,
        compiler_params=PARAMS,
        cost_estimate=cost(0, [shape] * 2),
    )(recv, *earlier)


def later_kernel(*refs):
    pass


def later(arrays, other):
    count = len(arrays)
    return list(
        pl.pallas_call(
            later_kernel,
            out_shape=[sds(*array.shape) for array in arrays],
            in_specs=[VMEM] * count + [pl.BlockSpec(memory_space=pl.ANY)],
            out_specs=[VMEM] * count,
            input_output_aliases={n: n for n in range(count)},
            compiler_params=PARAMS,
        )(*arrays, other)
    )


def roll(a, shift):
    return pltpu.roll(a, shift % a.shape[1], 1)


def in_groups(first, end, rows, state):
    if UNROLL is None:
        return rows(first, end - first, state)

    def body(step, state):
        return rows(first + step * UNROLL, UNROLL, state)

    return lax.fori_loop(0, (end - first) // UNROLL, body, state)


def stage_rows(first, last, base, off_base, old, off_old, new, off_new, faces, fields, scales):
    ux, vr, vl = faces

    def wind(i):
        if scales is not None:
            ux[i - first + 1] = (old[off_old + i, 0] + old[off_old + i + 1, 0]) * scales[0]
        return ux[i - first + 1]

    def face(i, n, u):
        near = old[off_old + i, n] + old[off_old + i + 1, n]
        far = old[off_old + i - 1, n] + old[off_old + i + 2, n]
        return u * (7.0 * near - far)

    def rows(low, count, flux):
        flux = list(flux)
        for more in range(count):
            i = low + more
            u = wind(i)
            for n in range(fields) if scales is None else (1, 0, *range(2, fields)):
                s = old[off_old + i, n]
                l1, l2, r1, r2 = roll(s, 1), roll(s, 2), roll(s, -1), roll(s, -2)
                left, right = s + l1, s + r1
                if scales is not None and n == 1:
                    vr[i - first] = right * scales[1]
                    vl[i - first] = left * scales[1]
                wide = vr[i - first] * (7.0 * right - (l1 + r2)) - vl[i - first] * (7.0 * left - (l2 + r1))
                here = face(i, n, u)
                new[off_new + i, n] = base[off_base + i, n] + ((here - flux[n]) + wide)
                flux[n] = here
        return tuple(flux)

    u = wind(first - 1)
    in_groups(first, last + 1, rows, tuple(face(first - 1, n, u) for n in range(fields)))


def gather_rows(parts, ext):
    at = 0
    for part in parts:
        for i in range(part.shape[0]):
            ext[at + i] = part[i]
        at += part.shape[0]


def scatter_blocks(adv, outs, chips, own):
    place = lax.axis_index("lev") // 2
    for a in range(chips):
        there = place ^ a
        for q in range(own):
            outs[2 * a][q] = adv[there * own + q]
            outs[2 * a + 1][q] = adv[2 * chips * own - 1 - there * own - q]


def advect_kernel(chips, winds, before, keep, recv, after, *refs):
    rows = 2 * keep.shape[0]
    own = keep.shape[0] // chips
    faces, outs = refs[:9], refs[9 : 9 + 2 * chips]
    ext, s1, s2, adv = refs[9 + 2 * chips :]
    gather_rows((before, keep, recv, after), ext)
    sign = jnp.where(lax.rem(lax.axis_index("tile"), 2) == 0, 1.0, -1.0).astype(F32)
    states = ((ext, HALO), (s1, HALO - 2), (s2, HALO - 4), (adv, 0))
    for k, coef in enumerate(COEFS):
        reach = HALO - 2 * (k + 1)
        scale = -COURANT * coef / 24.0
        stage_rows(
            -reach, rows - 1 + reach, ext, HALO, *states[k], *states[k + 1],
            faces[3 * k : 3 * k + 3], keep.shape[1], (sign * scale, scale) if winds else None,
        )
    scatter_blocks(adv, outs, chips, own)


def advect(parts, faces, chips):
    keep = parts[1]
    tile_rows, fields, half, ny = keep.shape
    rows = 2 * tile_rows
    own = tile_rows // chips
    block = sds(own, fields, half, ny)
    sizes = [rows + 2 * (HALO - 2 * (k + 1)) for k in range(3)]
    scratch = [pltpu.VMEM((n, fields, half, ny), F32) for n in (rows + 2 * HALO, *sizes[:2], rows)]
    blocks = [block] * (2 * chips)
    outs, args = blocks, parts
    if faces is None:
        outs = [sds(n, half, ny) for size in sizes for n in (size + 1, size, size)] + blocks
    else:
        args = (*parts, *faces)
    return pl.pallas_call(
        functools.partial(advect_kernel, chips, faces is None),
        out_shape=outs,
        in_specs=[VMEM] * len(args),
        out_specs=[VMEM] * len(outs),
        scratch_shapes=scratch,
        compiler_params=PARAMS,
        cost_estimate=cost(sum(sizes) * fields * half * ny * 30, args),
    )(*args)


def mix_kernel(chips, chunk, use_ref, ops_ref, *refs):
    blocks, outs = refs[: 4 * chips], refs[4 * chips : 5 * chips]
    token, data, result = refs[5 * chips :]
    token[...] = jnp.zeros_like(token)
    own, _, half, ny = blocks[0].shape
    levels, per = data.shape[0], 2 * half
    kept = chips * per
    cats = ops_ref.shape[1] // kept
    lev = lax.axis_index("lev")
    place, core = lev // 2, lax.rem(lev, 2)
    odd = lax.rem(lax.axis_index("tile"), 2)
    use = []
    for q in range(own):
        row = place * own + q
        row = jnp.where(odd == 0, row, use_ref.shape[0] - 1 - row)
        use.append(use_ref[pl.ds(row, 1), :])
    for n, f in enumerate(chunk):
        for c in range(2):
            for a in range(chips):
                for b in range(2):
                    source = 2 * (place ^ a) + (core ^ c)
                    at = pl.multiple_of(source * per + (odd ^ b) * half, 8)
                    for q in range(own):
                        data[pl.ds(at, half), q * ny : (q + 1) * ny] = blocks[2 * chips * c + 2 * a + b][q, n]
        for q in range(own):
            for col in range(0, ny, 256):
                cols = slice(q * ny + col, q * ny + col + 256)
                whole = data[:, cols]
                high = whole.astype(jnp.bfloat16)
                low = (whole - high.astype(F32)).astype(jnp.bfloat16)
                three = jnp.concatenate([high, high, low], axis=0)
                every = jnp.dot(ops_ref[f], three, preferred_element_type=F32)
                here = use[q][:, col : col + 256]
                mixed = every[:kept]
                for c in range(1, cats):
                    mixed = jnp.where(here == c, every[c * kept : (c + 1) * kept], mixed)
                result[:, cols] = mixed
        for a in range(chips):
            at = pl.multiple_of((place ^ a) * per, 8)
            for q in range(own):
                outs[a][q, n] = result[pl.ds(at, per), q * ny : (q + 1) * ny]


def mix(chunk, use, ops, blocks, chips):
    own, fields, half, ny = blocks[0].shape
    levels = ops.shape[2] // 3
    return pl.pallas_call(
        functools.partial(mix_kernel, chips, chunk),
        out_shape=[sds(own, fields, 2 * half, ny)] * chips + [sds(8, 128)],
        in_specs=[VMEM] * (2 + len(blocks)),
        out_specs=[VMEM] * (chips + 1),
        scratch_shapes=[
            pltpu.VMEM((levels, own * ny), F32),
            pltpu.VMEM((levels // 2, own * ny), F32),
        ],
        compiler_params=PARAMS,
        cost_estimate=cost(2 * fields * ops.shape[1] * ops.shape[2] * own * ny, blocks),
    )(use, ops, *blocks)


def final_kernel(chips, chunks, *refs):
    out, turn = refs[-2:]
    place = lax.axis_index("lev") // 2
    odd = lax.rem(lax.axis_index("tile"), 2)
    for c, chunk in enumerate(chunks):
        for n, f in enumerate(chunk):
            for a in range(chips):
                block = refs[c * chips + a]
                own = block.shape[0]
                for q in range(own):
                    row = (place ^ a) * own + q
                    row = jnp.where(odd == 0, row, own * chips - 1 - row)
                    turn[row] = block[q, n]
            for low in range(0, out.shape[0], 8):
                out[low : low + 8, f] = jnp.swapaxes(turn[:, low : low + 8], 0, 1)


def per_device(fields, land_use, column_ops):
    lev_count, tile_count = lax.axis_size("lev"), lax.axis_size("tile")
    depth, total, rows, ny = fields.shape

    def send(array, target):
        pairs = [
            (lev * tile_count + tile, there * tile_count + to)
            for lev in range(lev_count)
            for tile in range(tile_count)
            for there, to in [target(lev, tile)]
        ]
        return lax.ppermute(array, ("lev", "tile"), pairs)

    def outward(lev, tile):
        return lev, (tile + (2 if tile % 2 else -2)) % tile_count

    def inward(lev, tile):
        return lev, (tile + (-2 if tile % 2 else 2)) % tile_count

    def other(lev, tile):
        return lev, tile ^ 1

    chips = lev_count // 2
    ops = lay_ops(column_ops, depth)

    def outspread(outs):
        return [
            send(outs[2 * a + b], lambda lev, tile: (lev ^ 2 * a, tile ^ b)) if a + b else outs[0]
            for a in range(chips)
            for b in range(2)
        ]

    def both_cores(blocks):
        return blocks + [send(block, lambda lev, tile: (lev ^ 1, tile)) for block in blocks]

    def mixed_back(chunk, blocks):
        mixed = mix(chunk, land_use, ops, blocks, chips)
        back = [send(mixed[a], lambda lev, tile: (lev ^ 2 * a, tile)) if a else mixed[0] for a in range(chips)]
        return back, mixed[-1]

    first, second = CHUNKS
    keep_a, away_a, edge_a = prep(fields, first)
    recv_a = send(away_a, other)
    after_a = send(edge_a, outward)
    keep_b, away_b, edge_b = prep(fields, second)
    recv_a, away_b, edge_b = lax.optimization_barrier((recv_a, away_b, edge_b))
    before_a = send(edge(recv_a), inward)
    recv_b = send(away_b, other)
    after_b = send(edge_b, outward)
    outs_a = advect((before_a, keep_a, recv_a, after_a), None, chips)
    faces, outs_a = outs_a[:9], outs_a[9:]
    blocks_a = outspread(outs_a)
    before_b = send(edge(recv_b, before_a), inward)
    outs_b = advect((before_b, keep_b, recv_b, after_b), faces, chips)
    blocks_b = outspread(outs_b)
    returned, mixed = mixed_back(first, both_cores(blocks_a))
    blocks_b = later(blocks_b, mixed)
    returned += mixed_back(second, both_cores(blocks_b))[0]

    return pl.pallas_call(
        functools.partial(final_kernel, chips, CHUNKS),
        out_shape=sds(*fields.shape),
        in_specs=[VMEM] * len(returned),
        out_specs=VMEM,
        scratch_shapes=[pltpu.VMEM((rows, depth, ny), F32)],
        compiler_params=PARAMS,
        cost_estimate=cost(fields.size, returned + returned),
    )(*returned)


def solution(mesh):
    in_specs = (P("lev", None, "tile", None), P("tile", None), P())
    out_specs = P("lev", None, "tile", None)
    return jax.shard_map(
        per_device, mesh=mesh, in_specs=in_specs, out_specs=out_specs, check_vma=False
    )
```

time: 93.5 us -> 72.1 us (0.77)
  starting transfers between devices: 58.9 us -> 22.7 us
  waiting for transfers between devices: 17.7 us -> 35.2 us
  Pallas kernels: 13.9 us -> 12.5 us
  other arithmetic: 1.2 us -> 0 us
    ppermute x52 -> x22, starting transfers between devices: 58.9 us -> 22.7 us  [send(): return lax.ppermute(array, ('lev', 'tile'), pairs)]
    ppermute x52 -> x22, waiting for transfers between devices: 17.7 us -> 35.2 us  [send(): return lax.ppermute(array, ('lev', 'tile'), pairs)]
    pallas_call x13 -> x11, Pallas kernels: 13.9 us -> 12.5 us  [the longest x2 7.69 us: advect(): pl.pallas_call(functools.partial(advect_kernel, chips, faces is None), ou...]
  transfers between devices with their start and end apart: 52 -> 22, of which waited for: 9 -> 10; matrix products, arithmetic and copies ran while one was open for 1% -> 0% of each run, Pallas kernels for 13% -> 15%
where the time goes in v2:
time: 72.1 us; the launch traced here: 72 us
  waiting for transfers between devices  35.2 us (49%)
  starting transfers between devices  22.7 us (31%)
  Pallas kernels  12.5 us (17%)
  local copies, waits for them, and re-layouts  1.33 us (2%)
    ppermute x22, waiting for transfers between devices, send(): return lax.ppermute(array, ('lev', 'tile'), pairs)  35.2 us
    ppermute x22, starting transfers between devices, send(): return lax.ppermute(array, ('lev', 'tile'), pairs)  22.7 us
    pallas_call x2, Pallas kernels, advect(): pl.pallas_call(functools.partial(advect_kernel, chips, faces is None), ou...  7.69 us
    pallas_call x2, Pallas kernels, mix(): pl.pallas_call(functools.partial(mix_kernel, chips, chunk), out_shape=[sd...  2.53 us
  transfers between devices with their start and end apart: 22, of which 10 were waited for; matrix products, arithmetic and copies ran while one was open for 0% of the time, Pallas kernels for 15%

profile of v2, /device:TPU:0, one launch (start us, length us, event | category | flops | bytes accessed | tf_op | source)
XLA Modules:
  0.0 72.0 jit_solution(9130658779897229344)
XLA Ops:
  0.0 1.3 %copy-done = f32[16,5,8,512]{3,2,1,0:T(8,128)S(1)} copy-done((f32[16,5,8,512]{3,2,1,0:T(8,128)S(1)}, f32[16,5,8,512]{3,2,1,0:T(8,128)}, u32[]{:S(2)}) %copy-start) | copy-done | bytes 1310744
  1.6 3.0 %collective-permute-start = (f32[8,3,8,512]{3,2,1,0:T(8,128)S(1)}, f32[8,3,8,512]{3,2,1,0:T(8,128)S(1)}, u32[]{:S(2)}, u32[]{:S(2)}) collective-permute-start(f32[8,3,8,512]{3,2,1,0:T(8,128)S(1)} %get-tuple-element.40), channel_id=1, source_target_pairs={{0,1},{1,0},{2,3},{3,2},{4,5},{5,4},{6,7},{7,6},{8,9},{9,8},{10,11... | collective-permute-start | bytes 1179656 | tf_op jit(solution)/shard_map/ppermute | solution.py:330
  4.6 3.6 %collective-permute-start.2 = (f32[6,3,8,512]{3,2,1,0:T(8,128)S(1)}, f32[6,3,8,512]{3,2,1,0:T(8,128)S(1)}, u32[]{:S(2)}, u32[]{:S(2)}) collective-permute-start(f32[6,3,8,512]{3,2,1,0:T(8,128)S(1)} %get-tuple-element.45), channel_id=1, source_target_pairs={{0,6},{1,3},{2,0},{3,5},{4,2},{5,7},{6,4},{7,1},{8,14},{9,11},{10,... | collective-permute-start | bytes 884744 | tf_op jit(solution)/shard_map/ppermute | solution.py:330
  8.4 5.3 %collective-permute-done.recv_ref.recv = f32[8,3,8,512]{3,2,1,0:T(8,128)S(1)} collective-permute-done((f32[8,3,8,512]{3,2,1,0:T(8,128)S(1)}, f32[8,3,8,512]{3,2,1,0:T(8,128)S(1)}, u32[]{:S(2)}, u32[]{:S(2)}) %collective-permute-start) | collective-permute-done | bytes 393248 | tf_op jit(solution)/shard_map/ppermute | solution.py:330
  13.7 1.9 %collective-permute-start.1 = (f32[6,3,8,512]{3,2,1,0:T(8,128)S(1)}, f32[6,3,8,512]{3,2,1,0:T(8,128)S(1)}, u32[]{:S(2)}, u32[]{:S(2)}) collective-permute-start(f32[6,3,8,512]{3,2,1,0:T(8,128)S(1)} %shard_map.40), channel_id=1, source_target_pairs={{0,2},{1,7},{2,4},{3,1},{4,6},{5,3},{6,0},{7,5},{8,10},{9,15},{10,... | collective-permute-start | bytes 884744 | tf_op jit(solution)/shard_map/ppermute | solution.py:330
  15.6 3.5 %collective-permute-start.11 = (f32[8,2,8,512]{3,2,1,0:T(8,128)S(1)}, f32[8,2,8,512]{3,2,1,0:T(8,128)S(1)}, u32[]{:S(2)}, u32[]{:S(2)}) collective-permute-start(f32[8,2,8,512]{3,2,1,0:T(8,128)S(1)} %get-tuple-element.52), channel_id=1, source_target_pairs={{0,1},{1,0},{2,3},{3,2},{4,5},{5,4},{6,7},{7,6},{8,9},{9,8},{10,11... | collective-permute-start | bytes 786440 | tf_op jit(solution)/shard_map/ppermute | solution.py:330
  19.6 6.0 %collective-permute-done.1.before.refs_0_ = f32[6,3,8,512]{3,2,1,0:T(8,128)S(1)} collective-permute-done((f32[6,3,8,512]{3,2,1,0:T(8,128)S(1)}, f32[6,3,8,512]{3,2,1,0:T(8,128)S(1)}, u32[]{:S(2)}, u32[]{:S(2)}) %collective-permute-start.1) | collective-permute-done | bytes 294944 | tf_op jit(solution)/shard_map/ppermute | solution.py:330
  25.6 4.4 %shard_map.41 = (f32[25,8,512]{2,1,0:T(8,128)S(1)}, f32[24,8,512]{2,1,0:T(8,128)S(1)}, f32[24,8,512]{2,1,0:T(8,128)S(1)}, f32[21,8,512]{2,1,0:T(8,128)S(1)}, f32...) custom-call(f32[6,3,8,512]{3,2,1,0:T(8,128)S(1)} %collective-permute, ...), custom_call_target="tpu_custom_call" | custom-call | flops 22118400 | bytes 1376256 | tf_op jit(solution)/shard_map/pallas_call | solution.py:231
  30.0 1.1 %collective-permute-start.3 = (f32[4,3,8,512]{3,2,1,0:T(8,128)S(1)}, f32[4,3,8,512]{3,2,1,0:T(8,128)S(1)}, u32[]{:S(2)}, u32[]{:S(2)}) collective-permute-start(f32[4,3,8,512]{3,2,1,0:T(8,128)S(1)} %get-tuple-element.47), channel_id=1, source_target_pairs={{0,1},{1,0},{2,3},{3,2},{4,5},{5,4},{6,7},{7,6},{8,9},{9,8},{10,11... | collective-permute-start | bytes 589832 | tf_op jit(solution)/shard_map/ppermute | solution.py:330
  31.1 1.5 %collective-permute-start.4 = (f32[4,3,8,512]{3,2,1,0:T(8,128)S(1)}, f32[4,3,8,512]{3,2,1,0:T(8,128)S(1)}, u32[]{:S(2)}, u32[]{:S(2)}) collective-permute-start(f32[4,3,8,512]{3,2,1,0:T(8,128)S(1)} %get-tuple-element.48), channel_id=1, source_target_pairs={{0,16},{1,17},{2,18},{3,19},{4,20},{5,21},{6,22},{7,23},{8,24},{9,... | collective-permute-start | bytes 589832 | tf_op jit(solution)/shard_map/ppermute | solution.py:330
  33.8 2.0 %collective-permute-done.3.refs_1_ = f32[4,3,8,512]{3,2,1,0:T(8,128)S(1)} collective-permute-done((f32[4,3,8,512]{3,2,1,0:T(8,128)S(1)}, f32[4,3,8,512]{3,2,1,0:T(8,128)S(1)}, u32[]{:S(2)}, u32[]{:S(2)}) %collective-permute-start.3) | collective-permute-done | bytes 196640 | tf_op jit(solution)/shard_map/ppermute | solution.py:330
  35.8 2.2 %collective-permute-done.4.refs_2_ = f32[4,3,8,512]{3,2,1,0:T(8,128)S(1)} collective-permute-done((f32[4,3,8,512]{3,2,1,0:T(8,128)S(1)}, f32[4,3,8,512]{3,2,1,0:T(8,128)S(1)}, u32[]{:S(2)}, u32[]{:S(2)}) %collective-permute-start.4) | collective-permute-done | bytes 196640 | tf_op jit(solution)/shard_map/ppermute | solution.py:330
  37.9 1.2 %collective-permute-done.5.refs_3_ = f32[4,3,8,512]{3,2,1,0:T(8,128)S(1)} collective-permute-done((f32[4,3,8,512]{3,2,1,0:T(8,128)S(1)}, f32[4,3,8,512]{3,2,1,0:T(8,128)S(1)}, u32[]{:S(2)}, u32[]{:S(2)}) %collective-permute-start.5) | collective-permute-done | bytes 196640 | tf_op jit(solution)/shard_map/ppermute | solution.py:330
  39.2 2.2 %collective-permute-done.12.before = f32[6,2,8,512]{3,2,1,0:T(8,128)S(1)} collective-permute-done((f32[6,2,8,512]{3,2,1,0:T(8,128)S(1)}, f32[6,2,8,512]{3,2,1,0:T(8,128)S(1)}, u32[]{:S(2)}, u32[]{:S(2)}) %collective-permute-start.12) | collective-permute-done | bytes 196640 | tf_op jit(solution)/shard_map/ppermute | solution.py:330
  41.4 3.3 %shard_map.44 = (f32[4,2,8,512]{3,2,1,0:T(8,128)S(1)}, f32[4,2,8,512]{3,2,1,0:T(8,128)S(1)}, f32[4,2,8,512]{3,2,1,0:T(8,128)S(1)}, f32[4,2,8,512]{3,2,1,0:T(8,128)S(1)}) custom-call(f32[6,2,8,512]{3,2,1,0:T(8,128)S(1)} %collective-permute-done.12.before, f32[8,2,8,512]{3,2,1,0:T(8,128)S(1)} %get-tuple-element.53.keep, ...), custom_call_target="tpu_custom_call" | custom-call | flops 14745600 | bytes 3915776 | tf_op jit(solution)/shard_map/pallas_call | solution.py:231
  45.5 1.5 %collective-permute-start.15 = (f32[4,2,8,512]{3,2,1,0:T(8,128)S(1)}, f32[4,2,8,512]{3,2,1,0:T(8,128)S(1)}, u32[]{:S(2)}, u32[]{:S(2)}) collective-permute-start(f32[4,2,8,512]{3,2,1,0:T(8,128)S(1)} %get-tuple-element.66), channel_id=1, source_target_pairs={{0,16},{1,17},{2,18},{3,19},{4,20},{5,21},{6,22},{7,23},{8,24},{9,... | collective-permute-start | bytes 393224 | tf_op jit(solution)/shard_map/ppermute | solution.py:330
  47.0 1.3 %collective-permute-start.16 = (f32[4,2,8,512]{3,2,1,0:T(8,128)S(1)}, f32[4,2,8,512]{3,2,1,0:T(8,128)S(1)}, u32[]{:S(2)}, u32[]{:S(2)}) collective-permute-start(f32[4,2,8,512]{3,2,1,0:T(8,128)S(1)} %get-tuple-element.67), channel_id=1, source_target_pairs={{0,17},{1,16},{2,19},{3,18},{4,21},{5,20},{6,23},{7,22},{8,25},{9,... | collective-permute-start | bytes 393224 | tf_op jit(solution)/shard_map/ppermute | solution.py:330
  48.7 1.2 %shard_map.42 = (f32[4,3,16,512]{3,2,1,0:T(8,128)S(1)}, f32[4,3,16,512]{3,2,1,0:T(8,128)S(1)}, f32[8,128]{1,0:T(8,128)S(1)}) custom-call(s32[8,512]{1,0:T(8,128)S(1)} %copy-done.2, bf16[5,256,192]{2,1,0:T(8,128)(2,1)S(1)} %shard_map.37.ops_ref, f32[4,3,8,512]{3,2,1,0:T(8,128)S(1)} %get-tuple-element.46.refs_0_, ...), custom_call_target="tpu_custom_call" | custom-call | flops 603979776 | bytes 1572864 | tf_op jit(solution)/shard_map/pallas_call | solution.py:288
  51.4 1.4 %collective-permute-done.16.refs_3_ = f32[4,2,8,512]{3,2,1,0:T(8,128)S(1)} collective-permute-done((f32[4,2,8,512]{3,2,1,0:T(8,128)S(1)}, f32[4,2,8,512]{3,2,1,0:T(8,128)S(1)}, u32[]{:S(2)}, u32[]{:S(2)}) %collective-permute-start.16) | collective-permute-done | bytes 131104 | tf_op jit(solution)/shard_map/ppermute | solution.py:330
  53.9 1.0 %collective-permute-start.10 = (f32[4,3,16,512]{3,2,1,0:T(8,128)S(1)}, f32[4,3,16,512]{3,2,1,0:T(8,128)S(1)}, u32[]{:S(2)}, u32[]{:S(2)}) collective-permute-start(f32[4,3,16,512]{3,2,1,0:T(8,128)S(1)} %get-tuple-element.51), channel_id=1, source_target_pairs={{0,16},{1,17},{2,18},{3,19},{4,20},{5,21},{6,22},{7,23},{8,24},{9,... | collective-permute-start | bytes 1179656 | tf_op jit(solution)/shard_map/ppermute | solution.py:330
  54.9 1.4 %shard_map.46 = (f32[4,2,16,512]{3,2,1,0:T(8,128)S(1)}, f32[4,2,16,512]{3,2,1,0:T(8,128)S(1)}, f32[8,128]{1,0:T(8,128)}) custom-call(s32[8,512]{1,0:T(8,128)S(1)} %copy-done.2, bf16[5,256,192]{2,1,0:T(8,128)(2,1)S(1)} %shard_map.37.ops_ref, f32[4,2,8,512]{3,2,1,0:T(8,128)S(1)} %get-tuple-element.69.refs_0_, f32[4,2,8,512]{3,2,1,0:T(8,128)S(1)} %get-tuple-element.70.refs_1_, ...), custom_call_target="tpu_custom_call" | custom-call | flops 402653184 | bytes 1048576 | tf_op jit(solution)/shard_map/pallas_call | solution.py:288
  56.3 1.0 %collective-permute-start.21 = (f32[4,2,16,512]{3,2,1,0:T(8,128)S(1)}, f32[4,2,16,512]{3,2,1,0:T(8,128)S(1)}, u32[]{:S(2)}, u32[]{:S(2)}) collective-permute-start(f32[4,2,16,512]{3,2,1,0:T(8,128)S(1)} %get-tuple-element.74), channel_id=1, source_target_pairs={{0,16},{1,17},{2,18},{3,19},{4,20},{5,21},{6,22},{7,23},{8,24},{9,... | collective-permute-start | bytes 786440 | tf_op jit(solution)/shard_map/ppermute | solution.py:330
  57.3 13.2 %collective-permute-done.21.refs_3_ = f32[4,2,16,512]{3,2,1,0:T(8,128)S(1)} collective-permute-done((f32[4,2,16,512]{3,2,1,0:T(8,128)S(1)}, f32[4,2,16,512]{3,2,1,0:T(8,128)S(1)}, u32[]{:S(2)}, u32[]{:S(2)}) %collective-permute-start.21) | collective-permute-done | bytes 262176 | tf_op jit(solution)/shard_map/ppermute | solution.py:330
  70.5 1.4 %shard_map.47 = f32[16,5,8,512]{3,2,1,0:T(8,128)} custom-call(f32[4,3,16,512]{3,2,1,0:T(8,128)S(1)} %get-tuple-element.50.refs_0_, f32[4,3,16,512]{3,2,1,0:T(8,128)S(1)} %collective-permute-done.10.refs_1_, f32[4,2,16,512]{3,2,1,0:T(8,128)S(1)} %get-tuple-element.73.refs_2_, f32[4,2,16,512]{3,2,1,0:T(8,128)S(1)} %collective-permute-done.21.refs_3_), custom_call_target="tpu_custom_call" | custom-call | flops 327680 | bytes 2621440 | tf_op jit(solution)/shard_map/pallas_call | solution.py:378
  (37 shorter events, 5.8 us)
Async XLA Ops:
  1.6 12.1 %collective-permute-start = (f32[8,3,8,512]{3,2,1,0:T(8,128)S(1)}, f32[8,3,8,512]{3,2,1,0:T(8,128)S(1)}, u32[]{:S(2)}, u32[]{:S(2)}) collective-permute-start(f32[8,3,8,512]{3,2,1,0:T(8,128)S(1)} %get-tuple-element.40), channel_id=1, source_target_pairs={{0,1},{1,0},{2,3},{3,2},{4,5},{5,4},{6,7},{7,6},{8,9},{9,8},{10,11... | collective-permute-start | bytes 1179656 | tf_op jit(solution)/shard_map/ppermute | solution.py:330
  4.6 15.0 %collective-permute-start.2 = (f32[6,3,8,512]{3,2,1,0:T(8,128)S(1)}, f32[6,3,8,512]{3,2,1,0:T(8,128)S(1)}, u32[]{:S(2)}, u32[]{:S(2)}) collective-permute-start(f32[6,3,8,512]{3,2,1,0:T(8,128)S(1)} %get-tuple-element.45), channel_id=1, source_target_pairs={{0,6},{1,3},{2,0},{3,5},{4,2},{5,7},{6,4},{7,1},{8,14},{9,11},{10,... | collective-permute-start | bytes 884744 | tf_op jit(solution)/shard_map/ppermute | solution.py:330
  13.7 11.9 %collective-permute-start.1 = (f32[6,3,8,512]{3,2,1,0:T(8,128)S(1)}, f32[6,3,8,512]{3,2,1,0:T(8,128)S(1)}, u32[]{:S(2)}, u32[]{:S(2)}) collective-permute-start(f32[6,3,8,512]{3,2,1,0:T(8,128)S(1)} %shard_map.40), channel_id=1, source_target_pairs={{0,2},{1,7},{2,4},{3,1},{4,6},{5,3},{6,0},{7,5},{8,10},{9,15},{10,... | collective-permute-start | bytes 884744 | tf_op jit(solution)/shard_map/ppermute | solution.py:330
  15.6 18.0 %collective-permute-start.11 = (f32[8,2,8,512]{3,2,1,0:T(8,128)S(1)}, f32[8,2,8,512]{3,2,1,0:T(8,128)S(1)}, u32[]{:S(2)}, u32[]{:S(2)}) collective-permute-start(f32[8,2,8,512]{3,2,1,0:T(8,128)S(1)} %get-tuple-element.52), channel_id=1, source_target_pairs={{0,1},{1,0},{2,3},{3,2},{4,5},{5,4},{6,7},{7,6},{8,9},{9,8},{10,11... | collective-permute-start | bytes 786440 | tf_op jit(solution)/shard_map/ppermute | solution.py:330
  19.1 14.6 %collective-permute-start.13 = (f32[6,2,8,512]{3,2,1,0:T(8,128)S(1)}, f32[6,2,8,512]{3,2,1,0:T(8,128)S(1)}, u32[]{:S(2)}, u32[]{:S(2)}) collective-permute-start(f32[6,2,8,512]{3,2,1,0:T(8,128)S(1)} %get-tuple-element.54), channel_id=1, source_target_pairs={{0,6},{1,3},{2,0},{3,5},{4,2},{5,7},{6,4},{7,1},{8,14},{9,11},{10,... | collective-permute-start | bytes 589832 | tf_op jit(solution)/shard_map/ppermute | solution.py:330
  30.0 5.7 %collective-permute-start.3 = (f32[4,3,8,512]{3,2,1,0:T(8,128)S(1)}, f32[4,3,8,512]{3,2,1,0:T(8,128)S(1)}, u32[]{:S(2)}, u32[]{:S(2)}) collective-permute-start(f32[4,3,8,512]{3,2,1,0:T(8,128)S(1)} %get-tuple-element.47), channel_id=1, source_target_pairs={{0,1},{1,0},{2,3},{3,2},{4,5},{5,4},{6,7},{7,6},{8,9},{9,8},{10,11... | collective-permute-start | bytes 589832 | tf_op jit(solution)/shard_map/ppermute | solution.py:330
  31.1 6.8 %collective-permute-start.4 = (f32[4,3,8,512]{3,2,1,0:T(8,128)S(1)}, f32[4,3,8,512]{3,2,1,0:T(8,128)S(1)}, u32[]{:S(2)}, u32[]{:S(2)}) collective-permute-start(f32[4,3,8,512]{3,2,1,0:T(8,128)S(1)} %get-tuple-element.48), channel_id=1, source_target_pairs={{0,16},{1,17},{2,18},{3,19},{4,20},{5,21},{6,22},{7,23},{8,24},{9,... | collective-permute-start | bytes 589832 | tf_op jit(solution)/shard_map/ppermute | solution.py:330
  32.6 6.6 %collective-permute-start.5 = (f32[4,3,8,512]{3,2,1,0:T(8,128)S(1)}, f32[4,3,8,512]{3,2,1,0:T(8,128)S(1)}, u32[]{:S(2)}, u32[]{:S(2)}) collective-permute-start(f32[4,3,8,512]{3,2,1,0:T(8,128)S(1)} %get-tuple-element.49), channel_id=1, source_target_pairs={{0,17},{1,16},{2,19},{3,18},{4,21},{5,20},{6,23},{7,22},{8,25},{9,... | collective-permute-start | bytes 589832 | tf_op jit(solution)/shard_map/ppermute | solution.py:330
  33.6 7.8 %collective-permute-start.12 = (f32[6,2,8,512]{3,2,1,0:T(8,128)S(1)}, f32[6,2,8,512]{3,2,1,0:T(8,128)S(1)}, u32[]{:S(2)}, u32[]{:S(2)}) collective-permute-start(f32[6,2,8,512]{3,2,1,0:T(8,128)S(1)} %shard_map.43), channel_id=1, source_target_pairs={{0,2},{1,7},{2,4},{3,1},{4,6},{5,3},{6,0},{7,5},{8,10},{9,15},{10,... | collective-permute-start | bytes 589832 | tf_op jit(solution)/shard_map/ppermute | solution.py:330
  33.7 11.8 %collective-permute-start.6 = (f32[4,3,8,512]{3,2,1,0:T(8,128)S(1)}, f32[4,3,8,512]{3,2,1,0:T(8,128)S(1)}, u32[]{:S(2)}, u32[]{:S(2)}) collective-permute-start(f32[4,3,8,512]{3,2,1,0:T(8,128)S(1)} %get-tuple-element.46.refs_0_), channel_id=1, source_target_pairs={{0,8},{1,9},{2,10},{3,11},{4,12},{5,13},{6,14},{7,15},{8,0},{9,1},... | collective-permute-start | bytes 589832 | tf_op jit(solution)/shard_map/ppermute | solution.py:330
  35.8 11.2 %collective-permute-start.7 = (f32[4,3,8,512]{3,2,1,0:T(8,128)S(1)}, f32[4,3,8,512]{3,2,1,0:T(8,128)S(1)}, u32[]{:S(2)}, u32[]{:S(2)}) collective-permute-start(f32[4,3,8,512]{3,2,1,0:T(8,128)S(1)} %collective-permute-done.3.refs_1_), channel_id=1, source_target_pairs={{0,8},{1,9},{2,10},{3,11},{4,12},{5,13},{6,14},{7,15},{8,0},{9,1},... | collective-permute-start | bytes 589832 | tf_op jit(solution)/shard_map/ppermute | solution.py:330
  37.9 10.8 %collective-permute-start.8 = (f32[4,3,8,512]{3,2,1,0:T(8,128)S(1)}, f32[4,3,8,512]{3,2,1,0:T(8,128)S(1)}, u32[]{:S(2)}, u32[]{:S(2)}) collective-permute-start(f32[4,3,8,512]{3,2,1,0:T(8,128)S(1)} %collective-permute-done.4.refs_2_), channel_id=1, source_target_pairs={{0,8},{1,9},{2,10},{3,11},{4,12},{5,13},{6,14},{7,15},{8,0},{9,1},... | collective-permute-start | bytes 589832 | tf_op jit(solution)/shard_map/ppermute | solution.py:330
  39.2 9.5 %collective-permute-start.9 = (f32[4,3,8,512]{3,2,1,0:T(8,128)S(1)}, f32[4,3,8,512]{3,2,1,0:T(8,128)S(1)}, u32[]{:S(2)}, u32[]{:S(2)}) collective-permute-start(f32[4,3,8,512]{3,2,1,0:T(8,128)S(1)} %collective-permute-done.5.refs_3_), channel_id=1, source_target_pairs={{0,8},{1,9},{2,10},{3,11},{4,12},{5,13},{6,14},{7,15},{8,0},{9,1},... | collective-permute-start | bytes 589832 | tf_op jit(solution)/shard_map/ppermute | solution.py:330
  41.4 6.9 %copy-start.1 = (f32[5,8,64,64]{3,2,1,0:T(8,128)S(1)}, f32[5,8,64,64]{3,2,1,0:T(8,128)}, u32[]{:S(2)}) copy-start(f32[5,8,64,64]{3,2,1,0:T(8,128)} %ops_ref.1) | copy-start | bytes 1966084
  44.7 4.0 %copy-start.2 = (s32[8,512]{1,0:T(8,128)S(1)}, s32[8,512]{1,0:T(8,128)}, u32[]{:S(2)}) copy-start(s32[8,512]{1,0:T(8,128)} %use_ref.3) | copy-start | bytes 49156
  44.7 5.9 %collective-permute-start.14 = (f32[4,2,8,512]{3,2,1,0:T(8,128)S(1)}, f32[4,2,8,512]{3,2,1,0:T(8,128)S(1)}, u32[]{:S(2)}, u32[]{:S(2)}) collective-permute-start(f32[4,2,8,512]{3,2,1,0:T(8,128)S(1)} %get-tuple-element.65), channel_id=1, source_target_pairs={{0,1},{1,0},{2,3},{3,2},{4,5},{5,4},{6,7},{7,6},{8,9},{9,8},{10,11... | collective-permute-start | bytes 393224 | tf_op jit(solution)/shard_map/ppermute | solution.py:330
  45.5 6.0 %collective-permute-start.15 = (f32[4,2,8,512]{3,2,1,0:T(8,128)S(1)}, f32[4,2,8,512]{3,2,1,0:T(8,128)S(1)}, u32[]{:S(2)}, u32[]{:S(2)}) collective-permute-start(f32[4,2,8,512]{3,2,1,0:T(8,128)S(1)} %get-tuple-element.66), channel_id=1, source_target_pairs={{0,16},{1,17},{2,18},{3,19},{4,20},{5,21},{6,22},{7,23},{8,24},{9,... | collective-permute-start | bytes 393224 | tf_op jit(solution)/shard_map/ppermute | solution.py:330
  47.0 5.9 %collective-permute-start.16 = (f32[4,2,8,512]{3,2,1,0:T(8,128)S(1)}, f32[4,2,8,512]{3,2,1,0:T(8,128)S(1)}, u32[]{:S(2)}, u32[]{:S(2)}) collective-permute-start(f32[4,2,8,512]{3,2,1,0:T(8,128)S(1)} %get-tuple-element.67), channel_id=1, source_target_pairs={{0,17},{1,16},{2,19},{3,18},{4,21},{5,20},{6,23},{7,22},{8,25},{9,... | collective-permute-start | bytes 393224 | tf_op jit(solution)/shard_map/ppermute | solution.py:330
  52.9 2.0 %collective-permute-start.17 = (f32[4,2,8,512]{3,2,1,0:T(8,128)S(1)}, f32[4,2,8,512]{3,2,1,0:T(8,128)S(1)}, u32[]{:S(2)}, u32[]{:S(2)}) collective-permute-start(f32[4,2,8,512]{3,2,1,0:T(8,128)S(1)} %get-tuple-element.69.refs_0_), channel_id=1, source_target_pairs={{0,8},{1,9},{2,10},{3,11},{4,12},{5,13},{6,14},{7,15},{8,0},{9,1},... | collective-permute-start | bytes 393224 | tf_op jit(solution)/shard_map/ppermute | solution.py:330
  52.9 2.0 %collective-permute-start.18 = (f32[4,2,8,512]{3,2,1,0:T(8,128)S(1)}, f32[4,2,8,512]{3,2,1,0:T(8,128)S(1)}, u32[]{:S(2)}, u32[]{:S(2)}) collective-permute-start(f32[4,2,8,512]{3,2,1,0:T(8,128)S(1)} %get-tuple-element.70.refs_1_), channel_id=1, source_target_pairs={{0,8},{1,9},{2,10},{3,11},{4,12},{5,13},{6,14},{7,15},{8,0},{9,1},... | collective-permute-start | bytes 393224 | tf_op jit(solution)/shard_map/ppermute | solution.py:330
  53.4 1.5 %collective-permute-start.19 = (f32[4,2,8,512]{3,2,1,0:T(8,128)S(1)}, f32[4,2,8,512]{3,2,1,0:T(8,128)S(1)}, u32[]{:S(2)}, u32[]{:S(2)}) collective-permute-start(f32[4,2,8,512]{3,2,1,0:T(8,128)S(1)} %get-tuple-element.71.refs_2_), channel_id=1, source_target_pairs={{0,8},{1,9},{2,10},{3,11},{4,12},{5,13},{6,14},{7,15},{8,0},{9,1},... | collective-permute-start | bytes 393224 | tf_op jit(solution)/shard_map/ppermute | solution.py:330
  53.4 1.5 %collective-permute-start.20 = (f32[4,2,8,512]{3,2,1,0:T(8,128)S(1)}, f32[4,2,8,512]{3,2,1,0:T(8,128)S(1)}, u32[]{:S(2)}, u32[]{:S(2)}) collective-permute-start(f32[4,2,8,512]{3,2,1,0:T(8,128)S(1)} %get-tuple-element.72.refs_3_), channel_id=1, source_target_pairs={{0,8},{1,9},{2,10},{3,11},{4,12},{5,13},{6,14},{7,15},{8,0},{9,1},... | collective-permute-start | bytes 393224 | tf_op jit(solution)/shard_map/ppermute | solution.py:330
  53.9 16.6 %collective-permute-start.10 = (f32[4,3,16,512]{3,2,1,0:T(8,128)S(1)}, f32[4,3,16,512]{3,2,1,0:T(8,128)S(1)}, u32[]{:S(2)}, u32[]{:S(2)}) collective-permute-start(f32[4,3,16,512]{3,2,1,0:T(8,128)S(1)} %get-tuple-element.51), channel_id=1, source_target_pairs={{0,16},{1,17},{2,18},{3,19},{4,20},{5,21},{6,22},{7,23},{8,24},{9,... | collective-permute-start | bytes 1179656 | tf_op jit(solution)/shard_map/ppermute | solution.py:330
  56.3 14.2 %collective-permute-start.21 = (f32[4,2,16,512]{3,2,1,0:T(8,128)S(1)}, f32[4,2,16,512]{3,2,1,0:T(8,128)S(1)}, u32[]{:S(2)}, u32[]{:S(2)}) collective-permute-start(f32[4,2,16,512]{3,2,1,0:T(8,128)S(1)} %get-tuple-element.74), channel_id=1, source_target_pairs={{0,16},{1,17},{2,18},{3,19},{4,20},{5,21},{6,22},{7,23},{8,24},{9,... | collective-permute-start | bytes 786440 | tf_op jit(solution)/shard_map/ppermute | solution.py:330
  (1 other events, 1.3 us)

commit v3 on v2

--- a/solution.py
+++ b/solution.py
@@ -18,15 +18,14 @@
 
 
 def cost(flops, arrays):
-    size = sum(a.size * a.dtype.itemsize for a in arrays)
-    return pl.CostEstimate(flops=int(flops), bytes_accessed=int(size), transcendentals=0)
+    return pl.CostEstimate(flops=1, bytes_accessed=1, transcendentals=0)
 
 
 def sds(*shape, dtype=F32):
     return jax.ShapeDtypeStruct(shape, dtype)
 
 
-def prep_kernel(chunk, x_ref, keep_ref, send_ref, edge_ref, buf, sem):
+def prep_kernel(chunk, x_ref, keep_ref, send_ref, near_ref, far_ref, buf, sem):
     rows, _, half, _ = keep_ref.shape
     odd = lax.rem(lax.axis_index("tile"), 2)
     copies = [pltpu.make_async_copy(x_ref.at[:, f], buf.at[n], sem.at[n]) for n, f in enumerate(chunk)]
@@ -41,7 +40,8 @@
             keep_ref[turned, n] = kept[r]
             send_ref[rows - 1 - turned, n] = sent[r]
     for r in range(HALO):
-        edge_ref[r] = keep_ref[r]
+        near_ref[r] = keep_ref[r]
+        far_ref[r] = send_ref[rows - HALO + r]
 
 
 def prep(fields, chunk):
@@ -49,9 +49,9 @@
     shape = sds(rows, len(chunk), depth // 2, ny)
     return pl.pallas_call(
         functools.partial(prep_kernel, chunk),
-        out_shape=[shape, shape, sds(HALO, *shape.shape[1:])],
+        out_shape=[shape, shape] + [sds(HALO, *shape.shape[1:])] * 2,
         in_specs=[pl.BlockSpec(memory_space=pltpu.HBM)],
-        out_specs=[VMEM] * 3,
+        out_specs=[VMEM] * 4,
         scratch_shapes=[
             pltpu.VMEM((len(chunk), depth, rows, ny), F32),
             pltpu.SemaphoreType.DMA((len(chunk),)),
@@ -94,39 +94,21 @@
     )(column_ops)
 
 
-def edge_kernel(recv_ref, *refs):
-    out = refs[-1]
-    for r in range(HALO):
-        out[r] = recv_ref[recv_ref.shape[0] - HALO + r]
-
-
-def edge(recv, *earlier):
-    shape = sds(HALO, *recv.shape[1:])
-    return pl.pallas_call(
-        edge_kernel,
-        out_shape=shape,
-        in_specs=[VMEM] + [pl.BlockSpec(memory_space=pl.ANY)] * len(earlier),
-        out_specs=VMEM,
-        compiler_params=PARAMS,
-        cost_estimate=cost(0, [shape] * 2),
-    )(recv, *earlier)
-
-
 def later_kernel(*refs):
     pass
 
 
-def later(arrays, other):
+def later(arrays, *others):
     count = len(arrays)
     return list(
         pl.pallas_call(
             later_kernel,
             out_shape=[sds(*array.shape) for array in arrays],
-            in_specs=[VMEM] * count + [pl.BlockSpec(memory_space=pl.ANY)],
+            in_specs=[VMEM] * count + [pl.BlockSpec(memory_space=pl.ANY)] * len(others),
             out_specs=[VMEM] * count,
             input_output_aliases={n: n for n in range(count)},
             compiler_params=PARAMS,
-        )(*arrays, other)
+        )(*arrays, *others)
     )
 
 
@@ -240,9 +222,8 @@
 
 
 def mix_kernel(chips, chunk, use_ref, ops_ref, *refs):
-    blocks, outs = refs[: 4 * chips], refs[4 * chips : 5 * chips]
-    token, data, result = refs[5 * chips :]
-    token[...] = jnp.zeros_like(token)
+    blocks, outs = refs[: 4 * chips], refs[4 * chips + 1 : 5 * chips + 1]
+    data, result = refs[5 * chips + 1 :]
     own, _, half, ny = blocks[0].shape
     levels, per = data.shape[0], 2 * half
     kept = chips * per
@@ -282,21 +263,21 @@
                 outs[a][q, n] = result[pl.ds(at, per), q * ny : (q + 1) * ny]
 
 
-def mix(chunk, use, ops, blocks, chips):
+def mix(chunk, use, ops, blocks, earlier, chips):
     own, fields, half, ny = blocks[0].shape
     levels = ops.shape[2] // 3
     return pl.pallas_call(
         functools.partial(mix_kernel, chips, chunk),
-        out_shape=[sds(own, fields, 2 * half, ny)] * chips + [sds(8, 128)],
-        in_specs=[VMEM] * (2 + len(blocks)),
-        out_specs=[VMEM] * (chips + 1),
+        out_shape=[sds(own, fields, 2 * half, ny)] * chips,
+        in_specs=[VMEM] * (2 + len(blocks)) + [pl.BlockSpec(memory_space=pl.ANY)],
+        out_specs=[VMEM] * chips,
         scratch_shapes=[
             pltpu.VMEM((levels, own * ny), F32),
             pltpu.VMEM((levels // 2, own * ny), F32),
         ],
         compiler_params=PARAMS,
         cost_estimate=cost(2 * fields * ops.shape[1] * ops.shape[2] * own * ny, blocks),
-    )(use, ops, *blocks)
+    )(use, ops, *blocks, earlier)
 
 
 def final_kernel(chips, chunks, *refs):
@@ -332,8 +313,8 @@
     def outward(lev, tile):
         return lev, (tile + (2 if tile % 2 else -2)) % tile_count
 
-    def inward(lev, tile):
-        return lev, (tile + (-2 if tile % 2 else 2)) % tile_count
+    def across(lev, tile):
+        return lev, (tile + (1 if tile % 2 else -1)) % tile_count
 
     def other(lev, tile):
         return lev, tile ^ 1
@@ -351,29 +332,28 @@
     def both_cores(blocks):
         return blocks + [send(block, lambda lev, tile: (lev ^ 1, tile)) for block in blocks]
 
-    def mixed_back(chunk, blocks):
-        mixed = mix(chunk, land_use, ops, blocks, chips)
-        back = [send(mixed[a], lambda lev, tile: (lev ^ 2 * a, tile)) if a else mixed[0] for a in range(chips)]
-        return back, mixed[-1]
+    def mixed_back(chunk, blocks, earlier):
+        mixed = mix(chunk, land_use, ops, blocks, earlier, chips)
+        return [send(mixed[a], lambda lev, tile: (lev ^ 2 * a, tile)) if a else mixed[0] for a in range(chips)]
 
     first, second = CHUNKS
-    keep_a, away_a, edge_a = prep(fields, first)
+    keep_a, away_a, near_a, far_a = prep(fields, first)
     recv_a = send(away_a, other)
-    after_a = send(edge_a, outward)
-    keep_b, away_b, edge_b = prep(fields, second)
-    recv_a, away_b, edge_b = lax.optimization_barrier((recv_a, away_b, edge_b))
-    before_a = send(edge(recv_a), inward)
+    before_a = send(far_a, across)
+    after_a = send(near_a, outward)
+    keep_b, away_b, near_b, far_b = prep(fields, second)
+    before_a, away_b, near_b, far_b = lax.optimization_barrier((before_a, away_b, near_b, far_b))
     recv_b = send(away_b, other)
-    after_b = send(edge_b, outward)
+    before_b = send(far_b, across)
+    after_b = send(near_b, outward)
     outs_a = advect((before_a, keep_a, recv_a, after_a), None, chips)
     faces, outs_a = outs_a[:9], outs_a[9:]
     blocks_a = outspread(outs_a)
-    before_b = send(edge(recv_b, before_a), inward)
     outs_b = advect((before_b, keep_b, recv_b, after_b), faces, chips)
     blocks_b = outspread(outs_b)
-    returned, mixed = mixed_back(first, both_cores(blocks_a))
-    blocks_b = later(blocks_b, mixed)
-    returned += mixed_back(second, both_cores(blocks_b))[0]
+    blocks_a = later(blocks_a, *blocks_b[1:])
+    returned = mixed_back(first, both_cores(blocks_a), outs_b[0])
+    returned += mixed_back(second, both_cores(blocks_b), returned[0])
 
     return pl.pallas_call(
         functools.partial(final_kernel, chips, CHUNKS),

time: 72.1 us -> 67.7 us (0.939)
  waiting for transfers between devices: 35.2 us -> 30.5 us
  starting transfers between devices: 22.7 us -> 23.6 us
    ppermute x22, waiting for transfers between devices: 35.2 us -> 30.5 us  [send(): return lax.ppermute(array, ('lev', 'tile'), pairs)]
    ppermute x22, starting transfers between devices: 22.7 us -> 23.6 us  [send(): return lax.ppermute(array, ('lev', 'tile'), pairs)]
  transfers between devices with their start and end apart: 22 -> 22, of which waited for: 10 -> 6; matrix products, arithmetic and copies ran while one was open for 0% -> 0% of each run, Pallas kernels for 15% -> 15%
where the time goes in v3:
time: 67.7 us; the launch traced here: 67.6 us
  waiting for transfers between devices  30.5 us (45%)
  starting transfers between devices  23.6 us (35%)
  Pallas kernels  11.9 us (18%)
  local copies, waits for them, and re-layouts  1.33 us (2%)
    ppermute x22, waiting for transfers between devices, send(): return lax.ppermute(array, ('lev', 'tile'), pairs)  30.5 us
    ppermute x22, starting transfers between devices, send(): return lax.ppermute(array, ('lev', 'tile'), pairs)  23.6 us
    pallas_call x2, Pallas kernels, advect(): pl.pallas_call(functools.partial(advect_kernel, chips, faces is None), ou...  7.7 us
    pallas_call x2, Pallas kernels, mix(): pl.pallas_call(functools.partial(mix_kernel, chips, chunk), out_shape=[sd...  1.93 us
    pallas_call x1, Pallas kernels, per_device(): pl.pallas_call(functools.partial(final_kernel, chips, CHUNKS), out_shape=...  1.42 us
  transfers between devices with their start and end apart: 22, of which 6 were waited for; matrix products, arithmetic and copies ran while one was open for 0% of the time, Pallas kernels for 15%

profile of v3, /device:TPU:0, one launch (start us, length us, event | category | flops | bytes accessed | tf_op | source)
XLA Modules:
  0.0 67.6 jit_solution(16872629041239817934)
XLA Ops:
  0.0 1.3 %copy-done = f32[16,5,8,512]{3,2,1,0:T(8,128)S(1)} copy-done((f32[16,5,8,512]{3,2,1,0:T(8,128)S(1)}, f32[16,5,8,512]{3,2,1,0:T(8,128)}, u32[]{:S(2)}) %copy-start) | copy-done | bytes 1310744
  1.6 3.0 %collective-permute-start.1 = (f32[8,3,8,512]{3,2,1,0:T(8,128)S(1)}, f32[8,3,8,512]{3,2,1,0:T(8,128)S(1)}, u32[]{:S(2)}, u32[]{:S(2)}) collective-permute-start(f32[8,3,8,512]{3,2,1,0:T(8,128)S(1)} %get-tuple-element.48), channel_id=1, source_target_pairs={{0,1},{1,0},{2,3},{3,2},{4,5},{5,4},{6,7},{7,6},{8,9},{9,8},{10,11... | collective-permute-start | bytes 1179656 | tf_op jit(solution)/shard_map/ppermute | solution.py:311
  4.6 3.6 %collective-permute-start = (f32[6,3,8,512]{3,2,1,0:T(8,128)S(1)}, f32[6,3,8,512]{3,2,1,0:T(8,128)S(1)}, u32[]{:S(2)}, u32[]{:S(2)}) collective-permute-start(f32[6,3,8,512]{3,2,1,0:T(8,128)S(1)} %get-tuple-element.42), channel_id=1, source_target_pairs={{0,7},{1,2},{2,1},{3,4},{4,3},{5,6},{6,5},{7,0},{8,15},{9,10},{10,... | collective-permute-start | bytes 884744 | tf_op jit(solution)/shard_map/ppermute | solution.py:311
  8.2 0.4 collective-permute-start.2
  8.8 8.4 %collective-permute-done.before = f32[6,3,8,512]{3,2,1,0:T(8,128)S(1)} collective-permute-done((f32[6,3,8,512]{3,2,1,0:T(8,128)S(1)}, f32[6,3,8,512]{3,2,1,0:T(8,128)S(1)}, u32[]{:S(2)}, u32[]{:S(2)}) %collective-permute-start) | collective-permute-done | bytes 294944 | tf_op jit(solution)/shard_map/ppermute | solution.py:311
  17.3 3.6 %collective-permute-start.6 = (f32[6,2,8,512]{3,2,1,0:T(8,128)S(1)}, f32[6,2,8,512]{3,2,1,0:T(8,128)S(1)}, u32[]{:S(2)}, u32[]{:S(2)}) collective-permute-start(f32[6,2,8,512]{3,2,1,0:T(8,128)S(1)} %get-tuple-element.54), channel_id=1, source_target_pairs={{0,7},{1,2},{2,1},{3,4},{4,3},{5,6},{6,5},{7,0},{8,15},{9,10},{10,... | collective-permute-start | bytes 589832 | tf_op jit(solution)/shard_map/ppermute | solution.py:311
  20.9 0.6 collective-permute-start.8
  21.4 0.5 collective-permute-done.2.after
  22.0 1.3 %collective-permute-done.1.recv = f32[8,3,8,512]{3,2,1,0:T(8,128)S(1)} collective-permute-done((f32[8,3,8,512]{3,2,1,0:T(8,128)S(1)}, f32[8,3,8,512]{3,2,1,0:T(8,128)S(1)}, u32[]{:S(2)}, u32[]{:S(2)}) %collective-permute-start.1) | collective-permute-done | bytes 393248 | tf_op jit(solution)/shard_map/ppermute | solution.py:311
  23.2 4.4 %shard_map.40 = (f32[25,8,512]{2,1,0:T(8,128)S(1)}, f32[24,8,512]{2,1,0:T(8,128)S(1)}, f32[24,8,512]{2,1,0:T(8,128)S(1)}, f32[21,8,512]{2,1,0:T(8,128)S(1)}, f32...) custom-call(f32[6,3,8,512]{3,2,1,0:T(8,128)S(1)} %collective-permute, ...), custom_call_target="tpu_custom_call" | custom-call | flops 1 | bytes 1 | tf_op jit(solution)/shard_map/pallas_call | solution.py:213
  27.7 3.0 %collective-permute-start.3 = (f32[4,3,8,512]{3,2,1,0:T(8,128)S(1)}, f32[4,3,8,512]{3,2,1,0:T(8,128)S(1)}, u32[]{:S(2)}, u32[]{:S(2)}) collective-permute-start(f32[4,3,8,512]{3,2,1,0:T(8,128)S(1)} %get-tuple-element.51), channel_id=1, source_target_pairs={{0,1},{1,0},{2,3},{3,2},{4,5},{5,4},{6,7},{7,6},{8,9},{9,8},{10,11... | collective-permute-start | bytes 589832 | tf_op jit(solution)/shard_map/ppermute | solution.py:311
  30.7 1.6 %collective-permute-start.4 = (f32[4,3,8,512]{3,2,1,0:T(8,128)S(1)}, f32[4,3,8,512]{3,2,1,0:T(8,128)S(1)}, u32[]{:S(2)}, u32[]{:S(2)}) collective-permute-start(f32[4,3,8,512]{3,2,1,0:T(8,128)S(1)} %get-tuple-element.52), channel_id=1, source_target_pairs={{0,16},{1,17},{2,18},{3,19},{4,20},{5,21},{6,22},{7,23},{8,24},{9,... | collective-permute-start | bytes 589832 | tf_op jit(solution)/shard_map/ppermute | solution.py:311
  32.3 3.3 %shard_map.41 = (f32[4,2,8,512]{3,2,1,0:T(8,128)S(1)}, f32[4,2,8,512]{3,2,1,0:T(8,128)S(1)}, f32[4,2,8,512]{3,2,1,0:T(8,128)S(1)}, f32[4,2,8,512]{3,2,1,0:T(8,128)S(1)}) custom-call(f32[6,2,8,512]{3,2,1,0:T(8,128)S(1)} %collective-permute-done.6.before, f32[8,2,8,512]{3,2,1,0:T(8,128)S(1)} %get-tuple-element.55.keep, ...), custom_call_target="tpu_custom_call" | custom-call | flops 1 | bytes 1 | tf_op jit(solution)/shard_map/pallas_call | solution.py:213
  35.6 1.6 %collective-permute-start.10 = (f32[4,2,8,512]{3,2,1,0:T(8,128)S(1)}, f32[4,2,8,512]{3,2,1,0:T(8,128)S(1)}, u32[]{:S(2)}, u32[]{:S(2)}) collective-permute-start(f32[4,2,8,512]{3,2,1,0:T(8,128)S(1)} %get-tuple-element.68), channel_id=1, source_target_pairs={{0,16},{1,17},{2,18},{3,19},{4,20},{5,21},{6,22},{7,23},{8,24},{9,... | collective-permute-start | bytes 393224 | tf_op jit(solution)/shard_map/ppermute | solution.py:311
  37.2 1.8 %collective-permute-start.11 = (f32[4,2,8,512]{3,2,1,0:T(8,128)S(1)}, f32[4,2,8,512]{3,2,1,0:T(8,128)S(1)}, u32[]{:S(2)}, u32[]{:S(2)}) collective-permute-start(f32[4,2,8,512]{3,2,1,0:T(8,128)S(1)} %get-tuple-element.69), channel_id=1, source_target_pairs={{0,17},{1,16},{2,19},{3,18},{4,21},{5,20},{6,23},{7,22},{8,25},{9,... | collective-permute-start | bytes 393224 | tf_op jit(solution)/shard_map/ppermute | solution.py:311
  39.1 5.1 %collective-permute-done.4.refs_2_ = f32[4,3,8,512]{3,2,1,0:T(8,128)S(1)} collective-permute-done((f32[4,3,8,512]{3,2,1,0:T(8,128)S(1)}, f32[4,3,8,512]{3,2,1,0:T(8,128)S(1)}, u32[]{:S(2)}, u32[]{:S(2)}) %collective-permute-start.4) | collective-permute-done | bytes 196640 | tf_op jit(solution)/shard_map/ppermute | solution.py:311
  44.2 1.4 %collective-permute-done.10.refs_5_.refs_2_ = f32[4,2,8,512]{3,2,1,0:T(8,128)S(1)} collective-permute-done((f32[4,2,8,512]{3,2,1,0:T(8,128)S(1)}, f32[4,2,8,512]{3,2,1,0:T(8,128)S(1)}, u32[]{:S(2)}, u32[]{:S(2)}) %collective-permute-start.10) | collective-permute-done | bytes 131104 | tf_op jit(solution)/shard_map/ppermute | solution.py:311
  45.7 0.5 collective-permute-start.13
  48.2 1.1 %shard_map.43 = (f32[4,3,16,512]{3,2,1,0:T(8,128)S(1)}, f32[4,3,16,512]{3,2,1,0:T(8,128)S(1)}) custom-call(s32[8,512]{1,0:T(8,128)S(1)} %copy-done.2, bf16[5,256,192]{2,1,0:T(8,128)(2,1)S(1)} %shard_map.37.ops_ref, f32[4,3,8,512]{3,2,1,0:T(8,128)S(1)} %get-tuple-element.70.refs_0_, f32[4,3,8,512]{3,2,1,0:T(8,128)S(1)} %get-tuple-element.71.refs_1_, ...), custom_call_target="tpu_custom_call" | custom-call | flops 1 | bytes 1 | tf_op jit(solution)/shard_map/pallas_call | solution.py:269
  49.4 0.9 %collective-permute-start.16 = (f32[4,3,16,512]{3,2,1,0:T(8,128)S(1)}, f32[4,3,16,512]{3,2,1,0:T(8,128)S(1)}, u32[]{:S(2)}, u32[]{:S(2)}) collective-permute-start(f32[4,3,16,512]{3,2,1,0:T(8,128)S(1)} %get-tuple-element.76), channel_id=1, source_target_pairs={{0,16},{1,17},{2,18},{3,19},{4,20},{5,21},{6,22},{7,23},{8,24},{9,... | collective-permute-start | bytes 1179656 | tf_op jit(solution)/shard_map/ppermute | solution.py:311
  50.2 0.8 %shard_map.44 = (f32[4,2,16,512]{3,2,1,0:T(8,128)S(1)}, f32[4,2,16,512]{3,2,1,0:T(8,128)S(1)}) custom-call(s32[8,512]{1,0:T(8,128)S(1)} %copy-done.2, bf16[5,256,192]{2,1,0:T(8,128)(2,1)S(1)} %shard_map.37.ops_ref, f32[4,2,8,512]{3,2,1,0:T(8,128)S(1)} %get-tuple-element.74.refs_8_.refs_0_, f32[4,2,8,512]{3,2,1,0:T(8,128)S(1)} %collective-permute-done.9.refs_4_.refs_1_, ...), custom_call_target="tpu_custom_call" | custom-call | flops 1 | bytes 1 | tf_op jit(solution)/shard_map/pallas_call | solution.py:269
  51.1 1.3 %collective-permute-start.21 = (f32[4,2,16,512]{3,2,1,0:T(8,128)S(1)}, f32[4,2,16,512]{3,2,1,0:T(8,128)S(1)}, u32[]{:S(2)}, u32[]{:S(2)}) collective-permute-start(f32[4,2,16,512]{3,2,1,0:T(8,128)S(1)} %get-tuple-element.78), channel_id=1, source_target_pairs={{0,16},{1,17},{2,18},{3,19},{4,20},{5,21},{6,22},{7,23},{8,24},{9,... | collective-permute-start | bytes 786440 | tf_op jit(solution)/shard_map/ppermute | solution.py:311
  52.4 13.8 %collective-permute-done.21.refs_3_ = f32[4,2,16,512]{3,2,1,0:T(8,128)S(1)} collective-permute-done((f32[4,2,16,512]{3,2,1,0:T(8,128)S(1)}, f32[4,2,16,512]{3,2,1,0:T(8,128)S(1)}, u32[]{:S(2)}, u32[]{:S(2)}) %collective-permute-start.21) | collective-permute-done | bytes 262176 | tf_op jit(solution)/shard_map/ppermute | solution.py:311
  66.1 1.4 %shard_map.45 = f32[16,5,8,512]{3,2,1,0:T(8,128)} custom-call(f32[4,3,16,512]{3,2,1,0:T(8,128)S(1)} %get-tuple-element.75.refs_8_.refs_0_, f32[4,3,16,512]{3,2,1,0:T(8,128)S(1)} %collective-permute-done.16.refs_1_, f32[4,2,16,512]{3,2,1,0:T(8,128)S(1)} %get-tuple-element.77.refs_2_, f32[4,2,16,512]{3,2,1,0:T(8,128)S(1)} %collective-permute-done.21.refs_3_), custom_call_target="tpu_custom_call" | custom-call | flops 1 | bytes 1 | tf_op jit(solution)/shard_map/pallas_call | solution.py:358
  (35 shorter events, 2.7 us)
Async XLA Ops:
  1.6 21.6 %collective-permute-start.1 = (f32[8,3,8,512]{3,2,1,0:T(8,128)S(1)}, f32[8,3,8,512]{3,2,1,0:T(8,128)S(1)}, u32[]{:S(2)}, u32[]{:S(2)}) collective-permute-start(f32[8,3,8,512]{3,2,1,0:T(8,128)S(1)} %get-tuple-element.48), channel_id=1, source_target_pairs={{0,1},{1,0},{2,3},{3,2},{4,5},{5,4},{6,7},{7,6},{8,9},{9,8},{10,11... | collective-permute-start | bytes 1179656 | tf_op jit(solution)/shard_map/ppermute | solution.py:311
  4.6 12.7 %collective-permute-start = (f32[6,3,8,512]{3,2,1,0:T(8,128)S(1)}, f32[6,3,8,512]{3,2,1,0:T(8,128)S(1)}, u32[]{:S(2)}, u32[]{:S(2)}) collective-permute-start(f32[6,3,8,512]{3,2,1,0:T(8,128)S(1)} %get-tuple-element.42), channel_id=1, source_target_pairs={{0,7},{1,2},{2,1},{3,4},{4,3},{5,6},{6,5},{7,0},{8,15},{9,10},{10,... | collective-permute-start | bytes 884744 | tf_op jit(solution)/shard_map/ppermute | solution.py:311
  8.2 13.8 %collective-permute-start.2 = (f32[6,3,8,512]{3,2,1,0:T(8,128)S(1)}, f32[6,3,8,512]{3,2,1,0:T(8,128)S(1)}, u32[]{:S(2)}, u32[]{:S(2)}) collective-permute-start(f32[6,3,8,512]{3,2,1,0:T(8,128)S(1)} %get-tuple-element.49), channel_id=1, source_target_pairs={{0,6},{1,3},{2,0},{3,5},{4,2},{5,7},{6,4},{7,1},{8,14},{9,11},{10,... | collective-permute-start | bytes 884744 | tf_op jit(solution)/shard_map/ppermute | solution.py:311
  17.3 15.0 %collective-permute-start.7 = (f32[8,2,8,512]{3,2,1,0:T(8,128)S(1)}, f32[8,2,8,512]{3,2,1,0:T(8,128)S(1)}, u32[]{:S(2)}, u32[]{:S(2)}) collective-permute-start(f32[8,2,8,512]{3,2,1,0:T(8,128)S(1)} %get-tuple-element.56), channel_id=1, source_target_pairs={{0,1},{1,0},{2,3},{3,2},{4,5},{5,4},{6,7},{7,6},{8,9},{9,8},{10,11... | collective-permute-start | bytes 786440 | tf_op jit(solution)/shard_map/ppermute | solution.py:311
  17.3 15.0 %collective-permute-start.6 = (f32[6,2,8,512]{3,2,1,0:T(8,128)S(1)}, f32[6,2,8,512]{3,2,1,0:T(8,128)S(1)}, u32[]{:S(2)}, u32[]{:S(2)}) collective-permute-start(f32[6,2,8,512]{3,2,1,0:T(8,128)S(1)} %get-tuple-element.54), channel_id=1, source_target_pairs={{0,7},{1,2},{2,1},{3,4},{4,3},{5,6},{6,5},{7,0},{8,15},{9,10},{10,... | collective-permute-start | bytes 589832 | tf_op jit(solution)/shard_map/ppermute | solution.py:311
  20.9 11.4 %collective-permute-start.8 = (f32[6,2,8,512]{3,2,1,0:T(8,128)S(1)}, f32[6,2,8,512]{3,2,1,0:T(8,128)S(1)}, u32[]{:S(2)}, u32[]{:S(2)}) collective-permute-start(f32[6,2,8,512]{3,2,1,0:T(8,128)S(1)} %get-tuple-element.57), channel_id=1, source_target_pairs={{0,6},{1,3},{2,0},{3,5},{4,2},{5,7},{6,4},{7,1},{8,14},{9,11},{10,... | collective-permute-start | bytes 589832 | tf_op jit(solution)/shard_map/ppermute | solution.py:311
  27.7 11.3 %collective-permute-start.3 = (f32[4,3,8,512]{3,2,1,0:T(8,128)S(1)}, f32[4,3,8,512]{3,2,1,0:T(8,128)S(1)}, u32[]{:S(2)}, u32[]{:S(2)}) collective-permute-start(f32[4,3,8,512]{3,2,1,0:T(8,128)S(1)} %get-tuple-element.51), channel_id=1, source_target_pairs={{0,1},{1,0},{2,3},{3,2},{4,5},{5,4},{6,7},{7,6},{8,9},{9,8},{10,11... | collective-permute-start | bytes 589832 | tf_op jit(solution)/shard_map/ppermute | solution.py:311
  30.7 13.5 %collective-permute-start.4 = (f32[4,3,8,512]{3,2,1,0:T(8,128)S(1)}, f32[4,3,8,512]{3,2,1,0:T(8,128)S(1)}, u32[]{:S(2)}, u32[]{:S(2)}) collective-permute-start(f32[4,3,8,512]{3,2,1,0:T(8,128)S(1)} %get-tuple-element.52), channel_id=1, source_target_pairs={{0,16},{1,17},{2,18},{3,19},{4,20},{5,21},{6,22},{7,23},{8,24},{9,... | collective-permute-start | bytes 589832 | tf_op jit(solution)/shard_map/ppermute | solution.py:311
  32.3 11.9 %collective-permute-start.5 = (f32[4,3,8,512]{3,2,1,0:T(8,128)S(1)}, f32[4,3,8,512]{3,2,1,0:T(8,128)S(1)}, u32[]{:S(2)}, u32[]{:S(2)}) collective-permute-start(f32[4,3,8,512]{3,2,1,0:T(8,128)S(1)} %get-tuple-element.53), channel_id=1, source_target_pairs={{0,17},{1,16},{2,19},{3,18},{4,21},{5,20},{6,23},{7,22},{8,25},{9,... | collective-permute-start | bytes 589832 | tf_op jit(solution)/shard_map/ppermute | solution.py:311
  32.3 14.4 %copy-start.1 = (f32[5,8,64,64]{3,2,1,0:T(8,128)S(1)}, f32[5,8,64,64]{3,2,1,0:T(8,128)}, u32[]{:S(2)}) copy-start(f32[5,8,64,64]{3,2,1,0:T(8,128)} %ops_ref.1) | copy-start | bytes 1966084
  35.6 10.0 %collective-permute-start.10 = (f32[4,2,8,512]{3,2,1,0:T(8,128)S(1)}, f32[4,2,8,512]{3,2,1,0:T(8,128)S(1)}, u32[]{:S(2)}, u32[]{:S(2)}) collective-permute-start(f32[4,2,8,512]{3,2,1,0:T(8,128)S(1)} %get-tuple-element.68), channel_id=1, source_target_pairs={{0,16},{1,17},{2,18},{3,19},{4,20},{5,21},{6,22},{7,23},{8,24},{9,... | collective-permute-start | bytes 393224 | tf_op jit(solution)/shard_map/ppermute | solution.py:311
  37.2 8.4 %collective-permute-start.11 = (f32[4,2,8,512]{3,2,1,0:T(8,128)S(1)}, f32[4,2,8,512]{3,2,1,0:T(8,128)S(1)}, u32[]{:S(2)}, u32[]{:S(2)}) collective-permute-start(f32[4,2,8,512]{3,2,1,0:T(8,128)S(1)} %get-tuple-element.69), channel_id=1, source_target_pairs={{0,17},{1,16},{2,19},{3,18},{4,21},{5,20},{6,23},{7,22},{8,25},{9,... | collective-permute-start | bytes 393224 | tf_op jit(solution)/shard_map/ppermute | solution.py:311
  39.0 6.6 %collective-permute-start.9 = (f32[4,2,8,512]{3,2,1,0:T(8,128)S(1)}, f32[4,2,8,512]{3,2,1,0:T(8,128)S(1)}, u32[]{:S(2)}, u32[]{:S(2)}) collective-permute-start(f32[4,2,8,512]{3,2,1,0:T(8,128)S(1)} %get-tuple-element.67), channel_id=1, source_target_pairs={{0,1},{1,0},{2,3},{3,2},{4,5},{5,4},{6,7},{7,6},{8,9},{9,8},{10,11... | collective-permute-start | bytes 393224 | tf_op jit(solution)/shard_map/ppermute | solution.py:311
  45.6 2.6 %copy-start.2 = (s32[8,512]{1,0:T(8,128)S(1)}, s32[8,512]{1,0:T(8,128)}, u32[]{:S(2)}) copy-start(s32[8,512]{1,0:T(8,128)} %use_ref.3) | copy-start | bytes 49156
  45.6 1.6 %collective-permute-start.12 = (f32[4,3,8,512]{3,2,1,0:T(8,128)S(1)}, f32[4,3,8,512]{3,2,1,0:T(8,128)S(1)}, u32[]{:S(2)}, u32[]{:S(2)}) collective-permute-start(f32[4,3,8,512]{3,2,1,0:T(8,128)S(1)} %get-tuple-element.70.refs_0_), channel_id=1, source_target_pairs={{0,8},{1,9},{2,10},{3,11},{4,12},{5,13},{6,14},{7,15},{8,0},{9,1},... | collective-permute-start | bytes 589832 | tf_op jit(solution)/shard_map/ppermute | solution.py:311
  45.7 2.0 %collective-permute-start.13 = (f32[4,3,8,512]{3,2,1,0:T(8,128)S(1)}, f32[4,3,8,512]{3,2,1,0:T(8,128)S(1)}, u32[]{:S(2)}, u32[]{:S(2)}) collective-permute-start(f32[4,3,8,512]{3,2,1,0:T(8,128)S(1)} %get-tuple-element.71.refs_1_), channel_id=1, source_target_pairs={{0,8},{1,9},{2,10},{3,11},{4,12},{5,13},{6,14},{7,15},{8,0},{9,1},... | collective-permute-start | bytes 589832 | tf_op jit(solution)/shard_map/ppermute | solution.py:311
  46.2 1.6 %collective-permute-start.14 = (f32[4,3,8,512]{3,2,1,0:T(8,128)S(1)}, f32[4,3,8,512]{3,2,1,0:T(8,128)S(1)}, u32[]{:S(2)}, u32[]{:S(2)}) collective-permute-start(f32[4,3,8,512]{3,2,1,0:T(8,128)S(1)} %get-tuple-element.72.refs_2_), channel_id=1, source_target_pairs={{0,8},{1,9},{2,10},{3,11},{4,12},{5,13},{6,14},{7,15},{8,0},{9,1},... | collective-permute-start | bytes 589832 | tf_op jit(solution)/shard_map/ppermute | solution.py:311
  46.3 1.9 %collective-permute-start.15 = (f32[4,3,8,512]{3,2,1,0:T(8,128)S(1)}, f32[4,3,8,512]{3,2,1,0:T(8,128)S(1)}, u32[]{:S(2)}, u32[]{:S(2)}) collective-permute-start(f32[4,3,8,512]{3,2,1,0:T(8,128)S(1)} %get-tuple-element.73.refs_3_), channel_id=1, source_target_pairs={{0,8},{1,9},{2,10},{3,11},{4,12},{5,13},{6,14},{7,15},{8,0},{9,1},... | collective-permute-start | bytes 589832 | tf_op jit(solution)/shard_map/ppermute | solution.py:311
  47.1 3.1 %collective-permute-start.17 = (f32[4,2,8,512]{3,2,1,0:T(8,128)S(1)}, f32[4,2,8,512]{3,2,1,0:T(8,128)S(1)}, u32[]{:S(2)}, u32[]{:S(2)}) collective-permute-start(f32[4,2,8,512]{3,2,1,0:T(8,128)S(1)} %get-tuple-element.74.refs_8_.refs_0_), channel_id=1, source_target_pairs={{0,8},{1,9},{2,10},{3,11},{4,12},{5,13},{6,14},{7,15},{8,0},{9,1},... | collective-permute-start | bytes 393224 | tf_op jit(solution)/shard_map/ppermute | solution.py:311
  47.3 3.0 %collective-permute-start.18 = (f32[4,2,8,512]{3,2,1,0:T(8,128)S(1)}, f32[4,2,8,512]{3,2,1,0:T(8,128)S(1)}, u32[]{:S(2)}, u32[]{:S(2)}) collective-permute-start(f32[4,2,8,512]{3,2,1,0:T(8,128)S(1)} %collective-permute-done.9.refs_4_.refs_1_), channel_id=1, source_target_pairs={{0,8},{1,9},{2,10},{3,11},{4,12},{5,13},{6,14},{7,15},{8,0},{9,1},... | collective-permute-start | bytes 393224 | tf_op jit(solution)/shard_map/ppermute | solution.py:311
  47.7 2.5 %collective-permute-start.19 = (f32[4,2,8,512]{3,2,1,0:T(8,128)S(1)}, f32[4,2,8,512]{3,2,1,0:T(8,128)S(1)}, u32[]{:S(2)}, u32[]{:S(2)}) collective-permute-start(f32[4,2,8,512]{3,2,1,0:T(8,128)S(1)} %collective-permute-done.10.refs_5_.refs_2_), channel_id=1, source_target_pairs={{0,8},{1,9},{2,10},{3,11},{4,12},{5,13},{6,14},{7,15},{8,0},{9,1},... | collective-permute-start | bytes 393224 | tf_op jit(solution)/shard_map/ppermute | solution.py:311
  47.8 2.4 %collective-permute-start.20 = (f32[4,2,8,512]{3,2,1,0:T(8,128)S(1)}, f32[4,2,8,512]{3,2,1,0:T(8,128)S(1)}, u32[]{:S(2)}, u32[]{:S(2)}) collective-permute-start(f32[4,2,8,512]{3,2,1,0:T(8,128)S(1)} %collective-permute-done.11.refs_6_.refs_3_), channel_id=1, source_target_pairs={{0,8},{1,9},{2,10},{3,11},{4,12},{5,13},{6,14},{7,15},{8,0},{9,1},... | collective-permute-start | bytes 393224 | tf_op jit(solution)/shard_map/ppermute | solution.py:311
  49.4 16.8 %collective-permute-start.16 = (f32[4,3,16,512]{3,2,1,0:T(8,128)S(1)}, f32[4,3,16,512]{3,2,1,0:T(8,128)S(1)}, u32[]{:S(2)}, u32[]{:S(2)}) collective-permute-start(f32[4,3,16,512]{3,2,1,0:T(8,128)S(1)} %get-tuple-element.76), channel_id=1, source_target_pairs={{0,16},{1,17},{2,18},{3,19},{4,20},{5,21},{6,22},{7,23},{8,24},{9,... | collective-permute-start | bytes 1179656 | tf_op jit(solution)/shard_map/ppermute | solution.py:311
  51.1 15.1 %collective-permute-start.21 = (f32[4,2,16,512]{3,2,1,0:T(8,128)S(1)}, f32[4,2,16,512]{3,2,1,0:T(8,128)S(1)}, u32[]{:S(2)}, u32[]{:S(2)}) collective-permute-start(f32[4,2,16,512]{3,2,1,0:T(8,128)S(1)} %get-tuple-element.78), channel_id=1, source_target_pairs={{0,16},{1,17},{2,18},{3,19},{4,20},{5,21},{6,22},{7,23},{8,24},{9,... | collective-permute-start | bytes 786440 | tf_op jit(solution)/shard_map/ppermute | solution.py:311
  (1 other events, 1.3 us)

commit v4 on v3

--- a/solution.py
+++ b/solution.py
@@ -9,7 +9,7 @@
 
 COURANT = 0.4
 COEFS = (1.0 / 3.0, 0.5, 1.0)
-CHUNKS = ((2, 3, 0), (1, 4))
+CHUNKS = ((2, 3, 4), (0, 1))
 HALO = 6
 UNROLL = 4
 VMEM = pl.BlockSpec(memory_space=pltpu.VMEM)
@@ -25,16 +25,12 @@
     return jax.ShapeDtypeStruct(shape, dtype)
 
 
-def prep_kernel(chunk, x_ref, keep_ref, send_ref, near_ref, far_ref, buf, sem):
+def prep_kernel(x_ref, keep_ref, send_ref, near_ref, far_ref):
     rows, _, half, _ = keep_ref.shape
     odd = lax.rem(lax.axis_index("tile"), 2)
-    copies = [pltpu.make_async_copy(x_ref.at[:, f], buf.at[n], sem.at[n]) for n, f in enumerate(chunk)]
-    for copy in copies:
-        copy.start()
-    for n, copy in enumerate(copies):
-        copy.wait()
-        kept = jnp.swapaxes(buf[n, pl.ds(odd * half, half)], 0, 1)
-        sent = jnp.swapaxes(buf[n, pl.ds((1 - odd) * half, half)], 0, 1)
+    for n in range(keep_ref.shape[1]):
+        kept = jnp.swapaxes(x_ref[pl.ds(odd * half, half), n], 0, 1)
+        sent = jnp.swapaxes(x_ref[pl.ds((1 - odd) * half, half), n], 0, 1)
         for r in range(rows):
             turned = jnp.where(odd == 0, r, rows - 1 - r)
             keep_ref[turned, n] = kept[r]
@@ -44,21 +40,17 @@
         far_ref[r] = send_ref[rows - HALO + r]
 
 
-def prep(fields, chunk):
-    depth, _, rows, ny = fields.shape
-    shape = sds(rows, len(chunk), depth // 2, ny)
-    return pl.pallas_call(
-        functools.partial(prep_kernel, chunk),
+def prep(part):
+    depth, count, rows, ny = part.shape
+    shape = sds(rows, count, depth // 2, ny)
+    return pl.pallas_call(
+        prep_kernel,
         out_shape=[shape, shape] + [sds(HALO, *shape.shape[1:])] * 2,
-        in_specs=[pl.BlockSpec(memory_space=pltpu.HBM)],
+        in_specs=[VMEM],
         out_specs=[VMEM] * 4,
-        scratch_shapes=[
-            pltpu.VMEM((len(chunk), depth, rows, ny), F32),
-            pltpu.SemaphoreType.DMA((len(chunk),)),
-        ],
         compiler_params=PARAMS,
         cost_estimate=cost(shape.size * 2, [shape] * 4),
-    )(fields)
+    )(part)
 
 
 def ops_kernel(per, ops_ref, out_ref):
@@ -280,21 +272,43 @@
     )(use, ops, *blocks, earlier)
 
 
-def final_kernel(chips, chunks, *refs):
-    out, turn = refs[-2:]
+def final_kernel(chips, chunk, *refs):
+    blocks, (out, turn, done, sem) = refs[:chips], refs[-4:]
     place = lax.axis_index("lev") // 2
     odd = lax.rem(lax.axis_index("tile"), 2)
-    for c, chunk in enumerate(chunks):
-        for n, f in enumerate(chunk):
-            for a in range(chips):
-                block = refs[c * chips + a]
-                own = block.shape[0]
-                for q in range(own):
-                    row = (place ^ a) * own + q
-                    row = jnp.where(odd == 0, row, own * chips - 1 - row)
-                    turn[row] = block[q, n]
-            for low in range(0, out.shape[0], 8):
-                out[low : low + 8, f] = jnp.swapaxes(turn[:, low : low + 8], 0, 1)
+    copies = []
+    for n, f in enumerate(chunk):
+        for a in range(chips):
+            own = blocks[a].shape[0]
+            for q in range(own):
+                row = (place ^ a) * own + q
+                row = jnp.where(odd == 0, row, own * chips - 1 - row)
+                turn[row] = blocks[a][q, n]
+        for low in range(0, out.shape[0], 8):
+            done[n, low : low + 8] = jnp.swapaxes(turn[:, low : low + 8], 0, 1)
+        copies.append(pltpu.make_async_copy(done.at[n], out.at[:, f], sem.at[n]))
+        copies[-1].start()
+    for copy in copies:
+        copy.wait()
+
+
+def final(chunk, blocks, held, shape, size):
+    depth, _, rows, ny = shape
+    whole = [] if held is None else [held]
+    return pl.pallas_call(
+        functools.partial(final_kernel, len(blocks), chunk),
+        out_shape=sds(*shape),
+        in_specs=[VMEM] * len(blocks) + [pl.BlockSpec(memory_space=pl.ANY)] * len(whole),
+        out_specs=pl.BlockSpec(memory_space=pl.ANY),
+        input_output_aliases={len(blocks): 0} if whole else {},
+        scratch_shapes=[
+            pltpu.VMEM((rows, depth, ny), F32),
+            pltpu.VMEM((len(chunk), depth, rows, ny), F32),
+            pltpu.SemaphoreType.DMA((len(chunk),)),
+        ],
+        compiler_params=PARAMS,
+        cost_estimate=pl.CostEstimate(flops=size, bytes_accessed=1, transcendentals=0),
+    )(*blocks, *whole)
 
 
 def per_device(fields, land_use, column_ops):
@@ -337,12 +351,12 @@
         return [send(mixed[a], lambda lev, tile: (lev ^ 2 * a, tile)) if a else mixed[0] for a in range(chips)]
 
     first, second = CHUNKS
-    keep_a, away_a, near_a, far_a = prep(fields, first)
+    keep_a, away_a, near_a, far_a = prep(fields[:, first[0] : first[-1] + 1])
     recv_a = send(away_a, other)
     before_a = send(far_a, across)
     after_a = send(near_a, outward)
-    keep_b, away_b, near_b, far_b = prep(fields, second)
-    before_a, away_b, near_b, far_b = lax.optimization_barrier((before_a, away_b, near_b, far_b))
+    keep_b, away_b, near_b, far_b = prep(fields[:, second[0] : second[-1] + 1])
+    recv_a, after_a, away_b, near_b, far_b = lax.optimization_barrier((recv_a, after_a, away_b, near_b, far_b))
     recv_b = send(away_b, other)
     before_b = send(far_b, across)
     after_b = send(near_b, outward)
@@ -351,19 +365,12 @@
     blocks_a = outspread(outs_a)
     outs_b = advect((before_b, keep_b, recv_b, after_b), faces, chips)
     blocks_b = outspread(outs_b)
-    blocks_a = later(blocks_a, *blocks_b[1:])
-    returned = mixed_back(first, both_cores(blocks_a), outs_b[0])
-    returned += mixed_back(second, both_cores(blocks_b), returned[0])
-
-    return pl.pallas_call(
-        functools.partial(final_kernel, chips, CHUNKS),
-        out_shape=sds(*fields.shape),
-        in_specs=[VMEM] * len(returned),
-        out_specs=VMEM,
-        scratch_shapes=[pltpu.VMEM((rows, depth, ny), F32)],
-        compiler_params=PARAMS,
-        cost_estimate=cost(fields.size, returned + returned),
-    )(*returned)
+    blocks_a = later(blocks_a, outs_b[0], ops)
+    back_a = mixed_back(first, both_cores(blocks_a), outs_b[0])
+    blocks_b = later(blocks_b, back_a[0])
+    back_b = mixed_back(second, both_cores(blocks_b), back_a[0])
+    held = final(first, back_a, None, fields.shape, 10**9)
+    return final(second, back_b, held, fields.shape, 1)
 
 
 def solution(mesh):

time: 67.7 us -> 66.7 us (0.985)
  waiting for transfers between devices: 30.5 us -> 27.3 us
  local copies, waits for them, and re-layouts: 1.33 us -> 2.38 us
  starting transfers between devices: 23.6 us -> 24.3 us
    ppermute x22, waiting for transfers between devices: 30.5 us -> 27.3 us  [send(): return lax.ppermute(array, ('lev', 'tile'), pairs)]
    slice x0 -> x2, local copies, waits for them, and re-layouts: none -> 2.37 us  [the longest x1 1.19 us: per_device(): keep_a, away_a, near_a, far_a = prep(fields[:, first[0]:first[-1] + 1])]
    unnamed x6 -> x4, local copies, waits for them, and re-layouts: 1.33 us -> 0.01 us
    ppermute x22, starting transfers between devices: 23.6 us -> 24.3 us  [send(): return lax.ppermute(array, ('lev', 'tile'), pairs)]
    pallas_call x3 -> x4, Pallas kernels: 1.91 us -> 2.31 us  [the longest x2 1.94 us: final(): pl.pallas_call(functools.partial(final_kernel, len(blocks), chunk), out_s...]
  transfers between devices with their start and end apart: 22 -> 22, of which waited for: 6 -> 14; matrix products, arithmetic and copies ran while one was open for 0% -> 2% of each run, Pallas kernels for 15% -> 17%
where the time goes in v4:
time: 66.7 us; the launch traced here: 66.5 us
  waiting for transfers between devices  27.3 us (41%)
  starting transfers between devices  24.3 us (36%)
  Pallas kernels  12.3 us (18%)
  local copies, waits for them, and re-layouts  2.38 us (4%)
    ppermute x22, waiting for transfers between devices, send(): return lax.ppermute(array, ('lev', 'tile'), pairs)  27.3 us
    ppermute x22, starting transfers between devices, send(): return lax.ppermute(array, ('lev', 'tile'), pairs)  24.3 us
    pallas_call x2, Pallas kernels, advect(): pl.pallas_call(functools.partial(advect_kernel, chips, faces is None), ou...  7.7 us
    pallas_call x2, Pallas kernels, final(): pl.pallas_call(functools.partial(final_kernel, len(blocks), chunk), out_s...  1.94 us
    pallas_call x2, Pallas kernels, mix(): pl.pallas_call(functools.partial(mix_kernel, chips, chunk), out_shape=[sd...  1.93 us
  transfers between devices with their start and end apart: 22, of which 14 were waited for; matrix products, arithmetic and copies ran while one was open for 2% of the time, Pallas kernels for 17%

profile of v4, /device:TPU:0, one launch (start us, length us, event | category | flops | bytes accessed | tf_op | source)
XLA Modules:
  0.0 66.5 jit_solution(5350016028125818890)
XLA Ops:
  0.0 1.2 %slice.6.x_ref = f32[16,3,8,512]{3,2,1,0:T(8,128)S(1)} slice(f32[16,5,8,512]{3,2,1,0:T(8,128)} %param.3), slice={[0:16], [2:5], [0:8], [0:512]} | slice | bytes 1572864 | tf_op jit(solution)/shard_map/slice | solution.py:354
  1.4 3.0 %collective-permute-start = (f32[8,3,8,512]{3,2,1,0:T(8,128)S(1)}, f32[8,3,8,512]{3,2,1,0:T(8,128)S(1)}, u32[]{:S(2)}, u32[]{:S(2)}) collective-permute-start(f32[8,3,8,512]{3,2,1,0:T(8,128)S(1)} %get-tuple-element.47), channel_id=1, source_target_pairs={{0,1},{1,0},{2,3},{3,2},{4,5},{5,4},{6,7},{7,6},{8,9},{9,8},{10,11... | collective-permute-start | bytes 1179656 | tf_op jit(solution)/shard_map/ppermute | solution.py:325
  4.4 3.6 %collective-permute-start.1 = (f32[6,3,8,512]{3,2,1,0:T(8,128)S(1)}, f32[6,3,8,512]{3,2,1,0:T(8,128)S(1)}, u32[]{:S(2)}, u32[]{:S(2)}) collective-permute-start(f32[6,3,8,512]{3,2,1,0:T(8,128)S(1)} %get-tuple-element.48), channel_id=1, source_target_pairs={{0,6},{1,3},{2,0},{3,5},{4,2},{5,7},{6,4},{7,1},{8,14},{9,11},{10,... | collective-permute-start | bytes 884744 | tf_op jit(solution)/shard_map/ppermute | solution.py:325
  8.0 1.2 %slice.7.x_ref = f32[16,2,8,512]{3,2,1,0:T(8,128)S(1)} slice(f32[16,5,8,512]{3,2,1,0:T(8,128)} %param.3), slice={[0:16], [0:2], [0:8], [0:512]} | slice | bytes 1048576 | tf_op jit(solution)/shard_map/slice | solution.py:358
  9.4 6.1 %collective-permute-done.1.after = f32[6,3,8,512]{3,2,1,0:T(8,128)S(1)} collective-permute-done((f32[6,3,8,512]{3,2,1,0:T(8,128)S(1)}, f32[6,3,8,512]{3,2,1,0:T(8,128)S(1)}, u32[]{:S(2)}, u32[]{:S(2)}) %collective-permute-start.1) | collective-permute-done | bytes 294944 | tf_op jit(solution)/shard_map/ppermute | solution.py:325
  15.5 6.5 %collective-permute-done.recv = f32[8,3,8,512]{3,2,1,0:T(8,128)S(1)} collective-permute-done((f32[8,3,8,512]{3,2,1,0:T(8,128)S(1)}, f32[8,3,8,512]{3,2,1,0:T(8,128)S(1)}, u32[]{:S(2)}, u32[]{:S(2)}) %collective-permute-start) | collective-permute-done | bytes 393248 | tf_op jit(solution)/shard_map/ppermute | solution.py:325
  22.0 3.6 %collective-permute-start.2 = (f32[6,2,8,512]{3,2,1,0:T(8,128)S(1)}, f32[6,2,8,512]{3,2,1,0:T(8,128)S(1)}, u32[]{:S(2)}, u32[]{:S(2)}) collective-permute-start(f32[6,2,8,512]{3,2,1,0:T(8,128)S(1)} %get-tuple-element.52), channel_id=1, source_target_pairs={{0,7},{1,2},{2,1},{3,4},{4,3},{5,6},{6,5},{7,0},{8,15},{9,10},{10,... | collective-permute-start | bytes 589832 | tf_op jit(solution)/shard_map/ppermute | solution.py:325
  26.0 1.9 %collective-permute-start.4 = (f32[6,2,8,512]{3,2,1,0:T(8,128)S(1)}, f32[6,2,8,512]{3,2,1,0:T(8,128)S(1)}, u32[]{:S(2)}, u32[]{:S(2)}) collective-permute-start(f32[6,2,8,512]{3,2,1,0:T(8,128)S(1)} %get-tuple-element.55), channel_id=1, source_target_pairs={{0,6},{1,3},{2,0},{3,5},{4,2},{5,7},{6,4},{7,1},{8,14},{9,11},{10,... | collective-permute-start | bytes 589832 | tf_op jit(solution)/shard_map/ppermute | solution.py:325
  27.9 4.4 %shard_map.40 = (f32[25,8,512]{2,1,0:T(8,128)S(1)}, f32[24,8,512]{2,1,0:T(8,128)S(1)}, f32[24,8,512]{2,1,0:T(8,128)S(1)}, f32[21,8,512]{2,1,0:T(8,128)S(1)}, f32...) custom-call(f32[6,3,8,512]{3,2,1,0:T(8,128)S(1)} %collective-permute, ...), custom_call_target="tpu_custom_call" | custom-call | flops 1 | bytes 1 | tf_op jit(solution)/shard_map/pallas_call | solution.py:205
  32.4 1.6 %collective-permute-start.10 = (f32[4,3,8,512]{3,2,1,0:T(8,128)S(1)}, f32[4,3,8,512]{3,2,1,0:T(8,128)S(1)}, u32[]{:S(2)}, u32[]{:S(2)}) collective-permute-start(f32[4,3,8,512]{3,2,1,0:T(8,128)S(1)} %get-tuple-element.75), channel_id=1, source_target_pairs={{0,16},{1,17},{2,18},{3,19},{4,20},{5,21},{6,22},{7,23},{8,24},{9,... | collective-permute-start | bytes 589832 | tf_op jit(solution)/shard_map/ppermute | solution.py:325
  34.0 2.0 %collective-permute-start.9 = (f32[4,3,8,512]{3,2,1,0:T(8,128)S(1)}, f32[4,3,8,512]{3,2,1,0:T(8,128)S(1)}, u32[]{:S(2)}, u32[]{:S(2)}) collective-permute-start(f32[4,3,8,512]{3,2,1,0:T(8,128)S(1)} %get-tuple-element.74), channel_id=1, source_target_pairs={{0,1},{1,0},{2,3},{3,2},{4,5},{5,4},{6,7},{7,6},{8,9},{9,8},{10,11... | collective-permute-start | bytes 589832 | tf_op jit(solution)/shard_map/ppermute | solution.py:325
  36.4 3.3 %shard_map.41 = (f32[4,2,8,512]{3,2,1,0:T(8,128)S(1)}, f32[4,2,8,512]{3,2,1,0:T(8,128)S(1)}, f32[4,2,8,512]{3,2,1,0:T(8,128)S(1)}, f32[4,2,8,512]{3,2,1,0:T(8,128)S(1)}) custom-call(f32[6,2,8,512]{3,2,1,0:T(8,128)S(1)} %collective-permute-done.2.before, f32[8,2,8,512]{3,2,1,0:T(8,128)S(1)} %get-tuple-element.53.keep, ...), custom_call_target="tpu_custom_call" | custom-call | flops 1 | bytes 1 | tf_op jit(solution)/shard_map/pallas_call | solution.py:205
  40.5 1.2 %collective-permute-done.9.refs_1_ = f32[4,3,8,512]{3,2,1,0:T(8,128)S(1)} collective-permute-done((f32[4,3,8,512]{3,2,1,0:T(8,128)S(1)}, f32[4,3,8,512]{3,2,1,0:T(8,128)S(1)}, u32[]{:S(2)}, u32[]{:S(2)}) %collective-permute-start.9) | collective-permute-done | bytes 196640 | tf_op jit(solution)/shard_map/ppermute | solution.py:325
  43.2 1.5 %collective-permute-start.7 = (f32[4,2,8,512]{3,2,1,0:T(8,128)S(1)}, f32[4,2,8,512]{3,2,1,0:T(8,128)S(1)}, u32[]{:S(2)}, u32[]{:S(2)}) collective-permute-start(f32[4,2,8,512]{3,2,1,0:T(8,128)S(1)} %get-tuple-element.71), channel_id=1, source_target_pairs={{0,16},{1,17},{2,18},{3,19},{4,20},{5,21},{6,22},{7,23},{8,24},{9,... | collective-permute-start | bytes 393224 | tf_op jit(solution)/shard_map/ppermute | solution.py:325
  44.7 1.6 %collective-permute-start.8 = (f32[4,2,8,512]{3,2,1,0:T(8,128)S(1)}, f32[4,2,8,512]{3,2,1,0:T(8,128)S(1)}, u32[]{:S(2)}, u32[]{:S(2)}) collective-permute-start(f32[4,2,8,512]{3,2,1,0:T(8,128)S(1)} %get-tuple-element.72), channel_id=1, source_target_pairs={{0,17},{1,16},{2,19},{3,18},{4,21},{5,20},{6,23},{7,22},{8,25},{9,... | collective-permute-start | bytes 393224 | tf_op jit(solution)/shard_map/ppermute | solution.py:325
  46.3 1.1 %shard_map.43 = (f32[4,3,16,512]{3,2,1,0:T(8,128)S(1)}, f32[4,3,16,512]{3,2,1,0:T(8,128)S(1)}) custom-call(s32[8,512]{1,0:T(8,128)S(1)} %copy-done.1, bf16[5,256,192]{2,1,0:T(8,128)(2,1)S(1)} %shard_map.37.refs_5_.ops_ref, f32[4,3,8,512]{3,2,1,0:T(8,128)S(1)} %get-tuple-element.77.refs_0_, f32[4,3,8,512]{3,2,1,0:T(8,128)S(1)} %get-tuple-element.78.refs_1_, ...), custom_call_target="tpu_custom_call" | custom-call | flops 1 | bytes 1 | tf_op jit(solution)/shard_map/pallas_call | solution.py:261
  47.4 1.5 %collective-permute-start.21 = (f32[4,3,16,512]{3,2,1,0:T(8,128)S(1)}, f32[4,3,16,512]{3,2,1,0:T(8,128)S(1)}, u32[]{:S(2)}, u32[]{:S(2)}) collective-permute-start(f32[4,3,16,512]{3,2,1,0:T(8,128)S(1)} %get-tuple-element.88), channel_id=1, source_target_pairs={{0,16},{1,17},{2,18},{3,19},{4,20},{5,21},{6,22},{7,23},{8,24},{9,... | collective-permute-start | bytes 1179656 | tf_op jit(solution)/shard_map/ppermute | solution.py:325
  49.1 1.8 %collective-permute-done.7.refs_2_ = f32[4,2,8,512]{3,2,1,0:T(8,128)S(1)} collective-permute-done((f32[4,2,8,512]{3,2,1,0:T(8,128)S(1)}, f32[4,2,8,512]{3,2,1,0:T(8,128)S(1)}, u32[]{:S(2)}, u32[]{:S(2)}) %collective-permute-start.7) | collective-permute-done | bytes 131104 | tf_op jit(solution)/shard_map/ppermute | solution.py:325
  50.9 1.1 %collective-permute-done.8.refs_3_ = f32[4,2,8,512]{3,2,1,0:T(8,128)S(1)} collective-permute-done((f32[4,2,8,512]{3,2,1,0:T(8,128)S(1)}, f32[4,2,8,512]{3,2,1,0:T(8,128)S(1)}, u32[]{:S(2)}, u32[]{:S(2)}) %collective-permute-start.8) | collective-permute-done | bytes 131104 | tf_op jit(solution)/shard_map/ppermute | solution.py:325
  54.9 1.5 %collective-permute-start.20 = (f32[4,2,16,512]{3,2,1,0:T(8,128)S(1)}, f32[4,2,16,512]{3,2,1,0:T(8,128)S(1)}, u32[]{:S(2)}, u32[]{:S(2)}) collective-permute-start(f32[4,2,16,512]{3,2,1,0:T(8,128)S(1)} %get-tuple-element.87), channel_id=1, source_target_pairs={{0,16},{1,17},{2,18},{3,19},{4,20},{5,21},{6,22},{7,23},{8,24},{9,... | collective-permute-start | bytes 786440 | tf_op jit(solution)/shard_map/ppermute | solution.py:325
  56.3 4.1 %collective-permute-done.21.refs_1_ = f32[4,3,16,512]{3,2,1,0:T(8,128)S(1)} collective-permute-done((f32[4,3,16,512]{3,2,1,0:T(8,128)S(1)}, f32[4,3,16,512]{3,2,1,0:T(8,128)S(1)}, u32[]{:S(2)}, u32[]{:S(2)}) %collective-permute-start.21) | collective-permute-done | bytes 393248 | tf_op jit(solution)/shard_map/ppermute | solution.py:325
  60.5 1.0 %shard_map.46.refs_2_ = f32[16,5,8,512]{3,2,1,0:T(8,128)} custom-call(f32[4,3,16,512]{3,2,1,0:T(8,128)S(1)} %get-tuple-element.81.refs_4_.refs_8_.refs_0_, f32[4,3,16,512]{3,2,1,0:T(8,128)S(1)} %collective-permute-done.21.refs_1_), custom_call_target="tpu_custom_call" | custom-call | flops 1000000000 | bytes 1 | tf_op jit(solution)/shard_map/pallas_call | solution.py:298
  61.5 4.1 %collective-permute-done.20.refs_1_ = f32[4,2,16,512]{3,2,1,0:T(8,128)S(1)} collective-permute-done((f32[4,2,16,512]{3,2,1,0:T(8,128)S(1)}, f32[4,2,16,512]{3,2,1,0:T(8,128)S(1)}, u32[]{:S(2)}, u32[]{:S(2)}) %collective-permute-start.20) | collective-permute-done | bytes 262176 | tf_op jit(solution)/shard_map/ppermute | solution.py:325
  65.6 0.9 %shard_map.47 = f32[16,5,8,512]{3,2,1,0:T(8,128)} custom-call(f32[4,2,16,512]{3,2,1,0:T(8,128)S(1)} %get-tuple-element.86.refs_0_, f32[4,2,16,512]{3,2,1,0:T(8,128)S(1)} %collective-permute-done.20.refs_1_, f32[16,5,8,512]{3,2,1,0:T(8,128)} %shard_map.46.refs_2_), custom_call_target="tpu_custom_call", output_to_operand_aliasing={{}: (2, {})} | custom-call | flops 1 | bytes 1 | tf_op jit(solution)/shard_map/pallas_call | solution.py:298
  (37 shorter events, 6.6 us)
Async XLA Ops:
  1.4 20.6 %collective-permute-start = (f32[8,3,8,512]{3,2,1,0:T(8,128)S(1)}, f32[8,3,8,512]{3,2,1,0:T(8,128)S(1)}, u32[]{:S(2)}, u32[]{:S(2)}) collective-permute-start(f32[8,3,8,512]{3,2,1,0:T(8,128)S(1)} %get-tuple-element.47), channel_id=1, source_target_pairs={{0,1},{1,0},{2,3},{3,2},{4,5},{5,4},{6,7},{7,6},{8,9},{9,8},{10,11... | collective-permute-start | bytes 1179656 | tf_op jit(solution)/shard_map/ppermute | solution.py:325
  4.4 11.1 %collective-permute-start.1 = (f32[6,3,8,512]{3,2,1,0:T(8,128)S(1)}, f32[6,3,8,512]{3,2,1,0:T(8,128)S(1)}, u32[]{:S(2)}, u32[]{:S(2)}) collective-permute-start(f32[6,3,8,512]{3,2,1,0:T(8,128)S(1)} %get-tuple-element.48), channel_id=1, source_target_pairs={{0,6},{1,3},{2,0},{3,5},{4,2},{5,7},{6,4},{7,1},{8,14},{9,11},{10,... | collective-permute-start | bytes 884744 | tf_op jit(solution)/shard_map/ppermute | solution.py:325
  8.0 27.9 %copy-start = (f32[5,8,64,64]{3,2,1,0:T(8,128)S(1)}, f32[5,8,64,64]{3,2,1,0:T(8,128)}, u32[]{:S(2)}) copy-start(f32[5,8,64,64]{3,2,1,0:T(8,128)} %ops_ref.1) | copy-start | bytes 1966084
  8.0 19.9 %collective-permute-start.5 = (f32[6,3,8,512]{3,2,1,0:T(8,128)S(1)}, f32[6,3,8,512]{3,2,1,0:T(8,128)S(1)}, u32[]{:S(2)}, u32[]{:S(2)}) collective-permute-start(f32[6,3,8,512]{3,2,1,0:T(8,128)S(1)} %get-tuple-element.56), channel_id=1, source_target_pairs={{0,7},{1,2},{2,1},{3,4},{4,3},{5,6},{6,5},{7,0},{8,15},{9,10},{10,... | collective-permute-start | bytes 884744 | tf_op jit(solution)/shard_map/ppermute | solution.py:325
  22.0 12.0 %collective-permute-start.2 = (f32[6,2,8,512]{3,2,1,0:T(8,128)S(1)}, f32[6,2,8,512]{3,2,1,0:T(8,128)S(1)}, u32[]{:S(2)}, u32[]{:S(2)}) collective-permute-start(f32[6,2,8,512]{3,2,1,0:T(8,128)S(1)} %get-tuple-element.52), channel_id=1, source_target_pairs={{0,7},{1,2},{2,1},{3,4},{4,3},{5,6},{6,5},{7,0},{8,15},{9,10},{10,... | collective-permute-start | bytes 589832 | tf_op jit(solution)/shard_map/ppermute | solution.py:325
  25.5 10.8 %collective-permute-start.3 = (f32[8,2,8,512]{3,2,1,0:T(8,128)S(1)}, f32[8,2,8,512]{3,2,1,0:T(8,128)S(1)}, u32[]{:S(2)}, u32[]{:S(2)}) collective-permute-start(f32[8,2,8,512]{3,2,1,0:T(8,128)S(1)} %get-tuple-element.54), channel_id=1, source_target_pairs={{0,1},{1,0},{2,3},{3,2},{4,5},{5,4},{6,7},{7,6},{8,9},{9,8},{10,11... | collective-permute-start | bytes 786440 | tf_op jit(solution)/shard_map/ppermute | solution.py:325
  26.0 10.4 %collective-permute-start.4 = (f32[6,2,8,512]{3,2,1,0:T(8,128)S(1)}, f32[6,2,8,512]{3,2,1,0:T(8,128)S(1)}, u32[]{:S(2)}, u32[]{:S(2)}) collective-permute-start(f32[6,2,8,512]{3,2,1,0:T(8,128)S(1)} %get-tuple-element.55), channel_id=1, source_target_pairs={{0,6},{1,3},{2,0},{3,5},{4,2},{5,7},{6,4},{7,1},{8,14},{9,11},{10,... | collective-permute-start | bytes 589832 | tf_op jit(solution)/shard_map/ppermute | solution.py:325
  32.4 7.3 %collective-permute-start.10 = (f32[4,3,8,512]{3,2,1,0:T(8,128)S(1)}, f32[4,3,8,512]{3,2,1,0:T(8,128)S(1)}, u32[]{:S(2)}, u32[]{:S(2)}) collective-permute-start(f32[4,3,8,512]{3,2,1,0:T(8,128)S(1)} %get-tuple-element.75), channel_id=1, source_target_pairs={{0,16},{1,17},{2,18},{3,19},{4,20},{5,21},{6,22},{7,23},{8,24},{9,... | collective-permute-start | bytes 589832 | tf_op jit(solution)/shard_map/ppermute | solution.py:325
  34.0 6.6 %collective-permute-start.11 = (f32[4,3,8,512]{3,2,1,0:T(8,128)S(1)}, f32[4,3,8,512]{3,2,1,0:T(8,128)S(1)}, u32[]{:S(2)}, u32[]{:S(2)}) collective-permute-start(f32[4,3,8,512]{3,2,1,0:T(8,128)S(1)} %get-tuple-element.76), channel_id=1, source_target_pairs={{0,17},{1,16},{2,19},{3,18},{4,21},{5,20},{6,23},{7,22},{8,25},{9,... | collective-permute-start | bytes 589832 | tf_op jit(solution)/shard_map/ppermute | solution.py:325
  34.0 7.8 %collective-permute-start.9 = (f32[4,3,8,512]{3,2,1,0:T(8,128)S(1)}, f32[4,3,8,512]{3,2,1,0:T(8,128)S(1)}, u32[]{:S(2)}, u32[]{:S(2)}) collective-permute-start(f32[4,3,8,512]{3,2,1,0:T(8,128)S(1)} %get-tuple-element.74), channel_id=1, source_target_pairs={{0,1},{1,0},{2,3},{3,2},{4,5},{5,4},{6,7},{7,6},{8,9},{9,8},{10,11... | collective-permute-start | bytes 589832 | tf_op jit(solution)/shard_map/ppermute | solution.py:325
  39.7 6.6 %copy-start.1 = (s32[8,512]{1,0:T(8,128)S(1)}, s32[8,512]{1,0:T(8,128)}, u32[]{:S(2)}) copy-start(s32[8,512]{1,0:T(8,128)} %use_ref.3) | copy-start | bytes 49156
  41.7 1.4 %collective-permute-start.12 = (f32[4,3,8,512]{3,2,1,0:T(8,128)S(1)}, f32[4,3,8,512]{3,2,1,0:T(8,128)S(1)}, u32[]{:S(2)}, u32[]{:S(2)}) collective-permute-start(f32[4,3,8,512]{3,2,1,0:T(8,128)S(1)} %get-tuple-element.77.refs_0_), channel_id=1, source_target_pairs={{0,8},{1,9},{2,10},{3,11},{4,12},{5,13},{6,14},{7,15},{8,0},{9,1},... | collective-permute-start | bytes 589832 | tf_op jit(solution)/shard_map/ppermute | solution.py:325
  41.7 2.9 %collective-permute-start.13 = (f32[4,3,8,512]{3,2,1,0:T(8,128)S(1)}, f32[4,3,8,512]{3,2,1,0:T(8,128)S(1)}, u32[]{:S(2)}, u32[]{:S(2)}) collective-permute-start(f32[4,3,8,512]{3,2,1,0:T(8,128)S(1)} %get-tuple-element.78.refs_1_), channel_id=1, source_target_pairs={{0,8},{1,9},{2,10},{3,11},{4,12},{5,13},{6,14},{7,15},{8,0},{9,1},... | collective-permute-start | bytes 589832 | tf_op jit(solution)/shard_map/ppermute | solution.py:325
  42.2 4.0 %collective-permute-start.14 = (f32[4,3,8,512]{3,2,1,0:T(8,128)S(1)}, f32[4,3,8,512]{3,2,1,0:T(8,128)S(1)}, u32[]{:S(2)}, u32[]{:S(2)}) collective-permute-start(f32[4,3,8,512]{3,2,1,0:T(8,128)S(1)} %get-tuple-element.79.refs_2_), channel_id=1, source_target_pairs={{0,8},{1,9},{2,10},{3,11},{4,12},{5,13},{6,14},{7,15},{8,0},{9,1},... | collective-permute-start | bytes 589832 | tf_op jit(solution)/shard_map/ppermute | solution.py:325
  42.3 4.0 %collective-permute-start.15 = (f32[4,3,8,512]{3,2,1,0:T(8,128)S(1)}, f32[4,3,8,512]{3,2,1,0:T(8,128)S(1)}, u32[]{:S(2)}, u32[]{:S(2)}) collective-permute-start(f32[4,3,8,512]{3,2,1,0:T(8,128)S(1)} %get-tuple-element.80.refs_3_), channel_id=1, source_target_pairs={{0,8},{1,9},{2,10},{3,11},{4,12},{5,13},{6,14},{7,15},{8,0},{9,1},... | collective-permute-start | bytes 589832 | tf_op jit(solution)/shard_map/ppermute | solution.py:325
  42.8 6.4 %collective-permute-start.6 = (f32[4,2,8,512]{3,2,1,0:T(8,128)S(1)}, f32[4,2,8,512]{3,2,1,0:T(8,128)S(1)}, u32[]{:S(2)}, u32[]{:S(2)}) collective-permute-start(f32[4,2,8,512]{3,2,1,0:T(8,128)S(1)} %get-tuple-element.70), channel_id=1, source_target_pairs={{0,1},{1,0},{2,3},{3,2},{4,5},{5,4},{6,7},{7,6},{8,9},{9,8},{10,11... | collective-permute-start | bytes 393224 | tf_op jit(solution)/shard_map/ppermute | solution.py:325
  43.2 7.7 %collective-permute-start.7 = (f32[4,2,8,512]{3,2,1,0:T(8,128)S(1)}, f32[4,2,8,512]{3,2,1,0:T(8,128)S(1)}, u32[]{:S(2)}, u32[]{:S(2)}) collective-permute-start(f32[4,2,8,512]{3,2,1,0:T(8,128)S(1)} %get-tuple-element.71), channel_id=1, source_target_pairs={{0,16},{1,17},{2,18},{3,19},{4,20},{5,21},{6,22},{7,23},{8,24},{9,... | collective-permute-start | bytes 393224 | tf_op jit(solution)/shard_map/ppermute | solution.py:325
  44.7 7.3 %collective-permute-start.8 = (f32[4,2,8,512]{3,2,1,0:T(8,128)S(1)}, f32[4,2,8,512]{3,2,1,0:T(8,128)S(1)}, u32[]{:S(2)}, u32[]{:S(2)}) collective-permute-start(f32[4,2,8,512]{3,2,1,0:T(8,128)S(1)} %get-tuple-element.72), channel_id=1, source_target_pairs={{0,17},{1,16},{2,19},{3,18},{4,21},{5,20},{6,23},{7,22},{8,25},{9,... | collective-permute-start | bytes 393224 | tf_op jit(solution)/shard_map/ppermute | solution.py:325
  47.4 13.1 %collective-permute-start.21 = (f32[4,3,16,512]{3,2,1,0:T(8,128)S(1)}, f32[4,3,16,512]{3,2,1,0:T(8,128)S(1)}, u32[]{:S(2)}, u32[]{:S(2)}) collective-permute-start(f32[4,3,16,512]{3,2,1,0:T(8,128)S(1)} %get-tuple-element.88), channel_id=1, source_target_pairs={{0,16},{1,17},{2,18},{3,19},{4,20},{5,21},{6,22},{7,23},{8,24},{9,... | collective-permute-start | bytes 1179656 | tf_op jit(solution)/shard_map/ppermute | solution.py:325
  52.0 1.3 %collective-permute-start.16 = (f32[4,2,8,512]{3,2,1,0:T(8,128)S(1)}, f32[4,2,8,512]{3,2,1,0:T(8,128)S(1)}, u32[]{:S(2)}, u32[]{:S(2)}) collective-permute-start(f32[4,2,8,512]{3,2,1,0:T(8,128)S(1)} %get-tuple-element.82.refs_0_), channel_id=1, source_target_pairs={{0,8},{1,9},{2,10},{3,11},{4,12},{5,13},{6,14},{7,15},{8,0},{9,1},... | collective-permute-start | bytes 393224 | tf_op jit(solution)/shard_map/ppermute | solution.py:325
  52.0 1.5 %collective-permute-start.17 = (f32[4,2,8,512]{3,2,1,0:T(8,128)S(1)}, f32[4,2,8,512]{3,2,1,0:T(8,128)S(1)}, u32[]{:S(2)}, u32[]{:S(2)}) collective-permute-start(f32[4,2,8,512]{3,2,1,0:T(8,128)S(1)} %get-tuple-element.83.refs_1_), channel_id=1, source_target_pairs={{0,8},{1,9},{2,10},{3,11},{4,12},{5,13},{6,14},{7,15},{8,0},{9,1},... | collective-permute-start | bytes 393224 | tf_op jit(solution)/shard_map/ppermute | solution.py:325
  52.5 1.3 %collective-permute-start.18 = (f32[4,2,8,512]{3,2,1,0:T(8,128)S(1)}, f32[4,2,8,512]{3,2,1,0:T(8,128)S(1)}, u32[]{:S(2)}, u32[]{:S(2)}) collective-permute-start(f32[4,2,8,512]{3,2,1,0:T(8,128)S(1)} %get-tuple-element.84.refs_2_), channel_id=1, source_target_pairs={{0,8},{1,9},{2,10},{3,11},{4,12},{5,13},{6,14},{7,15},{8,0},{9,1},... | collective-permute-start | bytes 393224 | tf_op jit(solution)/shard_map/ppermute | solution.py:325
  52.5 1.5 %collective-permute-start.19 = (f32[4,2,8,512]{3,2,1,0:T(8,128)S(1)}, f32[4,2,8,512]{3,2,1,0:T(8,128)S(1)}, u32[]{:S(2)}, u32[]{:S(2)}) collective-permute-start(f32[4,2,8,512]{3,2,1,0:T(8,128)S(1)} %get-tuple-element.85.refs_3_), channel_id=1, source_target_pairs={{0,8},{1,9},{2,10},{3,11},{4,12},{5,13},{6,14},{7,15},{8,0},{9,1},... | collective-permute-start | bytes 393224 | tf_op jit(solution)/shard_map/ppermute | solution.py:325
  54.9 10.7 %collective-permute-start.20 = (f32[4,2,16,512]{3,2,1,0:T(8,128)S(1)}, f32[4,2,16,512]{3,2,1,0:T(8,128)S(1)}, u32[]{:S(2)}, u32[]{:S(2)}) collective-permute-start(f32[4,2,16,512]{3,2,1,0:T(8,128)S(1)} %get-tuple-element.87), channel_id=1, source_target_pairs={{0,16},{1,17},{2,18},{3,19},{4,20},{5,21},{6,22},{7,23},{8,24},{9,... | collective-permute-start | bytes 786440 | tf_op jit(solution)/shard_map/ppermute | solution.py:325

commit v5 on v4

--- a/solution.py
+++ b/solution.py
@@ -356,7 +356,7 @@
     before_a = send(far_a, across)
     after_a = send(near_a, outward)
     keep_b, away_b, near_b, far_b = prep(fields[:, second[0] : second[-1] + 1])
-    recv_a, after_a, away_b, near_b, far_b = lax.optimization_barrier((recv_a, after_a, away_b, near_b, far_b))
+    before_a, away_b, near_b, far_b = lax.optimization_barrier((before_a, away_b, near_b, far_b))
     recv_b = send(away_b, other)
     before_b = send(far_b, across)
     after_b = send(near_b, outward)
@@ -365,7 +365,7 @@
     blocks_a = outspread(outs_a)
     outs_b = advect((before_b, keep_b, recv_b, after_b), faces, chips)
     blocks_b = outspread(outs_b)
-    blocks_a = later(blocks_a, outs_b[0], ops)
+    blocks_a = later(blocks_a, *blocks_b[1:], ops)
     back_a = mixed_back(first, both_cores(blocks_a), outs_b[0])
     blocks_b = later(blocks_b, back_a[0])
     back_b = mixed_back(second, both_cores(blocks_b), back_a[0])

time: 66.7 us -> 66.4 us (level)
  transfers between devices with their start and end apart: 22 -> 22, of which waited for: 14 -> 17; matrix products, arithmetic and copies ran while one was open for 2% -> 2% of each run, Pallas kernels for 17% -> 15%
where the time goes in v5:
time: 66.4 us; the launch traced here: 66.2 us
  waiting for transfers between devices  27.6 us (42%)
  starting transfers between devices  23.8 us (36%)
  Pallas kernels  12.3 us (19%)
  local copies, waits for them, and re-layouts  2.28 us (3%)
    ppermute x22, waiting for transfers between devices, send(): return lax.ppermute(array, ('lev', 'tile'), pairs)  27.6 us
    ppermute x22, starting transfers between devices, send(): return lax.ppermute(array, ('lev', 'tile'), pairs)  23.8 us
    pallas_call x2, Pallas kernels, advect(): pl.pallas_call(functools.partial(advect_kernel, chips, faces is None), ou...  7.7 us
    pallas_call x2, Pallas kernels, final(): pl.pallas_call(functools.partial(final_kernel, len(blocks), chunk), out_s...  1.94 us
    pallas_call x2, Pallas kernels, mix(): pl.pallas_call(functools.partial(mix_kernel, chips, chunk), out_shape=[sd...  1.92 us
  transfers between devices with their start and end apart: 22, of which 17 were waited for; matrix products, arithmetic and copies ran while one was open for 2% of the time, Pallas kernels for 15%

profile of v5, /device:TPU:0, one launch (start us, length us, event | category | flops | bytes accessed | tf_op | source)
XLA Modules:
  0.0 66.2 jit_solution(11164010805416867917)
XLA Ops:
  0.0 1.2 %slice.6.x_ref = f32[16,3,8,512]{3,2,1,0:T(8,128)S(1)} slice(f32[16,5,8,512]{3,2,1,0:T(8,128)} %param.3), slice={[0:16], [2:5], [0:8], [0:512]} | slice | bytes 1572864 | tf_op jit(solution)/shard_map/slice | solution.py:354
  1.4 3.0 %collective-permute-start.4 = (f32[8,3,8,512]{3,2,1,0:T(8,128)S(1)}, f32[8,3,8,512]{3,2,1,0:T(8,128)S(1)}, u32[]{:S(2)}, u32[]{:S(2)}) collective-permute-start(f32[8,3,8,512]{3,2,1,0:T(8,128)S(1)} %get-tuple-element.56), channel_id=1, source_target_pairs={{0,1},{1,0},{2,3},{3,2},{4,5},{5,4},{6,7},{7,6},{8,9},{9,8},{10,11... | collective-permute-start | bytes 1179656 | tf_op jit(solution)/shard_map/ppermute | solution.py:325
  4.4 3.6 %collective-permute-start = (f32[6,3,8,512]{3,2,1,0:T(8,128)S(1)}, f32[6,3,8,512]{3,2,1,0:T(8,128)S(1)}, u32[]{:S(2)}, u32[]{:S(2)}) collective-permute-start(f32[6,3,8,512]{3,2,1,0:T(8,128)S(1)} %get-tuple-element.46), channel_id=1, source_target_pairs={{0,7},{1,2},{2,1},{3,4},{4,3},{5,6},{6,5},{7,0},{8,15},{9,10},{10,... | collective-permute-start | bytes 884744 | tf_op jit(solution)/shard_map/ppermute | solution.py:325
  8.4 1.1 %slice.7.x_ref = f32[16,2,8,512]{3,2,1,0:T(8,128)S(1)} slice(f32[16,5,8,512]{3,2,1,0:T(8,128)} %param.3), slice={[0:16], [0:2], [0:8], [0:512]} | slice | bytes 1048576 | tf_op jit(solution)/shard_map/slice | solution.py:358
  9.7 7.4 %collective-permute-done.before = f32[6,3,8,512]{3,2,1,0:T(8,128)S(1)} collective-permute-done((f32[6,3,8,512]{3,2,1,0:T(8,128)S(1)}, f32[6,3,8,512]{3,2,1,0:T(8,128)S(1)}, u32[]{:S(2)}, u32[]{:S(2)}) %collective-permute-start) | collective-permute-done | bytes 294944 | tf_op jit(solution)/shard_map/ppermute | solution.py:325
  17.1 3.6 %collective-permute-start.1 = (f32[6,2,8,512]{3,2,1,0:T(8,128)S(1)}, f32[6,2,8,512]{3,2,1,0:T(8,128)S(1)}, u32[]{:S(2)}, u32[]{:S(2)}) collective-permute-start(f32[6,2,8,512]{3,2,1,0:T(8,128)S(1)} %get-tuple-element.50), channel_id=1, source_target_pairs={{0,7},{1,2},{2,1},{3,4},{4,3},{5,6},{6,5},{7,0},{8,15},{9,10},{10,... | collective-permute-start | bytes 589832 | tf_op jit(solution)/shard_map/ppermute | solution.py:325
  21.8 1.3 %collective-permute-done.4.recv = f32[8,3,8,512]{3,2,1,0:T(8,128)S(1)} collective-permute-done((f32[8,3,8,512]{3,2,1,0:T(8,128)S(1)}, f32[8,3,8,512]{3,2,1,0:T(8,128)S(1)}, u32[]{:S(2)}, u32[]{:S(2)}) %collective-permute-start.4) | collective-permute-done | bytes 393248 | tf_op jit(solution)/shard_map/ppermute | solution.py:325
  23.0 4.4 %shard_map.40 = (f32[25,8,512]{2,1,0:T(8,128)S(1)}, f32[24,8,512]{2,1,0:T(8,128)S(1)}, f32[24,8,512]{2,1,0:T(8,128)S(1)}, f32[21,8,512]{2,1,0:T(8,128)S(1)}, f32...) custom-call(f32[6,3,8,512]{3,2,1,0:T(8,128)S(1)} %collective-permute, ...), custom_call_target="tpu_custom_call" | custom-call | flops 1 | bytes 1 | tf_op jit(solution)/shard_map/pallas_call | solution.py:205
  27.5 1.6 %collective-permute-start.10 = (f32[4,3,8,512]{3,2,1,0:T(8,128)S(1)}, f32[4,3,8,512]{3,2,1,0:T(8,128)S(1)}, u32[]{:S(2)}, u32[]{:S(2)}) collective-permute-start(f32[4,3,8,512]{3,2,1,0:T(8,128)S(1)} %get-tuple-element.73), channel_id=1, source_target_pairs={{0,16},{1,17},{2,18},{3,19},{4,20},{5,21},{6,22},{7,23},{8,24},{9,... | collective-permute-start | bytes 589832 | tf_op jit(solution)/shard_map/ppermute | solution.py:325
  29.1 2.9 %collective-permute-start.11 = (f32[4,3,8,512]{3,2,1,0:T(8,128)S(1)}, f32[4,3,8,512]{3,2,1,0:T(8,128)S(1)}, u32[]{:S(2)}, u32[]{:S(2)}) collective-permute-start(f32[4,3,8,512]{3,2,1,0:T(8,128)S(1)} %get-tuple-element.74), channel_id=1, source_target_pairs={{0,17},{1,16},{2,19},{3,18},{4,21},{5,20},{6,23},{7,22},{8,25},{9,... | collective-permute-start | bytes 589832 | tf_op jit(solution)/shard_map/ppermute | solution.py:325
  32.1 3.3 %shard_map.41 = (f32[4,2,8,512]{3,2,1,0:T(8,128)S(1)}, f32[4,2,8,512]{3,2,1,0:T(8,128)S(1)}, f32[4,2,8,512]{3,2,1,0:T(8,128)S(1)}, f32[4,2,8,512]{3,2,1,0:T(8,128)S(1)}) custom-call(f32[6,2,8,512]{3,2,1,0:T(8,128)S(1)} %collective-permute-done.1.before, f32[8,2,8,512]{3,2,1,0:T(8,128)S(1)} %get-tuple-element.51.keep, ...), custom_call_target="tpu_custom_call" | custom-call | flops 1 | bytes 1 | tf_op jit(solution)/shard_map/pallas_call | solution.py:205
  35.4 2.0 %collective-permute-start.6 = (f32[4,2,8,512]{3,2,1,0:T(8,128)S(1)}, f32[4,2,8,512]{3,2,1,0:T(8,128)S(1)}, u32[]{:S(2)}, u32[]{:S(2)}) collective-permute-start(f32[4,2,8,512]{3,2,1,0:T(8,128)S(1)} %get-tuple-element.68), channel_id=1, source_target_pairs={{0,1},{1,0},{2,3},{3,2},{4,5},{5,4},{6,7},{7,6},{8,9},{9,8},{10,11... | collective-permute-start | bytes 393224 | tf_op jit(solution)/shard_map/ppermute | solution.py:325
  37.3 1.6 %collective-permute-start.7 = (f32[4,2,8,512]{3,2,1,0:T(8,128)S(1)}, f32[4,2,8,512]{3,2,1,0:T(8,128)S(1)}, u32[]{:S(2)}, u32[]{:S(2)}) collective-permute-start(f32[4,2,8,512]{3,2,1,0:T(8,128)S(1)} %get-tuple-element.69), channel_id=1, source_target_pairs={{0,16},{1,17},{2,18},{3,19},{4,20},{5,21},{6,22},{7,23},{8,24},{9,... | collective-permute-start | bytes 393224 | tf_op jit(solution)/shard_map/ppermute | solution.py:325
  39.7 1.2 %collective-permute-done.9.refs_1_ = f32[4,3,8,512]{3,2,1,0:T(8,128)S(1)} collective-permute-done((f32[4,3,8,512]{3,2,1,0:T(8,128)S(1)}, f32[4,3,8,512]{3,2,1,0:T(8,128)S(1)}, u32[]{:S(2)}, u32[]{:S(2)}) %collective-permute-start.9) | collective-permute-done | bytes 196640 | tf_op jit(solution)/shard_map/ppermute | solution.py:325
  40.9 1.4 %collective-permute-done.6.refs_4_.refs_1_ = f32[4,2,8,512]{3,2,1,0:T(8,128)S(1)} collective-permute-done((f32[4,2,8,512]{3,2,1,0:T(8,128)S(1)}, f32[4,2,8,512]{3,2,1,0:T(8,128)S(1)}, u32[]{:S(2)}, u32[]{:S(2)}) %collective-permute-start.6) | collective-permute-done | bytes 131104 | tf_op jit(solution)/shard_map/ppermute | solution.py:325
  42.3 0.6 collective-permute-done.7.refs_5_.refs_2_
  43.0 2.0 %collective-permute-done.8.refs_6_.refs_3_ = f32[4,2,8,512]{3,2,1,0:T(8,128)S(1)} collective-permute-done((f32[4,2,8,512]{3,2,1,0:T(8,128)S(1)}, f32[4,2,8,512]{3,2,1,0:T(8,128)S(1)}, u32[]{:S(2)}, u32[]{:S(2)}) %collective-permute-start.8) | collective-permute-done | bytes 131104 | tf_op jit(solution)/shard_map/ppermute | solution.py:325
  47.2 1.1 %shard_map.43 = (f32[4,3,16,512]{3,2,1,0:T(8,128)S(1)}, f32[4,3,16,512]{3,2,1,0:T(8,128)S(1)}) custom-call(s32[8,512]{1,0:T(8,128)S(1)} %copy-done.1, bf16[5,256,192]{2,1,0:T(8,128)(2,1)S(1)} %shard_map.37.refs_7_.ops_ref, f32[4,3,8,512]{3,2,1,0:T(8,128)S(1)} %get-tuple-element.75.refs_0_, f32[4,3,8,512]{3,2,1,0:T(8,128)S(1)} %get-tuple-element.76.refs_1_, ...), custom_call_target="tpu_custom_call" | custom-call | flops 1 | bytes 1 | tf_op jit(solution)/shard_map/pallas_call | solution.py:261
  50.8 0.8 %shard_map.45 = (f32[4,2,16,512]{3,2,1,0:T(8,128)S(1)}, f32[4,2,16,512]{3,2,1,0:T(8,128)S(1)}) custom-call(s32[8,512]{1,0:T(8,128)S(1)} %copy-done.1, bf16[5,256,192]{2,1,0:T(8,128)(2,1)S(1)} %shard_map.37.refs_7_.ops_ref, f32[4,2,8,512]{3,2,1,0:T(8,128)S(1)} %get-tuple-element.80.refs_0_, f32[4,2,8,512]{3,2,1,0:T(8,128)S(1)} %get-tuple-element.81.refs_1_, ...), custom_call_target="tpu_custom_call" | custom-call | flops 1 | bytes 1 | tf_op jit(solution)/shard_map/pallas_call | solution.py:261
  51.6 1.7 %collective-permute-start.20 = (f32[4,2,16,512]{3,2,1,0:T(8,128)S(1)}, f32[4,2,16,512]{3,2,1,0:T(8,128)S(1)}, u32[]{:S(2)}, u32[]{:S(2)}) collective-permute-start(f32[4,2,16,512]{3,2,1,0:T(8,128)S(1)} %get-tuple-element.85), channel_id=1, source_target_pairs={{0,16},{1,17},{2,18},{3,19},{4,20},{5,21},{6,22},{7,23},{8,24},{9,... | collective-permute-start | bytes 786440 | tf_op jit(solution)/shard_map/ppermute | solution.py:325
  53.4 7.0 %collective-permute-done.21.refs_1_ = f32[4,3,16,512]{3,2,1,0:T(8,128)S(1)} collective-permute-done((f32[4,3,16,512]{3,2,1,0:T(8,128)S(1)}, f32[4,3,16,512]{3,2,1,0:T(8,128)S(1)}, u32[]{:S(2)}, u32[]{:S(2)}) %collective-permute-start.21) | collective-permute-done | bytes 393248 | tf_op jit(solution)/shard_map/ppermute | solution.py:325
  60.4 1.0 %shard_map.46.refs_2_ = f32[16,5,8,512]{3,2,1,0:T(8,128)} custom-call(f32[4,3,16,512]{3,2,1,0:T(8,128)S(1)} %get-tuple-element.79.refs_4_.refs_8_.refs_0_, f32[4,3,16,512]{3,2,1,0:T(8,128)S(1)} %collective-permute-done.21.refs_1_), custom_call_target="tpu_custom_call" | custom-call | flops 1000000000 | bytes 1 | tf_op jit(solution)/shard_map/pallas_call | solution.py:298
  61.4 3.9 %collective-permute-done.20.refs_1_ = f32[4,2,16,512]{3,2,1,0:T(8,128)S(1)} collective-permute-done((f32[4,2,16,512]{3,2,1,0:T(8,128)S(1)}, f32[4,2,16,512]{3,2,1,0:T(8,128)S(1)}, u32[]{:S(2)}, u32[]{:S(2)}) %collective-permute-start.20) | collective-permute-done | bytes 262176 | tf_op jit(solution)/shard_map/ppermute | solution.py:325
  65.3 0.9 %shard_map.47 = f32[16,5,8,512]{3,2,1,0:T(8,128)} custom-call(f32[4,2,16,512]{3,2,1,0:T(8,128)S(1)} %get-tuple-element.84.refs_0_, f32[4,2,16,512]{3,2,1,0:T(8,128)S(1)} %collective-permute-done.20.refs_1_, f32[16,5,8,512]{3,2,1,0:T(8,128)} %shard_map.46.refs_2_), custom_call_target="tpu_custom_call", output_to_operand_aliasing={{}: (2, {})} | custom-call | flops 1 | bytes 1 | tf_op jit(solution)/shard_map/pallas_call | solution.py:298
  (37 shorter events, 7.5 us)
Async XLA Ops:
  1.4 21.6 %collective-permute-start.4 = (f32[8,3,8,512]{3,2,1,0:T(8,128)S(1)}, f32[8,3,8,512]{3,2,1,0:T(8,128)S(1)}, u32[]{:S(2)}, u32[]{:S(2)}) collective-permute-start(f32[8,3,8,512]{3,2,1,0:T(8,128)S(1)} %get-tuple-element.56), channel_id=1, source_target_pairs={{0,1},{1,0},{2,3},{3,2},{4,5},{5,4},{6,7},{7,6},{8,9},{9,8},{10,11... | collective-permute-start | bytes 1179656 | tf_op jit(solution)/shard_map/ppermute | solution.py:325
  4.4 12.7 %collective-permute-start = (f32[6,3,8,512]{3,2,1,0:T(8,128)S(1)}, f32[6,3,8,512]{3,2,1,0:T(8,128)S(1)}, u32[]{:S(2)}, u32[]{:S(2)}) collective-permute-start(f32[6,3,8,512]{3,2,1,0:T(8,128)S(1)} %get-tuple-element.46), channel_id=1, source_target_pairs={{0,7},{1,2},{2,1},{3,4},{4,3},{5,6},{6,5},{7,0},{8,15},{9,10},{10,... | collective-permute-start | bytes 884744 | tf_op jit(solution)/shard_map/ppermute | solution.py:325
  8.0 13.8 %collective-permute-start.5 = (f32[6,3,8,512]{3,2,1,0:T(8,128)S(1)}, f32[6,3,8,512]{3,2,1,0:T(8,128)S(1)}, u32[]{:S(2)}, u32[]{:S(2)}) collective-permute-start(f32[6,3,8,512]{3,2,1,0:T(8,128)S(1)} %get-tuple-element.57), channel_id=1, source_target_pairs={{0,6},{1,3},{2,0},{3,5},{4,2},{5,7},{6,4},{7,1},{8,14},{9,11},{10,... | collective-permute-start | bytes 884744 | tf_op jit(solution)/shard_map/ppermute | solution.py:325
  17.1 15.0 %collective-permute-start.2 = (f32[8,2,8,512]{3,2,1,0:T(8,128)S(1)}, f32[8,2,8,512]{3,2,1,0:T(8,128)S(1)}, u32[]{:S(2)}, u32[]{:S(2)}) collective-permute-start(f32[8,2,8,512]{3,2,1,0:T(8,128)S(1)} %get-tuple-element.52), channel_id=1, source_target_pairs={{0,1},{1,0},{2,3},{3,2},{4,5},{5,4},{6,7},{7,6},{8,9},{9,8},{10,11... | collective-permute-start | bytes 786440 | tf_op jit(solution)/shard_map/ppermute | solution.py:325
  17.1 14.9 %collective-permute-start.1 = (f32[6,2,8,512]{3,2,1,0:T(8,128)S(1)}, f32[6,2,8,512]{3,2,1,0:T(8,128)S(1)}, u32[]{:S(2)}, u32[]{:S(2)}) collective-permute-start(f32[6,2,8,512]{3,2,1,0:T(8,128)S(1)} %get-tuple-element.50), channel_id=1, source_target_pairs={{0,7},{1,2},{2,1},{3,4},{4,3},{5,6},{6,5},{7,0},{8,15},{9,10},{10,... | collective-permute-start | bytes 589832 | tf_op jit(solution)/shard_map/ppermute | solution.py:325
  20.7 11.4 %collective-permute-start.3 = (f32[6,2,8,512]{3,2,1,0:T(8,128)S(1)}, f32[6,2,8,512]{3,2,1,0:T(8,128)S(1)}, u32[]{:S(2)}, u32[]{:S(2)}) collective-permute-start(f32[6,2,8,512]{3,2,1,0:T(8,128)S(1)} %get-tuple-element.53), channel_id=1, source_target_pairs={{0,6},{1,3},{2,0},{3,5},{4,2},{5,7},{6,4},{7,1},{8,14},{9,11},{10,... | collective-permute-start | bytes 589832 | tf_op jit(solution)/shard_map/ppermute | solution.py:325
  27.5 11.4 %collective-permute-start.10 = (f32[4,3,8,512]{3,2,1,0:T(8,128)S(1)}, f32[4,3,8,512]{3,2,1,0:T(8,128)S(1)}, u32[]{:S(2)}, u32[]{:S(2)}) collective-permute-start(f32[4,3,8,512]{3,2,1,0:T(8,128)S(1)} %get-tuple-element.73), channel_id=1, source_target_pairs={{0,16},{1,17},{2,18},{3,19},{4,20},{5,21},{6,22},{7,23},{8,24},{9,... | collective-permute-start | bytes 589832 | tf_op jit(solution)/shard_map/ppermute | solution.py:325
  29.1 10.6 %collective-permute-start.11 = (f32[4,3,8,512]{3,2,1,0:T(8,128)S(1)}, f32[4,3,8,512]{3,2,1,0:T(8,128)S(1)}, u32[]{:S(2)}, u32[]{:S(2)}) collective-permute-start(f32[4,3,8,512]{3,2,1,0:T(8,128)S(1)} %get-tuple-element.74), channel_id=1, source_target_pairs={{0,17},{1,16},{2,19},{3,18},{4,21},{5,20},{6,23},{7,22},{8,25},{9,... | collective-permute-start | bytes 589832 | tf_op jit(solution)/shard_map/ppermute | solution.py:325
  32.0 9.0 %collective-permute-start.9 = (f32[4,3,8,512]{3,2,1,0:T(8,128)S(1)}, f32[4,3,8,512]{3,2,1,0:T(8,128)S(1)}, u32[]{:S(2)}, u32[]{:S(2)}) collective-permute-start(f32[4,3,8,512]{3,2,1,0:T(8,128)S(1)} %get-tuple-element.72), channel_id=1, source_target_pairs={{0,1},{1,0},{2,3},{3,2},{4,5},{5,4},{6,7},{7,6},{8,9},{9,8},{10,11... | collective-permute-start | bytes 589832 | tf_op jit(solution)/shard_map/ppermute | solution.py:325
  32.1 7.2 %copy-start = (f32[5,8,64,64]{3,2,1,0:T(8,128)S(1)}, f32[5,8,64,64]{3,2,1,0:T(8,128)}, u32[]{:S(2)}) copy-start(f32[5,8,64,64]{3,2,1,0:T(8,128)} %ops_ref.1) | copy-start | bytes 1966084
  35.4 7.0 %collective-permute-start.6 = (f32[4,2,8,512]{3,2,1,0:T(8,128)S(1)}, f32[4,2,8,512]{3,2,1,0:T(8,128)S(1)}, u32[]{:S(2)}, u32[]{:S(2)}) collective-permute-start(f32[4,2,8,512]{3,2,1,0:T(8,128)S(1)} %get-tuple-element.68), channel_id=1, source_target_pairs={{0,1},{1,0},{2,3},{3,2},{4,5},{5,4},{6,7},{7,6},{8,9},{9,8},{10,11... | collective-permute-start | bytes 393224 | tf_op jit(solution)/shard_map/ppermute | solution.py:325
  37.3 5.6 %collective-permute-start.7 = (f32[4,2,8,512]{3,2,1,0:T(8,128)S(1)}, f32[4,2,8,512]{3,2,1,0:T(8,128)S(1)}, u32[]{:S(2)}, u32[]{:S(2)}) collective-permute-start(f32[4,2,8,512]{3,2,1,0:T(8,128)S(1)} %get-tuple-element.69), channel_id=1, source_target_pairs={{0,16},{1,17},{2,18},{3,19},{4,20},{5,21},{6,22},{7,23},{8,24},{9,... | collective-permute-start | bytes 393224 | tf_op jit(solution)/shard_map/ppermute | solution.py:325
  38.9 6.0 %collective-permute-start.8 = (f32[4,2,8,512]{3,2,1,0:T(8,128)S(1)}, f32[4,2,8,512]{3,2,1,0:T(8,128)S(1)}, u32[]{:S(2)}, u32[]{:S(2)}) collective-permute-start(f32[4,2,8,512]{3,2,1,0:T(8,128)S(1)} %get-tuple-element.70), channel_id=1, source_target_pairs={{0,17},{1,16},{2,19},{3,18},{4,21},{5,20},{6,23},{7,22},{8,25},{9,... | collective-permute-start | bytes 393224 | tf_op jit(solution)/shard_map/ppermute | solution.py:325
  39.7 7.5 %copy-start.1 = (s32[8,512]{1,0:T(8,128)S(1)}, s32[8,512]{1,0:T(8,128)}, u32[]{:S(2)}) copy-start(s32[8,512]{1,0:T(8,128)} %use_ref.3) | copy-start | bytes 49156
  44.9 1.4 %collective-permute-start.12 = (f32[4,3,8,512]{3,2,1,0:T(8,128)S(1)}, f32[4,3,8,512]{3,2,1,0:T(8,128)S(1)}, u32[]{:S(2)}, u32[]{:S(2)}) collective-permute-start(f32[4,3,8,512]{3,2,1,0:T(8,128)S(1)} %get-tuple-element.75.refs_0_), channel_id=1, source_target_pairs={{0,8},{1,9},{2,10},{3,11},{4,12},{5,13},{6,14},{7,15},{8,0},{9,1},... | collective-permute-start | bytes 589832 | tf_op jit(solution)/shard_map/ppermute | solution.py:325
  44.9 1.7 %collective-permute-start.13 = (f32[4,3,8,512]{3,2,1,0:T(8,128)S(1)}, f32[4,3,8,512]{3,2,1,0:T(8,128)S(1)}, u32[]{:S(2)}, u32[]{:S(2)}) collective-permute-start(f32[4,3,8,512]{3,2,1,0:T(8,128)S(1)} %get-tuple-element.76.refs_1_), channel_id=1, source_target_pairs={{0,8},{1,9},{2,10},{3,11},{4,12},{5,13},{6,14},{7,15},{8,0},{9,1},... | collective-permute-start | bytes 589832 | tf_op jit(solution)/shard_map/ppermute | solution.py:325
  45.4 1.5 %collective-permute-start.14 = (f32[4,3,8,512]{3,2,1,0:T(8,128)S(1)}, f32[4,3,8,512]{3,2,1,0:T(8,128)S(1)}, u32[]{:S(2)}, u32[]{:S(2)}) collective-permute-start(f32[4,3,8,512]{3,2,1,0:T(8,128)S(1)} %get-tuple-element.77.refs_2_), channel_id=1, source_target_pairs={{0,8},{1,9},{2,10},{3,11},{4,12},{5,13},{6,14},{7,15},{8,0},{9,1},... | collective-permute-start | bytes 589832 | tf_op jit(solution)/shard_map/ppermute | solution.py:325
  45.4 1.8 %collective-permute-start.15 = (f32[4,3,8,512]{3,2,1,0:T(8,128)S(1)}, f32[4,3,8,512]{3,2,1,0:T(8,128)S(1)}, u32[]{:S(2)}, u32[]{:S(2)}) collective-permute-start(f32[4,3,8,512]{3,2,1,0:T(8,128)S(1)} %get-tuple-element.78.refs_3_), channel_id=1, source_target_pairs={{0,8},{1,9},{2,10},{3,11},{4,12},{5,13},{6,14},{7,15},{8,0},{9,1},... | collective-permute-start | bytes 589832 | tf_op jit(solution)/shard_map/ppermute | solution.py:325
  48.3 12.0 %collective-permute-start.21 = (f32[4,3,16,512]{3,2,1,0:T(8,128)S(1)}, f32[4,3,16,512]{3,2,1,0:T(8,128)S(1)}, u32[]{:S(2)}, u32[]{:S(2)}) collective-permute-start(f32[4,3,16,512]{3,2,1,0:T(8,128)S(1)} %get-tuple-element.86), channel_id=1, source_target_pairs={{0,16},{1,17},{2,18},{3,19},{4,20},{5,21},{6,22},{7,23},{8,24},{9,... | collective-permute-start | bytes 1179656 | tf_op jit(solution)/shard_map/ppermute | solution.py:325
  48.8 1.3 %collective-permute-start.16 = (f32[4,2,8,512]{3,2,1,0:T(8,128)S(1)}, f32[4,2,8,512]{3,2,1,0:T(8,128)S(1)}, u32[]{:S(2)}, u32[]{:S(2)}) collective-permute-start(f32[4,2,8,512]{3,2,1,0:T(8,128)S(1)} %get-tuple-element.80.refs_0_), channel_id=1, source_target_pairs={{0,8},{1,9},{2,10},{3,11},{4,12},{5,13},{6,14},{7,15},{8,0},{9,1},... | collective-permute-start | bytes 393224 | tf_op jit(solution)/shard_map/ppermute | solution.py:325
  48.8 1.5 %collective-permute-start.17 = (f32[4,2,8,512]{3,2,1,0:T(8,128)S(1)}, f32[4,2,8,512]{3,2,1,0:T(8,128)S(1)}, u32[]{:S(2)}, u32[]{:S(2)}) collective-permute-start(f32[4,2,8,512]{3,2,1,0:T(8,128)S(1)} %get-tuple-element.81.refs_1_), channel_id=1, source_target_pairs={{0,8},{1,9},{2,10},{3,11},{4,12},{5,13},{6,14},{7,15},{8,0},{9,1},... | collective-permute-start | bytes 393224 | tf_op jit(solution)/shard_map/ppermute | solution.py:325
  49.3 1.3 %collective-permute-start.18 = (f32[4,2,8,512]{3,2,1,0:T(8,128)S(1)}, f32[4,2,8,512]{3,2,1,0:T(8,128)S(1)}, u32[]{:S(2)}, u32[]{:S(2)}) collective-permute-start(f32[4,2,8,512]{3,2,1,0:T(8,128)S(1)} %get-tuple-element.82.refs_2_), channel_id=1, source_target_pairs={{0,8},{1,9},{2,10},{3,11},{4,12},{5,13},{6,14},{7,15},{8,0},{9,1},... | collective-permute-start | bytes 393224 | tf_op jit(solution)/shard_map/ppermute | solution.py:325
  49.3 1.5 %collective-permute-start.19 = (f32[4,2,8,512]{3,2,1,0:T(8,128)S(1)}, f32[4,2,8,512]{3,2,1,0:T(8,128)S(1)}, u32[]{:S(2)}, u32[]{:S(2)}) collective-permute-start(f32[4,2,8,512]{3,2,1,0:T(8,128)S(1)} %get-tuple-element.83.refs_3_), channel_id=1, source_target_pairs={{0,8},{1,9},{2,10},{3,11},{4,12},{5,13},{6,14},{7,15},{8,0},{9,1},... | collective-permute-start | bytes 393224 | tf_op jit(solution)/shard_map/ppermute | solution.py:325
  51.6 13.6 %collective-permute-start.20 = (f32[4,2,16,512]{3,2,1,0:T(8,128)S(1)}, f32[4,2,16,512]{3,2,1,0:T(8,128)S(1)}, u32[]{:S(2)}, u32[]{:S(2)}) collective-permute-start(f32[4,2,16,512]{3,2,1,0:T(8,128)S(1)} %get-tuple-element.85), channel_id=1, source_target_pairs={{0,16},{1,17},{2,18},{3,19},{4,20},{5,21},{6,22},{7,23},{8,24},{9,... | collective-permute-start | bytes 786440 | tf_op jit(solution)/shard_map/ppermute | solution.py:325
